TPU v7x, 256 devices: a whole 4x4x8 slice. The times are simulated.
256 devices in a mesh: pipe: 8 (over x, y_hi), expert: 32 (over z, y_lo, core).
Axes of the slice: x: 4, y: 4 (y_hi: 2, y_lo: 2; y = y_hi * 2 + y_lo), z: 8, core: 2. Of those that a mesh axis runs over, the one named last changes fastest.
Arguments:
- forward_rows: bfloat16 [8, 2048, 7168], P('pipe', 'expert'), may hold values from -6 to 6
- forward_ids: int32 [8, 2048, 2], P('pipe', 'expert'), may hold values from 0 to 3, all different within a row; in each aligned block of 64 rows (0 to 63, 64 to 127, ..., all dimensions but the last counted through in order) at most 36 rows name the same one
- backward_rows: bfloat16 [8, 2048, 7168], P('pipe', 'expert'), may hold values from -6 to 6
- backward_ids: int32 [8, 2048, 2], P('pipe', 'expert'), may hold values from 0 to 3, all different within a row; in each aligned block of 64 rows (0 to 63, 64 to 127, ..., all dimensions but the last counted through in order) at most 36 rows name the same one
- backward_grad: bfloat16 [8, 2048, 7168], P('pipe', 'expert'), may hold values from -6 to 6
- backward_stash: bfloat16 [8, 2048, 2, 2, 1024], P('pipe', 'expert'), may hold values from -6 to 6
- router: bfloat16 [8, 4, 7168], P('pipe'), may hold values from -0.0625 to 0.0625
- w_gate: bfloat16 [8, 32, 7168, 128], P('pipe', 'expert'), may hold values from -0.0625 to 0.0625
- w_up: bfloat16 [8, 32, 7168, 128], P('pipe', 'expert'), may hold values from -0.0625 to 0.0625
- w_down: bfloat16 [8, 32, 128, 7168], P('pipe', 'expert'), may hold values from -0.1875 to 0.1875
Outputs:
- forward_next: bfloat16 [8, 2048, 7168], P('pipe', 'expert')
- backward_next: bfloat16 [8, 2048, 7168], P('pipe', 'expert')
- router_grad: float32 [8, 4, 7168], P('pipe')
Inputs may be any that keep to these rules, and one draw needn't show every extreme that they name: `forward_ids`: among the rows of one device of the expert axis no expert is named by more than 36 rows, and in every draw some device names one expert exactly 36 times. The 2 experts of a row differ. `backward_ids`: among the rows of one device of the expert axis no expert is named by more than 36 rows, and in every draw some device names one expert exactly 36 times. The 2 experts of a row differ.
All inputs are finite; a program needn't handle non-finite values.
Results may differ from a plain program's by a relative error of at most 0.012.
Values may be sent and summed in bfloat16 or wider, within the bound.
No kernel may reach another device: no remote copies, remote signals or barrier semaphores. Data moves between devices by JAX's collectives and lax.ppermute only.
A program may use at most 192 MiB of HBM per device.

v0:
```python
import jax
import jax.numpy as jnp
from jax import lax
from jax.sharding import PartitionSpec as P

CAP = 36


ROUTE_SCALE = 2.5


def shifted(block, axis, distance):
    devices = range(lax.axis_size(axis))
    route = [((i - distance) % len(devices), i) for i in devices]
    return lax.ppermute(block, axis, route)


def silu_slope(pre_act):
    sigmoid_v = jax.nn.sigmoid(pre_act)
    return sigmoid_v * (1.0 + pre_act * (1.0 - sigmoid_v))


def gate_terms(tok_rows, ids, router_rows):
    experts = router_rows.shape[0]
    logits = lax.dot_general(
        tok_rows, router_rows, (((1,), (1,)), ((), ())), preferred_element_type=jnp.float32
    )
    one_hot = (ids[:, :, None] == jnp.arange(experts, dtype=jnp.int32)[None, None, :]).astype(
        jnp.float32
    )
    probs_m = jax.nn.sigmoid(jnp.sum(one_hot * logits[:, None, :], axis=2))
    total_m = jnp.sum(probs_m, axis=1, keepdims=True)
    return (one_hot, probs_m, total_m)


def route_plan(ids, experts, capacity):
    assigned = ids.shape[0] * ids.shape[1]
    flat_ids = ids.reshape(assigned)
    one_hot = (flat_ids[:, None] == jnp.arange(experts, dtype=jnp.int32)[None, :]).astype(jnp.int32)
    before = jnp.cumsum(one_hot, axis=0) - one_hot
    slot_of = flat_ids * capacity + jnp.sum(before * one_hot, axis=1)
    select = (jnp.arange(experts * capacity, dtype=jnp.int32)[:, None] == slot_of[None, :]).astype(
        jnp.bfloat16
    )
    return (slot_of, select)


def pack_rows(select, tok_rows, top_count):
    repeated = jnp.repeat(tok_rows, top_count, axis=0)
    return jnp.dot(select, repeated, preferred_element_type=jnp.float32).astype(jnp.bfloat16)


def fan_out(packed, experts, group_size, capacity):
    rest = packed.shape[1:]
    shaped = packed.reshape((experts, 1, capacity) + rest)
    spread = jnp.broadcast_to(shaped, (experts, group_size, capacity) + rest)
    return spread.reshape((experts * group_size, capacity) + rest)


def collect(returned, slot_of, experts, top_count):
    members = returned.shape[0]
    capacity = returned.shape[1]
    rest = returned.shape[2:]
    summed = jnp.sum(
        returned.reshape((experts, members // experts, capacity) + rest), axis=1, dtype=jnp.float32
    )
    summed = summed.reshape((experts * capacity,) + rest)
    picked = jnp.take(summed, slot_of, axis=0)
    return picked.reshape((slot_of.shape[0] // top_count, top_count) + rest)


def forward_expert(arrived, gate_w, up_w, down_w):
    tok_rows = arrived.reshape(arrived.shape[0] * arrived.shape[1], arrived.shape[2])
    pre_gate = jnp.dot(tok_rows, gate_w, preferred_element_type=jnp.float32)
    pre_up = jnp.dot(tok_rows, up_w, preferred_element_type=jnp.float32)
    hidden = (jax.nn.silu(pre_gate) * pre_up).astype(jnp.bfloat16)
    member_part = jnp.dot(hidden, down_w, preferred_element_type=jnp.float32).astype(jnp.bfloat16)
    return member_part.reshape(arrived.shape)


def backward_expert(grad_arrived, stash_arrived, scale_arrived, gate_w, up_w, down_w):
    sources = grad_arrived.shape[0]
    capacity = grad_arrived.shape[1]
    feature_dim = grad_arrived.shape[2]
    hidden_dev = down_w.shape[0]
    grad_rows = grad_arrived.reshape(sources * capacity, feature_dim)
    pre_acts = stash_arrived.reshape(sources * capacity, 2, hidden_dev).astype(jnp.float32)
    pre_gate = pre_acts[:, 0]
    pre_up = pre_acts[:, 1]
    activated = jax.nn.silu(pre_gate)
    hidden = (activated * pre_up).astype(jnp.bfloat16)
    raw_grad = lax.dot_general(
        grad_rows, down_w, (((1,), (1,)), ((), ())), preferred_element_type=jnp.float32
    )
    inner_part = jnp.sum(hidden.astype(jnp.float32) * raw_grad, axis=1).astype(jnp.bfloat16)
    back_grad = raw_grad * scale_arrived.reshape(sources * capacity, 1).astype(jnp.float32)
    d_gate = (back_grad * pre_up * silu_slope(pre_gate)).astype(jnp.bfloat16)
    d_up = (back_grad * activated).astype(jnp.bfloat16)
    d_joined = jnp.concatenate([d_gate, d_up], axis=1)
    w_joined = jnp.concatenate([gate_w, up_w], axis=1)
    d_rows = lax.dot_general(
        d_joined, w_joined, (((1,), (1,)), ((), ())), preferred_element_type=jnp.float32
    )
    return (
        d_rows.astype(jnp.bfloat16).reshape(sources, capacity, feature_dim),
        inner_part.reshape(sources, capacity),
    )


def shards(
    forward_rows,
    forward_ids,
    backward_rows,
    backward_ids,
    backward_grad,
    backward_stash,
    router,
    w_gate,
    w_up,
    w_down,
):
    fwd_rows = forward_rows[0]
    fwd_ids = forward_ids[0]
    bwd_rows = backward_rows[0]
    bwd_ids = backward_ids[0]
    bwd_grad = backward_grad[0]
    router_rows = router[0]
    gate_w = w_gate[0, 0]
    up_w = w_up[0, 0]
    down_w = w_down[0, 0]
    members = lax.axis_size("expert")
    experts = router_rows.shape[0]
    group_size = members // experts
    hidden_dev = down_w.shape[0]
    top_count = fwd_ids.shape[1]
    tok_count = fwd_rows.shape[0]
    assigned = tok_count * top_count
    one_hot_f, probs_f, total_f = gate_terms(fwd_rows, fwd_ids, router_rows)
    weights_f = ROUTE_SCALE * probs_f / total_f
    slot_f, select_f = route_plan(fwd_ids, experts, CAP)
    send_rows = fan_out(pack_rows(select_f, fwd_rows, top_count), experts, group_size, CAP)
    one_hot_b, probs_b, total_b = gate_terms(bwd_rows, bwd_ids, router_rows)
    share_b = probs_b / total_b
    scale_b = (ROUTE_SCALE * share_b).astype(jnp.bfloat16)
    slot_b, select_b = route_plan(bwd_ids, experts, CAP)
    send_grad = fan_out(pack_rows(select_b, bwd_grad, top_count), experts, group_size, CAP)
    scale_packed = jnp.dot(
        select_b, scale_b.reshape(assigned, 1), preferred_element_type=jnp.float32
    ).astype(jnp.bfloat16)
    send_scale = fan_out(scale_packed, experts, group_size, CAP)
    stash_flat = backward_stash[0].reshape(
        assigned, backward_stash.shape[3] * backward_stash.shape[4]
    )
    stash_packed = jnp.dot(select_b, stash_flat, preferred_element_type=jnp.float32).astype(
        jnp.bfloat16
    )
    stash_packed = stash_packed.reshape(experts, CAP, 2, group_size, hidden_dev).transpose(
        0, 3, 1, 2, 4
    )
    send_stash = stash_packed.reshape(experts * group_size, CAP, 2 * hidden_dev)
    got_rows, got_grad, got_stash, got_scale = (
        lax.all_to_all(send_rows, "expert", split_axis=0, concat_axis=0, tiled=True),
        lax.all_to_all(send_grad, "expert", split_axis=0, concat_axis=0, tiled=True),
        lax.all_to_all(send_stash, "expert", split_axis=0, concat_axis=0, tiled=True),
        lax.all_to_all(send_scale, "expert", split_axis=0, concat_axis=0, tiled=True),
    )
    part_f = forward_expert(got_rows, gate_w, up_w, down_w)
    part_b, inner_b = backward_expert(got_grad, got_stash, got_scale, gate_w, up_w, down_w)
    back_f, back_b, back_inner = (
        lax.all_to_all(part_f, "expert", split_axis=0, concat_axis=0, tiled=True),
        lax.all_to_all(part_b, "expert", split_axis=0, concat_axis=0, tiled=True),
        lax.all_to_all(inner_b, "expert", split_axis=0, concat_axis=0, tiled=True),
    )
    picked_f = collect(back_f, slot_f, experts, top_count)
    layer_out = (
        fwd_rows.astype(jnp.float32) + jnp.sum(weights_f[:, :, None] * picked_f, axis=1)
    ).astype(jnp.bfloat16)
    d_expert = jnp.sum(collect(back_b, slot_b, experts, top_count), axis=1)
    inner_sum = collect(back_inner, slot_b, experts, top_count)
    d_logit = (
        ROUTE_SCALE
        / total_b
        * (inner_sum - jnp.sum(share_b * inner_sum, axis=1, keepdims=True))
        * probs_b
        * (1.0 - probs_b)
    )
    score_grad = jnp.sum(one_hot_b * d_logit[:, :, None], axis=1)
    router_part = jnp.dot(
        score_grad, router_rows.astype(jnp.float32), precision=lax.Precision.HIGHEST
    )
    input_grad = (bwd_grad.astype(jnp.float32) + d_expert + router_part).astype(jnp.bfloat16)
    local_grad = jnp.dot(
        score_grad.T, bwd_rows.astype(jnp.float32), precision=lax.Precision.HIGHEST
    )
    local_grad = local_grad * (1.0 / (tok_count * members))
    router_total = lax.psum(local_grad, "expert")
    forward_out_rows = shifted(layer_out, "pipe", 1)
    backward_out_rows = shifted(input_grad, "pipe", -1)
    return (forward_out_rows[None], backward_out_rows[None], router_total[None])


def solution(mesh):
    return jax.shard_map(
        shards,
        mesh=mesh,
        in_specs=(
            P("pipe", "expert", None),
            P("pipe", "expert", None),
            P("pipe", "expert", None),
            P("pipe", "expert", None),
            P("pipe", "expert", None),
            P("pipe", "expert", None, None, None),
            P("pipe", None, None),
            P("pipe", "expert", None, None),
            P("pipe", "expert", None, None),
            P("pipe", "expert", None, None),
        ),
        out_specs=(P("pipe", "expert", None), P("pipe", "expert", None), P("pipe", None, None)),
        check_vma=False,
    )
```

profile of v0, /device:TPU:1, one launch (start us, length us, event | category | flops | bytes accessed | tf_op | source)
XLA Modules:
  0.0 2007.7 jit_solution(9350754460937703024)
XLA Ops:
  14.9 11.1 all-to-all-start.3
  29.5 2.2 copy.91
  31.7 2.2 all-to-all-done.3
  33.9 6.1 all-to-all-start.4
  42.2 5.0 reshape.278
  47.1 3.5 convolution_convert_fusion.2
  50.6 2.8 broadcast_in_dim.73
  53.4 6.1 all-to-all-done.4
  59.6 7.7 broadcast_in_dim.74
  67.3 6.3 all-to-all-start.2
  74.1 2.2 broadcast_in_dim.68
  76.3 5.0 reshape.272
  81.9 3.6 convolution_convert_fusion.3
  85.5 2.8 broadcast_in_dim.69
  88.3 385.1 %all-to-all-done.2 = bf16[32,36,7168]{2,1,0:T(8,128)(2,1)} async-done(((bf16[32,36,7168]{2,1,0:T(8,128)(2,1)}), bf16[32,36,7168]{2,1,0:T(8,128)(2,1)}, u32[]{:S(2)}, u32[]{:S(2)}) %all-to-all-start.2) | async-done | bytes 16515104 | tf_op jit(solution)/shard_map/all_to_all | solution.py:163
  473.4 7.4 broadcast_in_dim.70
  480.9 5.9 all-to-all-start
  490.6 18.9 reshape.280
  509.5 11.0 multiply_convert_fusion.2
  521.2 365.3 %all-to-all-done = bf16[32,36,7168]{2,1,0:T(8,128)(2,1)} async-done(((bf16[32,36,7168]{2,1,0:T(8,128)(2,1)}), bf16[32,36,7168]{2,1,0:T(8,128)(2,1)}, u32[]{:S(2)}, u32[]{:S(2)}) %all-to-all-start) | async-done | bytes 16515104 | tf_op jit(solution)/shard_map/all_to_all | solution.py:162
  886.6 4.8 all-to-all-start.6
  891.3 12.3 convolution_convert_fusion
  903.6 18.7 reshape.284
  922.3 8.7 all-to-all-start.5
  931.0 18.8 reshape.274
  949.8 8.5 fusion.38
  958.4 24.4 %convolution_convert_fusion.1 = bf16[1152,7168]{1,0:T(8,128)(2,1)} fusion(bf16[1152,7168]{1,0:T(8,128)(2,1)} %reshape.274, bf16[1,1,128,7168]{3,2,1,0:T(8,128)(2,1)S(1)} %copy-done, f32[1152,128]{1,0:T(8,128)S(1)} %fusion.38, bf16[1,1,7168,128]{3,2,1,0:T(8,128)(2,1)} %param.20), kind=kOutput, calls=%fused_computation.6 | convolution fusion | flops 4237000704 | bytes 37289984 | tf_op jit(solution)/shard_map/dot_general | solution.py:77
  982.8 18.6 reshape.275
  1001.4 329.2 %all-to-all-done.5 = bf16[32,36,7168]{2,1,0:T(8,128)(2,1)} async-done(((bf16[32,36,7168]{2,1,0:T(8,128)(2,1)}), bf16[32,36,7168]{2,1,0:T(8,128)(2,1)}, u32[]{:S(2)}, u32[]{:S(2)}) %all-to-all-start.5) | async-done | bytes 16515104 | tf_op jit(solution)/shard_map/all_to_all | solution.py:171
  1330.7 5.3 all-to-all-start.1
  1338.6 11.6 convert_reduce_fusion
  1350.2 3.9 reshape.285
  1354.1 7.2 gather_fusion.2
  1361.3 4.3 broadcast_select_fusion
  1365.5 5.5 reshape.286
  1371.0 6.5 reduce_sum.139
  1379.4 5.0 collective-permute-start.1
  1384.5 351.3 %all-to-all-done.1 = bf16[32,36,7168]{2,1,0:T(8,128)(2,1)} async-done(((bf16[32,36,7168]{2,1,0:T(8,128)(2,1)}), bf16[32,36,7168]{2,1,0:T(8,128)(2,1)}, u32[]{:S(2)}, u32[]{:S(2)}) %all-to-all-start.1) | async-done | bytes 16515104 | tf_op jit(solution)/shard_map/all_to_all | solution.py:170
  1735.8 11.6 convert_reduce_fusion.1
  1747.4 3.9 reshape.276
  1751.3 7.2 gather_fusion.1
  1758.4 4.2 broadcast_select_fusion.1
  1762.7 5.6 reshape.277
  1768.2 7.3 multiply_reduce_fusion
  1775.7 2.8 collective-permute-start
  1779.6 21.3 %collective-permute-done = bf16[64,7168]{1,0:T(8,128)(2,1)} collective-permute-done((bf16[64,7168]{1,0:T(8,128)(2,1)S(1)}, bf16[64,7168]{1,0:T(8,128)(2,1)}, u32[]{:S(2)}, u32[]{:S(2)}) %collective-permute-start) | collective-permute-done | bytes 917536 | tf_op jit(solution)/shard_map/ppermute | solution.py:15
  1800.9 194.5 %all-reduce.2.cloned.1.call-done = f32[1,4,7168]{2,1,0:T(4,128)} async-done(((f32[1,4,7168]{2,1,0:T(4,128)}), f32[1,4,7168]{2,1,0:T(4,128)}) %all-reduce.2.cloned.1.call-update) | async-done | bytes 114704 | tf_op jit(solution)/shard_map/psum | solution.py:196
  1995.4 2.2 copy.109
  (100 shorter events, 27.4 us)
Async XLA Ops:
  7.2 502.3 %copy-start = (bf16[1,1,128,7168]{3,2,1,0:T(8,128)(2,1)S(1)}, bf16[1,1,128,7168]{3,2,1,0:T(8,128)(2,1)}, u32[]{:S(2)}) copy-start(bf16[1,1,128,7168]{3,2,1,0:T(8,128)(2,1)} %param.21) | copy-start | bytes 5505028
  14.9 18.9 all-to-all-start.3
  27.3 12.7 copy-start.4
  33.9 25.7 %all-to-all-start.4 = ((bf16[32,36,256]{2,1,0:T(8,128)(2,1)}), bf16[32,36,256]{2,1,0:T(8,128)(2,1)S(1)}, u32[]{:S(2)}, u32[]{:S(2)}) async-start(bf16[32,36,256]{2,1,0:T(8,128)(2,1)} %copy.91), calls=%async_computation.4 | async-start | bytes 1310720 | tf_op jit(solution)/shard_map/all_to_all | solution.py:164
  59.6 7.7 copy-start.6
  67.3 6.3 copy-start.13
  67.3 6.8 copy-start.2
  67.3 406.2 %all-to-all-start.2 = ((bf16[32,36,7168]{2,1,0:T(8,128)(2,1)}), bf16[32,36,7168]{2,1,0:T(8,128)(2,1)}, u32[]{:S(2)}, u32[]{:S(2)}) async-start(bf16[32,36,7168]{2,1,0:T(8,128)(2,1)} %bitcast.88), calls=%async_computation.2 | async-start | bytes 36700160 | tf_op jit(solution)/shard_map/all_to_all | solution.py:163
  480.9 405.7 %all-to-all-start = ((bf16[32,36,7168]{2,1,0:T(8,128)(2,1)}), bf16[32,36,7168]{2,1,0:T(8,128)(2,1)}, u32[]{:S(2)}, u32[]{:S(2)}) async-start(bf16[32,36,7168]{2,1,0:T(8,128)(2,1)} %bitcast.87), calls=%async_computation | async-start | bytes 36700160 | tf_op jit(solution)/shard_map/all_to_all | solution.py:162
  490.6 18.9 copy-start.8
  490.6 18.9 copy-start.9
  886.6 35.8 %all-to-all-start.6 = ((bf16[32,1,36]{2,1,0:T(2,128)(2,1)}), bf16[32,1,36]{2,1,0:T(2,128)(2,1)S(1)}, u32[]{:S(2)}, u32[]{:S(2)}) async-start(bf16[32,1,36]{2,1,0:T(2,128)(2,1)} %convert_element_type.151), calls=%async_computation.6 | async-start | bytes 32768 | tf_op jit(solution)/shard_map/all_to_all | solution.py:172
  922.3 408.3 %all-to-all-start.5 = ((bf16[32,36,7168]{2,1,0:T(8,128)(2,1)}), bf16[32,36,7168]{2,1,0:T(8,128)(2,1)}, u32[]{:S(2)}, u32[]{:S(2)}) async-start(bf16[32,36,7168]{2,1,0:T(8,128)(2,1)} %reshape.284), calls=%async_computation.5 | async-start | bytes 36700160 | tf_op jit(solution)/shard_map/all_to_all | solution.py:171
  1001.4 334.9 %copy-start.12 = (s32[1,64,2]{1,2,0:T(2,128)S(1)}, s32[1,64,2]{1,2,0:T(2,128)}, u32[]{:S(2)}) copy-start(s32[1,64,2]{1,2,0:T(2,128)} %param.15) | copy-start | bytes 1540
  1330.7 405.1 %all-to-all-start.1 = ((bf16[32,36,7168]{2,1,0:T(8,128)(2,1)}), bf16[32,36,7168]{2,1,0:T(8,128)(2,1)}, u32[]{:S(2)}, u32[]{:S(2)}) async-start(bf16[32,36,7168]{2,1,0:T(8,128)(2,1)} %reshape.275), calls=%async_computation.1 | async-start | bytes 36700160 | tf_op jit(solution)/shard_map/all_to_all | solution.py:170
  1336.0 659.4 %all-reduce.2.cloned.1.call-start = ((), (), s32[]{:S(2)}) async-start(), calls=%async_computation.7 | async-start | bytes 229376 | tf_op jit(solution)/shard_map/psum | solution.py:196
  1354.1 7.2 copy-start.14
  1371.0 6.5 copy-start.5
  1371.0 6.5 copy-start.11
  1379.4 400.2 %collective-permute-start.1 = (bf16[64,7168]{1,0:T(8,128)(2,1)}, bf16[64,7168]{1,0:T(8,128)(2,1)}, u32[]{:S(2)}, u32[]{:S(2)}) collective-permute-start(bf16[64,7168]{1,0:T(8,128)(2,1)} %fusion), channel_id=1, source_target_pairs={{32,0},{64,32},{96,64},{128,96},{160,128},{192,160},{224,192},{0,2... | collective-permute-start | bytes 2752520 | tf_op jit(solution)/shard_map/ppermute | solution.py:15
  1751.3 7.2 copy-start.15
  1768.2 7.3 copy-start.3
  1768.2 10.2 copy-start.7
  1768.2 232.1 %copy-start.1 = (bf16[1,1,128,7168]{3,2,1,0:T(8,128)(2,1)S(1)}, bf16[1,1,128,7168]{3,2,1,0:T(8,128)(2,1)}, u32[]{:S(2)}) copy-start(bf16[1,1,128,7168]{3,2,1,0:T(8,128)(2,1)} %param.21) | copy-start | bytes 5505028
  1775.7 25.2 %collective-permute-start = (bf16[64,7168]{1,0:T(8,128)(2,1)S(1)}, bf16[64,7168]{1,0:T(8,128)(2,1)}, u32[]{:S(2)}, u32[]{:S(2)}) collective-permute-start(bf16[64,7168]{1,0:T(8,128)(2,1)S(1)} %add_convert_fusion), channel_id=1, source_target_pairs={{224,0},{0,32},{32,64},{64,96},{96,128},{128,160},{160,192},{192,2... | collective-permute-start | bytes 2752520 | tf_op jit(solution)/shard_map/ppermute | solution.py:15
  1995.4 4.4 copy-start.10
Sparse Core Ops, SparseCore 0:
  1779.7 215.5 all-reduce.1
where the time goes:
time: 2020 us; the launch traced here: 2010 us
  waiting for transfers between devices  1660 us (82%)
  local copies, waits for them, and re-layouts  162 us (8%)
  matrix products  69.8 us (3%)
  starting transfers between devices  56.2 us (3%)
  other arithmetic  49.3 us (2%)
    all_to_all x1, waiting for transfers between devices, shards(): lax.all_to_all(send_grad, 'expert', split_axis=0, concat_axis=0, tiled=True)  385 us
    all_to_all x1, waiting for transfers between devices, shards(): lax.all_to_all(send_rows, 'expert', split_axis=0, concat_axis=0, tiled=True)  365 us
    all_to_all x1, waiting for transfers between devices, shards(): lax.all_to_all(part_f, 'expert', split_axis=0, concat_axis=0, tiled=True)  351 us
    all_to_all x1, waiting for transfers between devices, shards(): lax.all_to_all(part_b, 'expert', split_axis=0, concat_axis=0, tiled=True)  329 us
    psum x1, waiting for transfers between devices, shards(): router_total = lax.psum(local_grad, 'expert')  194 us
  transfers between devices with their start and end apart: 10, of which 8 were waited for; matrix products, arithmetic and copies ran while one was open for 13% of the time, Pallas kernels for 0%

commit v1 on v0

v1 whole, which is shorter than its diff:
```python
import jax
import jax.numpy as jnp
from jax import lax
from jax.experimental import pallas as pl
from jax.experimental.pallas import tpu as pltpu
from jax.sharding import PartitionSpec as P

CAP = 40
USED = 36
ROUTE_SCALE = 2.5
BF = jnp.bfloat16
F32 = jnp.float32
VMEM_BYTES = 48 * 1024 * 1024


def params(steps):
    return pltpu.CompilerParams(
        dimension_semantics=("arbitrary",) * steps, vmem_limit_bytes=VMEM_BYTES
    )


def shifted(block, axis, distance):
    devices = range(lax.axis_size(axis))
    route = [((i - distance) % len(devices), i) for i in devices]
    return lax.ppermute(block, axis, route)


def exchanged(block, mask):
    route = [(i, i ^ mask) for i in range(lax.axis_size("expert"))]
    return lax.ppermute(block, "expert", route)


def all_to_all(block):
    return lax.all_to_all(block, "expert", split_axis=0, concat_axis=0, tiled=True)


def gate_terms(tok_rows, ids, router_rows):
    experts = router_rows.shape[0]
    logits = lax.dot_general(
        tok_rows, router_rows, (((1,), (1,)), ((), ())), preferred_element_type=F32
    )
    one_hot = (ids[:, :, None] == jnp.arange(experts, dtype=jnp.int32)[None, None, :]).astype(F32)
    probs_m = jax.nn.sigmoid(jnp.sum(one_hot * logits[:, None, :], axis=2))
    total_m = jnp.sum(probs_m, axis=1, keepdims=True)
    return one_hot, probs_m, total_m


def route_plan(ids, experts):
    tokens, top = ids.shape
    flat_ids = ids.reshape(tokens * top)
    one_hot = (flat_ids[:, None] == jnp.arange(experts, dtype=jnp.int32)[None, :]).astype(jnp.int32)
    before = jnp.cumsum(one_hot, axis=0) - one_hot
    slot = flat_ids * CAP + jnp.sum(before * one_hot, axis=1)
    return slot.reshape(tokens, top)


def pack_forward(select, rows, experts, group):
    tokens, features = rows.shape
    width = features // group
    slots = select.shape[0]

    def body(select_ref, rows_ref, out_ref):
        got = jnp.dot(select_ref[...], rows_ref[...], preferred_element_type=F32)
        out_ref[:, 0] = got.reshape(experts, CAP, width).astype(BF)

    return pl.pallas_call(
        body,
        grid=(group,),
        in_specs=[
            pl.BlockSpec((slots, tokens), lambda g: (0, 0)),
            pl.BlockSpec((tokens, width), lambda g: (0, g)),
        ],
        out_specs=pl.BlockSpec((experts, 1, CAP, width), lambda g: (0, g, 0, 0)),
        out_shape=jax.ShapeDtypeStruct((experts, group, CAP, width), BF),
        compiler_params=params(1),
        name="pack_forward",
    )(select, rows)


def pack_backward(select, select_pairs, rows, stash, experts, group, hidden):
    tokens, features = rows.shape
    width = features // group
    slots, pairs = select_pairs.shape

    def body(select_ref, pairs_ref, rows_ref, gate_ref, up_ref, out_ref):
        got = jnp.dot(select_ref[...], rows_ref[...], preferred_element_type=F32)
        out_ref[:, 0, :, 0:width] = got.reshape(experts, CAP, width).astype(BF)
        for place, ref in enumerate((gate_ref, up_ref)):
            got = jnp.dot(pairs_ref[...], ref[...], preferred_element_type=F32)
            start = width + place * hidden
            out_ref[:, 0, :, start : start + hidden] = got.reshape(experts, CAP, hidden).astype(BF)

    return pl.pallas_call(
        body,
        grid=(group,),
        in_specs=[
            pl.BlockSpec((slots, tokens), lambda g: (0, 0)),
            pl.BlockSpec((slots, pairs), lambda g: (0, 0)),
            pl.BlockSpec((tokens, width), lambda g: (0, g)),
            pl.BlockSpec((pairs, hidden), lambda g: (0, g)),
            pl.BlockSpec((pairs, hidden), lambda g: (0, group + g)),
        ],
        out_specs=pl.BlockSpec((experts, 1, CAP, width + 2 * hidden), lambda g: (0, g, 0, 0)),
        out_shape=jax.ShapeDtypeStruct((experts, group, CAP, width + 2 * hidden), BF),
        compiler_params=params(1),
        name="pack_backward",
    )(select, select_pairs, rows, stash, stash)


def contract(left, right, right_dim):
    return lax.dot_general(left, right, (((1,), (right_dim,)), ((), ())), preferred_element_type=F32)


def first_stage(own, other, weights, width, hidden, right_dim, name):
    rows = own.shape[0]
    block = 256

    def body(own_ref, other_ref, *refs):
        for w_ref, out_ref in zip(refs[:4], refs[4:]):
            total = contract(own_ref[...], w_ref[0], right_dim)
            total += contract(other_ref[...], w_ref[1], right_dim)
            out_ref[...] = total.astype(out_ref.dtype)

    return pl.pallas_call(
        body,
        grid=(rows // block,),
        in_specs=[pl.BlockSpec((block, width), lambda r: (r, 0))] * 2
        + [pl.BlockSpec(weights[0].shape, lambda r: (0, 0, 0))] * 4,
        out_specs=[pl.BlockSpec((block, hidden), lambda r: (r, 0))] * 4,
        out_shape=[jax.ShapeDtypeStruct((rows, hidden), F32)]
        + [jax.ShapeDtypeStruct((rows, hidden), BF)] * 3,
        compiler_params=params(1),
        name=name,
    )(own, other, *weights)


def second_stage(pieces, weights, width, right_dim, name):
    rows, hidden = pieces[0].shape
    block = 256

    def body(*refs):
        for half, out_ref in enumerate(refs[8:]):
            total = contract(refs[0][...], refs[4][half], right_dim)
            for step in range(1, 4):
                total += contract(refs[step][...], refs[4 + step][half], right_dim)
            out_ref[...] = total.astype(BF)

    return pl.pallas_call(
        body,
        grid=(rows // block,),
        in_specs=[pl.BlockSpec((block, hidden), lambda r: (r, 0))] * 4
        + [pl.BlockSpec(weights[0].shape, lambda r: (0, 0, 0))] * 4,
        out_specs=[pl.BlockSpec((block, width), lambda r: (r, 0))] * 2,
        out_shape=[jax.ShapeDtypeStruct((rows, width), BF)] * 2,
        compiler_params=params(1),
        name=name,
    )(*pieces, *weights)


def combine(picks, factors, returned, rows, extra, name):
    tokens, features = rows.shape
    experts, group, cap, width = returned.shape
    top = len(picks)

    def body(*refs):
        pick_refs, factor_ref, back_ref, rows_ref = refs[:top], refs[top], refs[top + 1], refs[top + 2]
        out_ref = refs[-1]
        back = back_ref[:, 0].astype(F32).reshape(experts * cap, width).astype(BF)
        total = rows_ref[...].astype(F32)
        for k in range(top):
            picked = jnp.dot(pick_refs[k][...], back, preferred_element_type=F32)
            total += factor_ref[:, k : k + 1] * picked
        if extra is not None:
            score_ref, router_ref = refs[top + 3 : top + 5]
            for e in range(experts):
                total += score_ref[:, e : e + 1] * router_ref[e : e + 1, :].astype(F32)
        out_ref[...] = total.astype(BF)

    in_specs = [pl.BlockSpec(picks[0].shape, lambda g: (0, 0))] * top + [
        pl.BlockSpec(factors.shape, lambda g: (0, 0)),
        pl.BlockSpec((experts, 1, cap, width), lambda g: (0, g, 0, 0)),
        pl.BlockSpec((tokens, width), lambda g: (0, g)),
    ]
    operands = list(picks) + [factors, returned, rows]
    if extra is not None:
        in_specs += [
            pl.BlockSpec(extra[0].shape, lambda g: (0, 0)),
            pl.BlockSpec((experts, width), lambda g: (0, g)),
        ]
        operands += list(extra)
    return pl.pallas_call(
        body,
        grid=(group,),
        in_specs=in_specs,
        out_specs=pl.BlockSpec((tokens, width), lambda g: (0, g)),
        out_shape=jax.ShapeDtypeStruct((tokens, features), BF),
        compiler_params=params(1),
        name=name,
    )(*operands)


def silu_slope(pre_act):
    sigmoid_v = jax.nn.sigmoid(pre_act)
    return sigmoid_v * (1.0 + pre_act * (1.0 - sigmoid_v))


def shards(
    forward_rows,
    forward_ids,
    backward_rows,
    backward_ids,
    backward_grad,
    backward_stash,
    router,
    w_gate,
    w_up,
    w_down,
):
    fwd_rows, fwd_ids = forward_rows[0], forward_ids[0]
    bwd_rows, bwd_ids, bwd_grad = backward_rows[0], backward_ids[0], backward_grad[0]
    router_rows = router[0]
    gate_w, up_w, down_w = w_gate[0, 0], w_up[0, 0], w_down[0, 0]
    members = lax.axis_size("expert")
    experts, features = router_rows.shape
    group = members // experts
    hidden = down_w.shape[0]
    width = features // group
    tokens, top = fwd_ids.shape
    slots = experts * CAP
    place = lax.axis_index("expert") % group
    core = place % 2
    chip = place // 2
    slot_axis = jnp.arange(slots, dtype=jnp.int32)

    down_split = jnp.transpose(down_w.reshape(hidden, group, width), (1, 0, 2))
    joined_split = jnp.concatenate([gate_w, up_w], axis=1).reshape(group, width, 2 * hidden)

    def halves(split, step):
        first = 2 * (chip ^ step) + core
        second = 2 * (chip ^ step) + 1 - core
        return jnp.concatenate(
            [
                lax.dynamic_slice_in_dim(split, first, 1, 0),
                lax.dynamic_slice_in_dim(split, second, 1, 0),
            ],
            axis=0,
        )

    downs = [exchanged(halves(down_split, s), 2 * s) if s else halves(down_split, s) for s in range(4)]
    joins = [
        exchanged(halves(joined_split, s), 2 * s) if s else halves(joined_split, s) for s in range(4)
    ]

    slot_b = route_plan(bwd_ids, experts)
    pairs_b = (slot_axis[:, None] == slot_b.reshape(1, tokens * top)).astype(BF)
    select_b = jnp.sum(slot_axis[:, None, None] == slot_b[None], axis=2).astype(BF)
    stash = backward_stash[0].reshape(tokens * top, 2 * group * hidden)
    send_b = pack_backward(select_b, pairs_b, bwd_grad, stash, experts, group, hidden)
    got_b = all_to_all(send_b.reshape(members, CAP, width + 2 * hidden))
    got_b = got_b.reshape(members * CAP, width + 2 * hidden)

    slot_f = route_plan(fwd_ids, experts)
    select_f = jnp.sum(slot_axis[:, None, None] == slot_f[None], axis=2).astype(BF)
    send_f = pack_forward(select_f, fwd_rows, experts, group)
    got_f = all_to_all(send_f.reshape(members, CAP, width)).reshape(members * CAP, width)

    own_b = got_b[:, :width]
    raw_parts = first_stage(own_b, exchanged(own_b, 1), downs, width, hidden, 1, "raw_grad")
    raw_grad = raw_parts[0]
    for s in range(1, 4):
        raw_grad = raw_grad + exchanged(raw_parts[s], 2 * s).astype(F32)
    pre_gate = got_b[:, width : width + hidden].astype(F32)
    pre_up = got_b[:, width + hidden :].astype(F32)
    activated = jax.nn.silu(pre_gate)
    hidden_b = (activated * pre_up).astype(BF).astype(F32)
    inner_part = jnp.sum(hidden_b * raw_grad, axis=1).astype(BF)
    d_gate = (raw_grad * pre_up * silu_slope(pre_gate)).astype(BF)
    d_up = (raw_grad * activated).astype(BF)
    d_own = jnp.concatenate([d_gate, d_up], axis=1)
    d_pieces = [d_own] + [exchanged(d_own, 2 * s) for s in range(1, 4)]
    d_keep, d_give = second_stage(d_pieces, joins, width, 1, "d_rows")
    d_sum = (d_keep.astype(F32) + exchanged(d_give, 1).astype(F32)).astype(BF)
    d_sum = d_sum.reshape(members, CAP, width)
    inner_row = jnp.pad(inner_part.reshape(members, 1, CAP), ((0, 0), (0, 0), (0, width - CAP)))
    is_inner = lax.broadcasted_iota(jnp.int32, (1, CAP, 1), 1) == USED
    d_sum = jnp.where(is_inner, inner_row, d_sum)
    back_b = all_to_all(d_sum).reshape(experts, group, CAP, width)

    pre_parts = first_stage(got_f, exchanged(got_f, 1), joins, width, 2 * hidden, 0, "pre_acts")
    pre_acts = pre_parts[0]
    for s in range(1, 4):
        pre_acts = pre_acts + exchanged(pre_parts[s], 2 * s).astype(F32)
    hidden_f = (jax.nn.silu(pre_acts[:, :hidden]) * pre_acts[:, hidden:]).astype(BF)
    hidden_pieces = [hidden_f] + [exchanged(hidden_f, 2 * s) for s in range(1, 4)]
    y_keep, y_give = second_stage(hidden_pieces, downs, width, 0, "y_rows")
    y_sum = (y_keep.astype(F32) + exchanged(y_give, 1).astype(F32)).astype(BF)
    back_f = all_to_all(y_sum.reshape(members, CAP, width)).reshape(experts, group, CAP, width)

    one_hot_b, probs_b, total_b = gate_terms(bwd_rows, bwd_ids, router_rows)
    share_b = probs_b / total_b
    scale_b = (ROUTE_SCALE * share_b).astype(BF).astype(F32)
    picks_b = [(slot_b[:, k : k + 1] == slot_axis[None, :]).astype(BF) for k in range(top)]
    inner_all = jnp.sum(back_b[:, :, USED, :CAP].astype(F32), axis=1).reshape(1, slots)
    inner_sum = jnp.stack(
        [jnp.sum(picks_b[k].astype(F32) * inner_all, axis=1) for k in range(top)], axis=1
    )
    d_logit = (
        ROUTE_SCALE
        / total_b
        * (inner_sum - jnp.sum(share_b * inner_sum, axis=1, keepdims=True))
        * probs_b
        * (1.0 - probs_b)
    )
    score_grad = jnp.sum(one_hot_b * d_logit[:, :, None], axis=1)
    input_grad = combine(
        picks_b, scale_b, back_b, bwd_grad, (score_grad, router_rows), "combine_backward"
    )
    router_total = jnp.dot(score_grad.T, bwd_rows.astype(F32), precision=lax.Precision.HIGHEST)
    router_total = router_total * (1.0 / (tokens * members))
    mask = 1
    while mask < members:
        router_total = router_total + exchanged(router_total, mask)
        mask *= 2
    backward_out_rows = shifted(input_grad, "pipe", -1)

    one_hot_f, probs_f, total_f = gate_terms(fwd_rows, fwd_ids, router_rows)
    weights_f = ROUTE_SCALE * probs_f / total_f
    picks_f = [(slot_f[:, k : k + 1] == slot_axis[None, :]).astype(BF) for k in range(top)]
    layer_out = combine(picks_f, weights_f, back_f, fwd_rows, None, "combine_forward")
    forward_out_rows = shifted(layer_out, "pipe", 1)
    return (forward_out_rows[None], backward_out_rows[None], router_total[None])


def solution(mesh):
    return jax.shard_map(
        shards,
        mesh=mesh,
        in_specs=(
            P("pipe", "expert", None),
            P("pipe", "expert", None),
            P("pipe", "expert", None),
            P("pipe", "expert", None),
            P("pipe", "expert", None),
            P("pipe", "expert", None, None, None),
            P("pipe", None, None),
            P("pipe", "expert", None, None),
            P("pipe", "expert", None, None),
            P("pipe", "expert", None, None),
        ),
        out_specs=(P("pipe", "expert", None), P("pipe", "expert", None), P("pipe", None, None)),
        check_vma=False,
    )
```

time: 2020 us -> 509 us (0.25)
  waiting for transfers between devices: 1660 us -> 337 us
  local copies, waits for them, and re-layouts: 162 us -> 23.4 us
  matrix products: 69.8 us -> 2.36 us
  Pallas kernels: 0 us -> 43.4 us
  other arithmetic: 49.3 us -> 21.8 us
    all_to_all x7 -> x4, waiting for transfers between devices: 1440 us -> 90.4 us  [all_to_all(): lax.all_to_all(block, 'expert', split_axis=0, concat_axis=0, tiled=True)]
    ppermute x0 -> x27, waiting for transfers between devices: none -> 232 us  [exchanged(): return lax.ppermute(block, 'expert', route)]
    psum x1 -> x0, waiting for transfers between devices: 194 us -> none  [shards(): router_total = lax.psum(local_grad, 'expert')]
    reshape x14 -> x0, local copies, waits for them, and re-layouts: 108 us -> none  [the longest x1 18.9 us: backward_expert(): grad_rows = grad_arrived.reshape(sources * capacity, feature_dim)]
    dot_general x10 -> x1, matrix products: 66.8 us -> 0.48 us  [shards(): jnp.dot(score_grad.T, bwd_rows.astype(F32), precision=lax.Precision.HIGHEST)]
    pallas_call x0 -> x8, Pallas kernels: none -> 43.4 us  [the longest x2 15.4 us: first_stage(): pl.pallas_call(body, grid=(rows // block,), in_specs=[pl.BlockSpec((block...]
    ppermute x0 -> x27, starting transfers between devices: none -> 34.5 us  [exchanged(): return lax.ppermute(block, 'expert', route)]
    reduce_sum x7, other arithmetic: 37.3 us -> 3.02 us  [the longest x1 2.26 us: shards(): inner_part = jnp.sum(hidden_b * raw_grad, axis=1).astype(BF)]
  transfers between devices with their start and end apart: 10 -> 33, of which waited for: 8 -> 21; matrix products, arithmetic and copies ran while one was open for 13% -> 6% of each run, Pallas kernels for 0% -> 8%
where the time goes in v1:
time: 509 us; the launch traced here: 504 us
  waiting for transfers between devices  337 us (66%)
  starting transfers between devices  74.8 us (15%)
  Pallas kernels  43.4 us (9%)
  local copies, waits for them, and re-layouts  23.4 us (5%)
  other arithmetic  21.8 us (4%)
    ppermute x27, waiting for transfers between devices, exchanged(): return lax.ppermute(block, 'expert', route)  232 us
    all_to_all x4, waiting for transfers between devices, all_to_all(): lax.all_to_all(block, 'expert', split_axis=0, concat_axis=0, tiled=True)  90.4 us
    ppermute x27, starting transfers between devices, exchanged(): return lax.ppermute(block, 'expert', route)  34.5 us
    all_to_all x4, starting transfers between devices, all_to_all(): lax.all_to_all(block, 'expert', split_axis=0, concat_axis=0, tiled=True)  31.2 us
    pallas_call x2, Pallas kernels, first_stage(): pl.pallas_call(body, grid=(rows // block,), in_specs=[pl.BlockSpec((block...  15.4 us
    ppermute x2, waiting for transfers between devices, shifted(): return lax.ppermute(block, axis, route)  15.2 us
    pallas_call x2, Pallas kernels, second_stage(): pl.pallas_call(body, grid=(rows // block,), in_specs=[pl.BlockSpec((block...  14.8 us
    unnamed x60, local copies, waits for them, and re-layouts  14.6 us
  transfers between devices with their start and end apart: 33, of which 21 were waited for; matrix products, arithmetic and copies ran while one was open for 6% of the time, Pallas kernels for 8%

profile of v1, /device:TPU:1, one launch (start us, length us, event | category | flops | bytes accessed | tf_op | source)
XLA Modules:
  0.0 504.3 jit_solution(1012068024236017172)
XLA Ops:
  4.4 4.1 pack_forward.1
  8.5 11.3 %all-to-all-start = ((bf16[32,40,896]{2,1,0:T(8,128)(2,1)}), bf16[32,40,896]{2,1,0:T(8,128)(2,1)}, u32[]{:S(2)}, u32[]{:S(2)}) async-start(bf16[32,40,896]{2,1,0:T(8,128)(2,1)} %bitcast.6), calls=%async_computation | async-start | bytes 4587520 | tf_op jit(solution)/shard_map/all_to_all | solution.py:34
  21.2 2.5 pack_backward.1
  25.3 48.8 %all-to-all-done = bf16[32,40,896]{2,1,0:T(8,128)(2,1)} async-done(((bf16[32,40,896]{2,1,0:T(8,128)(2,1)}), bf16[32,40,896]{2,1,0:T(8,128)(2,1)}, u32[]{:S(2)}, u32[]{:S(2)}) %all-to-all-start) | async-done | bytes 2293792 | tf_op jit(solution)/shard_map/all_to_all | solution.py:34
  74.0 5.2 %all-to-all-start.2 = ((bf16[32,40,1152]{2,1,0:T(8,128)(2,1)}), bf16[32,40,1152]{2,1,0:T(8,128)(2,1)}, u32[]{:S(2)}, u32[]{:S(2)}) async-start(bf16[32,40,1152]{2,1,0:T(8,128)(2,1)} %bitcast.72), calls=%async_computation.2 | async-start | bytes 5898240 | tf_op jit(solution)/shard_map/all_to_all | solution.py:34
  81.7 2.6 collective-permute-start.3
  85.4 4.6 constant_dynamic-slice_fusion.1
  90.9 2.4 collective-permute-start.12
  93.3 71.9 %collective-permute-done.3.refs_3_.refs_7_ = bf16[2,896,256]{2,1,0:T(8,128)(2,1)S(1)} collective-permute-done((bf16[2,896,256]{2,1,0:T(8,128)(2,1)S(1)}, bf16[2,896,256]{2,1,0:T(8,128)(2,1)S(1)}, u32[]{:S(2)}, u32[]{:S(2)}) %collective-permute-start.3) | collective-permute-done | bytes 917536 | tf_op jit(solution)/shard_map/ppermute | solution.py:30
  165.2 18.8 %collective-permute-done.2.refs_2_.refs_6_ = bf16[2,896,256]{2,1,0:T(8,128)(2,1)S(1)} collective-permute-done((bf16[2,896,256]{2,1,0:T(8,128)(2,1)S(1)}, bf16[2,896,256]{2,1,0:T(8,128)(2,1)S(1)}, u32[]{:S(2)}, u32[]{:S(2)}) %collective-permute-start.2) | collective-permute-done | bytes 917536 | tf_op jit(solution)/shard_map/ppermute | solution.py:30
  184.0 8.7 %pre_acts.1 = (f32[1280,256]{1,0:T(8,128)}, bf16[1280,256]{1,0:T(8,128)(2,1)}, bf16[1280,256]{1,0:T(8,128)(2,1)S(1)}, bf16[1280,256]{1,0:T(8,128)(2,1)S(1)}) custom-call(bf16[1280,896]{1,0:T(8,128)(2,1)} %bitcast.7.own_ref, bf16[1280,896]{1,0:T(8,128)(2,1)} %collective-permute-done.other_ref, bf16[2,896,256]{2,1,0:T(8,128)(2,1)S(1)} %pad_maximum_fusion.refs_0_.refs_4_, ...), custom_call_target="tpu_custom_call" | custom-call | tf_op jit(solution)/shard_map/pre_acts/pallas_call | solution.py:124
  197.6 2.0 slice.44.own_ref
  199.5 8.5 %collective-permute-done.4 = bf16[1280,256]{1,0:T(8,128)(2,1)} collective-permute-done((bf16[1280,256]{1,0:T(8,128)(2,1)}, bf16[1280,256]{1,0:T(8,128)(2,1)}, u32[]{:S(2)}, u32[]{:S(2)}) %collective-permute-start.4) | collective-permute-done | bytes 655392 | tf_op jit(solution)/shard_map/ppermute | solution.py:30
  209.2 4.2 collective-permute-start.15
  213.4 9.4 %collective-permute-done.6 = bf16[1280,256]{1,0:T(8,128)(2,1)} collective-permute-done((bf16[1280,256]{1,0:T(8,128)(2,1)S(1)}, bf16[1280,256]{1,0:T(8,128)(2,1)}, u32[]{:S(2)}, u32[]{:S(2)}) %collective-permute-start.6) | collective-permute-done | bytes 655392 | tf_op jit(solution)/shard_map/ppermute | solution.py:30
  222.8 1.8 convert_add_fusion
  226.4 6.1 %collective-permute-done.11.refs_6_.refs_2_ = bf16[2,128,896]{2,1,0:T(8,128)(2,1)S(1)} collective-permute-done((bf16[2,128,896]{2,1,0:T(8,128)(2,1)}, bf16[2,128,896]{2,1,0:T(8,128)(2,1)S(1)}, u32[]{:S(2)}, u32[]{:S(2)}) %collective-permute-start.11) | collective-permute-done | bytes 458784 | tf_op jit(solution)/shard_map/ppermute | solution.py:30
  233.2 6.3 %collective-permute-done.7.refs_1_ = bf16[1280,128]{1,0:T(8,128)(2,1)S(1)} collective-permute-done((bf16[1280,128]{1,0:T(8,128)(2,1)S(1)}, bf16[1280,128]{1,0:T(8,128)(2,1)S(1)}, u32[]{:S(2)}, u32[]{:S(2)}) %collective-permute-start.7) | collective-permute-done | bytes 327712 | tf_op jit(solution)/shard_map/ppermute | solution.py:30
  239.5 7.0 %collective-permute-done.9.refs_3_ = bf16[1280,128]{1,0:T(8,128)(2,1)S(1)} collective-permute-done((bf16[1280,128]{1,0:T(8,128)(2,1)S(1)}, bf16[1280,128]{1,0:T(8,128)(2,1)S(1)}, u32[]{:S(2)}, u32[]{:S(2)}) %collective-permute-start.9) | collective-permute-done | bytes 327712 | tf_op jit(solution)/shard_map/ppermute | solution.py:30
  246.5 6.3 %y_rows.1 = (bf16[1280,896]{1,0:T(8,128)(2,1)S(1)}, bf16[1280,896]{1,0:T(8,128)(2,1)}) custom-call(bf16[1280,128]{1,0:T(8,128)(2,1)S(1)} %fusion.11.refs_0_, bf16[1280,128]{1,0:T(8,128)(2,1)S(1)} %collective-permute-done.7.refs_1_, bf16[1280,128]{1,0:T(8,128)(2,1)S(1)} %collective-permute-done.8.refs_2_, ...), custom_call_target="tpu_custom_call" | custom-call | tf_op jit(solution)/shard_map/y_rows/pallas_call | solution.py:148
  252.9 2.5 collective-permute-start.13
  256.8 6.7 %raw_grad.1 = (f32[1280,128]{1,0:T(8,128)S(1)}, bf16[1280,128]{1,0:T(8,128)(2,1)S(1)}, bf16[1280,128]{1,0:T(8,128)(2,1)S(1)}, bf16[1280,128]{1,0:T(8,128)(2,1)S(1)}) custom-call(bf16[1280,896]{1,0:T(8,128)(2,1)S(1)} %slice.44.own_ref, bf16[1280,896]{1,0:T(8,128)(2,1)} %copy-done.18, bf16[2,128,896]{2,1,0:T(8,128)(2,1)S(1)} %pad_maximum_fusion.5.refs_4_.refs_0_, ...), custom_call_target="tpu_custom_call" | custom-call | tf_op jit(solution)/shard_map/raw_grad/pallas_call | solution.py:124
  266.3 6.7 %collective-permute-done.16 = bf16[1280,128]{1,0:T(8,128)(2,1)S(1)} collective-permute-done((bf16[1280,128]{1,0:T(8,128)(2,1)S(1)}, bf16[1280,128]{1,0:T(8,128)(2,1)S(1)}, u32[]{:S(2)}, u32[]{:S(2)}) %collective-permute-start.16) | collective-permute-done | bytes 327712 | tf_op jit(solution)/shard_map/ppermute | solution.py:30
  273.8 7.0 %collective-permute-done.18 = bf16[1280,128]{1,0:T(8,128)(2,1)S(1)} collective-permute-done((bf16[1280,128]{1,0:T(8,128)(2,1)S(1)}, bf16[1280,128]{1,0:T(8,128)(2,1)S(1)}, u32[]{:S(2)}, u32[]{:S(2)}) %collective-permute-start.18) | collective-permute-done | bytes 327712 | tf_op jit(solution)/shard_map/ppermute | solution.py:30
  280.8 2.3 multiply_reduce_fusion
  283.1 2.0 add_convert_fusion.1
  285.1 8.4 %all-to-all-start.1 = ((bf16[32,40,896]{2,1,0:T(8,128)(2,1)}), bf16[32,40,896]{2,1,0:T(8,128)(2,1)S(1)}, u32[]{:S(2)}, u32[]{:S(2)}) async-start(bf16[32,40,896]{2,1,0:T(8,128)(2,1)} %bitcast.84), calls=%async_computation.1 | async-start | bytes 4587520 | tf_op jit(solution)/shard_map/all_to_all | solution.py:34
  293.6 1.8 fusion.5
  298.2 24.7 %collective-permute-done.19.refs_1_ = bf16[1280,256]{1,0:T(8,128)(2,1)S(1)} collective-permute-done((bf16[1280,256]{1,0:T(8,128)(2,1)S(1)}, bf16[1280,256]{1,0:T(8,128)(2,1)S(1)}, u32[]{:S(2)}, u32[]{:S(2)}) %collective-permute-start.19) | collective-permute-done | bytes 655392 | tf_op jit(solution)/shard_map/ppermute | solution.py:30
  322.9 36.0 %collective-permute-done.20.refs_2_ = bf16[1280,256]{1,0:T(8,128)(2,1)S(1)} collective-permute-done((bf16[1280,256]{1,0:T(8,128)(2,1)S(1)}, bf16[1280,256]{1,0:T(8,128)(2,1)S(1)}, u32[]{:S(2)}, u32[]{:S(2)}) %collective-permute-start.20) | collective-permute-done | bytes 655392 | tf_op jit(solution)/shard_map/ppermute | solution.py:30
  359.0 14.9 %collective-permute-done.21.refs_3_ = bf16[1280,256]{1,0:T(8,128)(2,1)S(1)} collective-permute-done((bf16[1280,256]{1,0:T(8,128)(2,1)S(1)}, bf16[1280,256]{1,0:T(8,128)(2,1)S(1)}, u32[]{:S(2)}, u32[]{:S(2)}) %collective-permute-start.21) | collective-permute-done | bytes 655392 | tf_op jit(solution)/shard_map/ppermute | solution.py:30
  373.9 8.4 %d_rows.1 = (bf16[1280,896]{1,0:T(8,128)(2,1)}, bf16[1280,896]{1,0:T(8,128)(2,1)}) custom-call(bf16[1280,256]{1,0:T(8,128)(2,1)S(1)} %pad_maximum_fusion.4.refs_0_, bf16[1280,256]{1,0:T(8,128)(2,1)S(1)} %collective-permute-done.19.refs_1_, bf16[1280,256]{1,0:T(8,128)(2,1)S(1)} %collective-permute-done.20.refs_2_, ...), custom_call_target="tpu_custom_call" | custom-call | tf_op jit(solution)/shard_map/d_rows/pallas_call | solution.py:148
  383.3 4.3 collective-permute-done.22
  387.6 2.9 add_convert_fusion
  390.5 1.7 broadcast_select_fusion
  393.7 6.3 %all-to-all-start.3 = ((bf16[32,40,896]{2,1,0:T(8,128)(2,1)}), bf16[32,40,896]{2,1,0:T(8,128)(2,1)S(1)}, u32[]{:S(2)}, u32[]{:S(2)}) async-start(bf16[32,40,896]{2,1,0:T(8,128)(2,1)} %broadcast_select_fusion), calls=%async_computation.3 | async-start | bytes 4587520 | tf_op jit(solution)/shard_map/all_to_all | solution.py:34
  405.9 4.0 combine_forward.1
  409.9 2.6 collective-permute-start.14
  412.6 41.6 %all-to-all-done.3 = bf16[32,40,896]{2,1,0:T(8,128)(2,1)S(1)} async-done(((bf16[32,40,896]{2,1,0:T(8,128)(2,1)}), bf16[32,40,896]{2,1,0:T(8,128)(2,1)S(1)}, u32[]{:S(2)}, u32[]{:S(2)}) %all-to-all-start.3) | async-done | bytes 2293792 | tf_op jit(solution)/shard_map/all_to_all | solution.py:34
  458.6 2.9 collective-permute-done.25
  461.6 1.9 collective-permute-start.26
  463.5 2.2 collective-permute-done.26
  467.2 3.1 collective-permute-done.27
  470.4 3.5 collective-permute-start.28
  475.3 2.7 combine_backward.1
  478.0 6.5 %collective-permute-start.23 = (bf16[64,7168]{1,0:T(8,128)(2,1)S(1)}, bf16[64,7168]{1,0:T(8,128)(2,1)S(1)}, u32[]{:S(2)}, u32[]{:S(2)}) collective-permute-start(bf16[64,7168]{1,0:T(8,128)(2,1)S(1)} %combine_backward.1), channel_id=1, source_target_pairs={{32,0},{64,32},{96,64},{128,96},{160,128},{192,160},{224,192},{0,2... | collective-permute-start | bytes 2752520 | tf_op jit(solution)/shard_map/ppermute | solution.py:25
  486.1 15.2 %collective-permute-done.23 = bf16[64,7168]{1,0:T(8,128)(2,1)S(1)} collective-permute-done((bf16[64,7168]{1,0:T(8,128)(2,1)S(1)}, bf16[64,7168]{1,0:T(8,128)(2,1)S(1)}, u32[]{:S(2)}, u32[]{:S(2)}) %collective-permute-start.23) | collective-permute-done | bytes 917536 | tf_op jit(solution)/shard_map/ppermute | solution.py:25
  501.2 2.2 copy.169
  (173 shorter events, 45.5 us)
Async XLA Ops:
  0.6 399.7 %copy-start = (bf16[1,64,7168]{2,1,0:T(8,128)(2,1)S(1)}, bf16[1,64,7168]{2,1,0:T(8,128)(2,1)}, u32[]{:S(2)}) copy-start(bf16[1,64,7168]{2,1,0:T(8,128)(2,1)} %param.12) | copy-start | bytes 2752516
  8.5 11.3 %copy-start.25 = (s32[1,64,2]{1,2,0:T(2,128)S(1)}, s32[1,64,2]{1,2,0:T(2,128)}, u32[]{:S(2)}) copy-start(s32[1,64,2]{1,2,0:T(2,128)} %param.13) | copy-start | bytes 1540
  8.5 12.5 %copy-start.23 = (bf16[1,64,2,2,1024]{4,3,2,1,0:T(2,128)(2,1)S(1)}, bf16[1,64,2,2,1024]{4,3,2,1,0:T(2,128)(2,1)}, u32[]{:S(2)}) copy-start(bf16[1,64,2,2,1024]{4,3,2,1,0:T(2,128)(2,1)} %param.15) | copy-start | bytes 1572868
  8.5 12.7 %copy-start.6 = (bf16[1,64,7168]{2,1,0:T(8,128)(2,1)S(1)}, bf16[1,64,7168]{2,1,0:T(8,128)(2,1)}, u32[]{:S(2)}) copy-start(bf16[1,64,7168]{2,1,0:T(8,128)(2,1)} %param.14) | copy-start | bytes 2752516
  8.5 65.5 %all-to-all-start = ((bf16[32,40,896]{2,1,0:T(8,128)(2,1)}), bf16[32,40,896]{2,1,0:T(8,128)(2,1)}, u32[]{:S(2)}, u32[]{:S(2)}) async-start(bf16[32,40,896]{2,1,0:T(8,128)(2,1)} %bitcast.6), calls=%async_computation | async-start | bytes 4587520 | tf_op jit(solution)/shard_map/all_to_all | solution.py:34
  74.0 123.5 %all-to-all-start.2 = ((bf16[32,40,1152]{2,1,0:T(8,128)(2,1)}), bf16[32,40,1152]{2,1,0:T(8,128)(2,1)}, u32[]{:S(2)}, u32[]{:S(2)}) async-start(bf16[32,40,1152]{2,1,0:T(8,128)(2,1)} %bitcast.72), calls=%async_computation.2 | async-start | bytes 5898240 | tf_op jit(solution)/shard_map/all_to_all | solution.py:34
  79.2 104.7 %collective-permute-start = (bf16[1280,896]{1,0:T(8,128)(2,1)}, bf16[1280,896]{1,0:T(8,128)(2,1)}, u32[]{:S(2)}, u32[]{:S(2)}) collective-permute-start(bf16[1280,896]{1,0:T(8,128)(2,1)} %bitcast.7.own_ref), channel_id=1, source_target_pairs={{0,1},{1,0},{2,3},{3,2},{4,5},{5,4},{6,7},{7,6},{8,9},{9,8},{10,11... | collective-permute-start | bytes 6881288 | tf_op jit(solution)/shard_map/ppermute | solution.py:30
  81.7 83.4 %collective-permute-start.3 = (bf16[2,896,256]{2,1,0:T(8,128)(2,1)S(1)}, bf16[2,896,256]{2,1,0:T(8,128)(2,1)S(1)}, u32[]{:S(2)}, u32[]{:S(2)}) collective-permute-start(bf16[2,896,256]{2,1,0:T(8,128)(2,1)S(1)} %pad_maximum_fusion.3), channel_id=1, source_target_pairs={{0,6},{1,7},{2,4},{3,5},{4,2},{5,3},{6,0},{7,1},{8,14},{9,15},{10,... | collective-permute-start | bytes 2752520 | tf_op jit(solution)/shard_map/ppermute | solution.py:30
  84.5 99.5 %collective-permute-start.2 = (bf16[2,896,256]{2,1,0:T(8,128)(2,1)S(1)}, bf16[2,896,256]{2,1,0:T(8,128)(2,1)S(1)}, u32[]{:S(2)}, u32[]{:S(2)}) collective-permute-start(bf16[2,896,256]{2,1,0:T(8,128)(2,1)S(1)} %pad_maximum_fusion.2), channel_id=1, source_target_pairs={{0,4},{1,5},{2,6},{3,7},{4,0},{5,1},{6,2},{7,3},{8,12},{9,13},{10,... | collective-permute-start | bytes 2752520 | tf_op jit(solution)/shard_map/ppermute | solution.py:30
  84.7 99.2 %collective-permute-start.1 = (bf16[2,896,256]{2,1,0:T(8,128)(2,1)S(1)}, bf16[2,896,256]{2,1,0:T(8,128)(2,1)S(1)}, u32[]{:S(2)}, u32[]{:S(2)}) collective-permute-start(bf16[2,896,256]{2,1,0:T(8,128)(2,1)S(1)} %pad_maximum_fusion.1), channel_id=1, source_target_pairs={{0,2},{1,3},{2,0},{3,1},{4,6},{5,7},{6,4},{7,5},{8,10},{9,11},{10,... | collective-permute-start | bytes 2752520 | tf_op jit(solution)/shard_map/ppermute | solution.py:30
  90.9 135.2 %collective-permute-start.12 = (bf16[2,128,896]{2,1,0:T(8,128)(2,1)}, bf16[2,128,896]{2,1,0:T(8,128)(2,1)S(1)}, u32[]{:S(2)}, u32[]{:S(2)}) collective-permute-start(bf16[2,128,896]{2,1,0:T(8,128)(2,1)} %pad_maximum_fusion.8), channel_id=1, source_target_pairs={{0,6},{1,7},{2,4},{3,5},{4,2},{5,3},{6,0},{7,1},{8,14},{9,15},{10,... | collective-permute-start | bytes 1376264 | tf_op jit(solution)/shard_map/ppermute | solution.py:30
  93.3 99.4 %copy-start.4 = (bf16[2,896,256]{2,1,0:T(8,128)(2,1)}, bf16[2,896,256]{2,1,0:T(8,128)(2,1)S(1)}, u32[]{:S(2)}) copy-start(bf16[2,896,256]{2,1,0:T(8,128)(2,1)S(1)} %pad_maximum_fusion.refs_0_.refs_4_) | copy-start | bytes 2752516
  165.2 27.5 %copy-start.8 = (bf16[2,896,256]{2,1,0:T(8,128)(2,1)}, bf16[2,896,256]{2,1,0:T(8,128)(2,1)S(1)}, u32[]{:S(2)}) copy-start(bf16[2,896,256]{2,1,0:T(8,128)(2,1)S(1)} %collective-permute-done.3.refs_3_.refs_7_) | copy-start | bytes 2752516
  183.9 8.7 %copy-start.11 = (bf16[2,896,256]{2,1,0:T(8,128)(2,1)}, bf16[2,896,256]{2,1,0:T(8,128)(2,1)S(1)}, u32[]{:S(2)}) copy-start(bf16[2,896,256]{2,1,0:T(8,128)(2,1)S(1)} %collective-permute-done.1.refs_1_.refs_5_) | copy-start | bytes 2752516
  192.7 15.3 %collective-permute-start.4 = (bf16[1280,256]{1,0:T(8,128)(2,1)}, bf16[1280,256]{1,0:T(8,128)(2,1)}, u32[]{:S(2)}, u32[]{:S(2)}) collective-permute-start(bf16[1280,256]{1,0:T(8,128)(2,1)} %get-tuple-element.16), channel_id=1, source_target_pairs={{0,2},{1,3},{2,0},{3,1},{4,6},{5,7},{6,4},{7,5},{8,10},{9,11},{10,... | collective-permute-start | bytes 1966088 | tf_op jit(solution)/shard_map/ppermute | solution.py:30
  194.0 15.2 %collective-permute-start.5 = (bf16[1280,256]{1,0:T(8,128)(2,1)S(1)}, bf16[1280,256]{1,0:T(8,128)(2,1)}, u32[]{:S(2)}, u32[]{:S(2)}) collective-permute-start(bf16[1280,256]{1,0:T(8,128)(2,1)S(1)} %get-tuple-element.17), channel_id=1, source_target_pairs={{0,4},{1,5},{2,6},{3,7},{4,0},{5,1},{6,2},{7,3},{8,12},{9,13},{10,... | collective-permute-start | bytes 1966088 | tf_op jit(solution)/shard_map/ppermute | solution.py:30
  194.3 28.4 %collective-permute-start.6 = (bf16[1280,256]{1,0:T(8,128)(2,1)S(1)}, bf16[1280,256]{1,0:T(8,128)(2,1)}, u32[]{:S(2)}, u32[]{:S(2)}) collective-permute-start(bf16[1280,256]{1,0:T(8,128)(2,1)S(1)} %get-tuple-element.18), channel_id=1, source_target_pairs={{0,6},{1,7},{2,4},{3,5},{4,2},{5,3},{6,0},{7,1},{8,14},{9,15},{10,... | collective-permute-start | bytes 1966088 | tf_op jit(solution)/shard_map/ppermute | solution.py:30
  196.3 36.1 %collective-permute-start.11 = (bf16[2,128,896]{2,1,0:T(8,128)(2,1)}, bf16[2,128,896]{2,1,0:T(8,128)(2,1)S(1)}, u32[]{:S(2)}, u32[]{:S(2)}) collective-permute-start(bf16[2,128,896]{2,1,0:T(8,128)(2,1)} %pad_maximum_fusion.7), channel_id=1, source_target_pairs={{0,4},{1,5},{2,6},{3,7},{4,0},{5,1},{6,2},{7,3},{8,12},{9,13},{10,... | collective-permute-start | bytes 1376264 | tf_op jit(solution)/shard_map/ppermute | solution.py:30
  197.5 10.4 %copy-start.24 = (bf16[2,128,896]{2,1,0:T(8,128)(2,1)S(1)}, bf16[2,128,896]{2,1,0:T(8,128)(2,1)}, u32[]{:S(2)}) copy-start(bf16[2,128,896]{2,1,0:T(8,128)(2,1)} %pad_maximum_fusion.6) | copy-start | bytes 1376260
  197.6 25.2 %copy-start.22 = (f32[1280,256]{1,0:T(8,128)S(1)}, f32[1280,256]{1,0:T(8,128)}, u32[]{:S(2)}) copy-start(f32[1280,256]{1,0:T(8,128)} %get-tuple-element.15) | copy-start | bytes 3932164
  208.0 25.2 %collective-permute-start.10 = (bf16[2,128,896]{2,1,0:T(8,128)(2,1)S(1)}, bf16[2,128,896]{2,1,0:T(8,128)(2,1)S(1)}, u32[]{:S(2)}, u32[]{:S(2)}) collective-permute-start(bf16[2,128,896]{2,1,0:T(8,128)(2,1)S(1)} %copy-done.24), channel_id=1, source_target_pairs={{0,2},{1,3},{2,0},{3,1},{4,6},{5,7},{6,4},{7,5},{8,10},{9,11},{10,... | collective-permute-start | bytes 1376264 | tf_op jit(solution)/shard_map/ppermute | solution.py:30
  209.2 46.3 %collective-permute-start.15 = (bf16[1280,896]{1,0:T(8,128)(2,1)S(1)}, bf16[1280,896]{1,0:T(8,128)(2,1)S(1)}, u32[]{:S(2)}, u32[]{:S(2)}) collective-permute-start(bf16[1280,896]{1,0:T(8,128)(2,1)S(1)} %slice.44.own_ref), channel_id=1, source_target_pairs={{0,1},{1,0},{2,3},{3,2},{4,5},{5,4},{6,7},{7,6},{8,9},{9,8},{10,11... | collective-permute-start | bytes 6881288 | tf_op jit(solution)/shard_map/ppermute | solution.py:30
  222.8 10.3 %copy-start.19 = (bf16[128,1,896]{2,1,0:T(2,128)(2,1)S(1)}, bf16[128,1,896]{2,1,0:T(2,128)(2,1)}, u32[]{:S(2)}) copy-start(bf16[128,1,896]{2,1,0:T(2,128)(2,1)} %get-tuple-element.46) | copy-start | bytes 688132
  222.8 10.3 %copy-start.20 = (bf16[128,1,896]{2,1,0:T(2,128)(2,1)S(1)}, bf16[128,1,896]{2,1,0:T(2,128)(2,1)}, u32[]{:S(2)}) copy-start(bf16[128,1,896]{2,1,0:T(2,128)(2,1)} %get-tuple-element.47) | copy-start | bytes 688132
  224.8 14.7 %collective-permute-start.7 = (bf16[1280,128]{1,0:T(8,128)(2,1)S(1)}, bf16[1280,128]{1,0:T(8,128)(2,1)S(1)}, u32[]{:S(2)}, u32[]{:S(2)}) collective-permute-start(bf16[1280,128]{1,0:T(8,128)(2,1)S(1)} %fusion.11.refs_0_), channel_id=1, source_target_pairs={{0,2},{1,3},{2,0},{3,1},{4,6},{5,7},{6,4},{7,5},{8,10},{9,11},{10,... | collective-permute-start | bytes 983048 | tf_op jit(solution)/shard_map/ppermute | solution.py:30
  226.1 13.5 %collective-permute-start.8 = (bf16[1280,128]{1,0:T(8,128)(2,1)S(1)}, bf16[1280,128]{1,0:T(8,128)(2,1)S(1)}, u32[]{:S(2)}, u32[]{:S(2)}) collective-permute-start(bf16[1280,128]{1,0:T(8,128)(2,1)S(1)} %fusion.11.refs_0_), channel_id=1, source_target_pairs={{0,4},{1,5},{2,6},{3,7},{4,0},{5,1},{6,2},{7,3},{8,12},{9,13},{10,... | collective-permute-start | bytes 983048 | tf_op jit(solution)/shard_map/ppermute | solution.py:30
  232.5 14.0 %collective-permute-start.9 = (bf16[1280,128]{1,0:T(8,128)(2,1)S(1)}, bf16[1280,128]{1,0:T(8,128)(2,1)S(1)}, u32[]{:S(2)}, u32[]{:S(2)}) collective-permute-start(bf16[1280,128]{1,0:T(8,128)(2,1)S(1)} %fusion.11.refs_0_), channel_id=1, source_target_pairs={{0,6},{1,7},{2,4},{3,5},{4,2},{5,3},{6,0},{7,1},{8,14},{9,15},{10,... | collective-permute-start | bytes 983048 | tf_op jit(solution)/shard_map/ppermute | solution.py:30
  252.9 30.2 %collective-permute-start.13 = (bf16[1280,896]{1,0:T(8,128)(2,1)}, bf16[1280,896]{1,0:T(8,128)(2,1)S(1)}, u32[]{:S(2)}, u32[]{:S(2)}) collective-permute-start(bf16[1280,896]{1,0:T(8,128)(2,1)} %get-tuple-element.20), channel_id=1, source_target_pairs={{0,1},{1,0},{2,3},{3,2},{4,5},{5,4},{6,7},{7,6},{8,9},{9,8},{10,11... | collective-permute-start | bytes 6881288 | tf_op jit(solution)/shard_map/ppermute | solution.py:30
  263.5 9.4 %collective-permute-start.16 = (bf16[1280,128]{1,0:T(8,128)(2,1)S(1)}, bf16[1280,128]{1,0:T(8,128)(2,1)S(1)}, u32[]{:S(2)}, u32[]{:S(2)}) collective-permute-start(bf16[1280,128]{1,0:T(8,128)(2,1)S(1)} %get-tuple-element.22), channel_id=1, source_target_pairs={{0,2},{1,3},{2,0},{3,1},{4,6},{5,7},{6,4},{7,5},{8,10},{9,11},{10,... | collective-permute-start | bytes 983048 | tf_op jit(solution)/shard_map/ppermute | solution.py:30
  264.8 9.0 %collective-permute-start.17 = (bf16[1280,128]{1,0:T(8,128)(2,1)S(1)}, bf16[1280,128]{1,0:T(8,128)(2,1)S(1)}, u32[]{:S(2)}, u32[]{:S(2)}) collective-permute-start(bf16[1280,128]{1,0:T(8,128)(2,1)S(1)} %get-tuple-element.23), channel_id=1, source_target_pairs={{0,4},{1,5},{2,6},{3,7},{4,0},{5,1},{6,2},{7,3},{8,12},{9,13},{10,... | collective-permute-start | bytes 983048 | tf_op jit(solution)/shard_map/ppermute | solution.py:30
  265.2 15.7 %collective-permute-start.18 = (bf16[1280,128]{1,0:T(8,128)(2,1)S(1)}, bf16[1280,128]{1,0:T(8,128)(2,1)S(1)}, u32[]{:S(2)}, u32[]{:S(2)}) collective-permute-start(bf16[1280,128]{1,0:T(8,128)(2,1)S(1)} %get-tuple-element.24), channel_id=1, source_target_pairs={{0,6},{1,7},{2,4},{3,5},{4,2},{5,3},{6,0},{7,1},{8,14},{9,15},{10,... | collective-permute-start | bytes 983048 | tf_op jit(solution)/shard_map/ppermute | solution.py:30
  285.1 107.2 %all-to-all-start.1 = ((bf16[32,40,896]{2,1,0:T(8,128)(2,1)}), bf16[32,40,896]{2,1,0:T(8,128)(2,1)S(1)}, u32[]{:S(2)}, u32[]{:S(2)}) async-start(bf16[32,40,896]{2,1,0:T(8,128)(2,1)} %bitcast.84), calls=%async_computation.1 | async-start | bytes 4587520 | tf_op jit(solution)/shard_map/all_to_all | solution.py:34
  293.5 80.4 %copy-start.5 = (bf16[2,896,256]{2,1,0:T(8,128)(2,1)S(1)}, bf16[2,896,256]{2,1,0:T(8,128)(2,1)}, u32[]{:S(2)}) copy-start(bf16[2,896,256]{2,1,0:T(8,128)(2,1)} %copy-done.4) | copy-start | bytes 2752516
  293.5 80.4 %copy-start.10 = (bf16[2,896,256]{2,1,0:T(8,128)(2,1)S(1)}, bf16[2,896,256]{2,1,0:T(8,128)(2,1)}, u32[]{:S(2)}) copy-start(bf16[2,896,256]{2,1,0:T(8,128)(2,1)} %copy-done.9) | copy-start | bytes 2752516
  293.5 80.4 %copy-start.12 = (bf16[2,896,256]{2,1,0:T(8,128)(2,1)S(1)}, bf16[2,896,256]{2,1,0:T(8,128)(2,1)}, u32[]{:S(2)}) copy-start(bf16[2,896,256]{2,1,0:T(8,128)(2,1)} %copy-done.11) | copy-start | bytes 2752516
  295.4 27.5 %collective-permute-start.19 = (bf16[1280,256]{1,0:T(8,128)(2,1)S(1)}, bf16[1280,256]{1,0:T(8,128)(2,1)S(1)}, u32[]{:S(2)}, u32[]{:S(2)}) collective-permute-start(bf16[1280,256]{1,0:T(8,128)(2,1)S(1)} %pad_maximum_fusion.4.refs_0_), channel_id=1, source_target_pairs={{0,2},{1,3},{2,0},{3,1},{4,6},{5,7},{6,4},{7,5},{8,10},{9,11},{10,... | collective-permute-start | bytes 1966088 | tf_op jit(solution)/shard_map/ppermute | solution.py:30
  296.9 62.1 %collective-permute-start.20 = (bf16[1280,256]{1,0:T(8,128)(2,1)S(1)}, bf16[1280,256]{1,0:T(8,128)(2,1)S(1)}, u32[]{:S(2)}, u32[]{:S(2)}) collective-permute-start(bf16[1280,256]{1,0:T(8,128)(2,1)S(1)} %pad_maximum_fusion.4.refs_0_), channel_id=1, source_target_pairs={{0,4},{1,5},{2,6},{3,7},{4,0},{5,1},{6,2},{7,3},{8,12},{9,13},{10,... | collective-permute-start | bytes 1966088 | tf_op jit(solution)/shard_map/ppermute | solution.py:30
  298.1 75.8 %collective-permute-start.21 = (bf16[1280,256]{1,0:T(8,128)(2,1)S(1)}, bf16[1280,256]{1,0:T(8,128)(2,1)S(1)}, u32[]{:S(2)}, u32[]{:S(2)}) collective-permute-start(bf16[1280,256]{1,0:T(8,128)(2,1)S(1)} %pad_maximum_fusion.4.refs_0_), channel_id=1, source_target_pairs={{0,6},{1,7},{2,4},{3,5},{4,2},{5,3},{6,0},{7,1},{8,14},{9,15},{10,... | collective-permute-start | bytes 1966088 | tf_op jit(solution)/shard_map/ppermute | solution.py:30
  382.3 5.3 %collective-permute-start.22 = (bf16[1280,896]{1,0:T(8,128)(2,1)}, bf16[1280,896]{1,0:T(8,128)(2,1)}, u32[]{:S(2)}, u32[]{:S(2)}) collective-permute-start(bf16[1280,896]{1,0:T(8,128)(2,1)} %get-tuple-element.26), channel_id=1, source_target_pairs={{0,1},{1,0},{2,3},{3,2},{4,5},{5,4},{6,7},{7,6},{8,9},{9,8},{10,11... | collective-permute-start | bytes 6881288 | tf_op jit(solution)/shard_map/ppermute | solution.py:30
  392.3 10.2 %copy-start.26 = (s32[1,64,2]{1,2,0:T(2,128)S(1)}, s32[1,64,2]{1,2,0:T(2,128)}, u32[]{:S(2)}) copy-start(s32[1,64,2]{1,2,0:T(2,128)} %param.11) | copy-start | bytes 1540
  393.7 60.5 %all-to-all-start.3 = ((bf16[32,40,896]{2,1,0:T(8,128)(2,1)}), bf16[32,40,896]{2,1,0:T(8,128)(2,1)S(1)}, u32[]{:S(2)}, u32[]{:S(2)}) async-start(bf16[32,40,896]{2,1,0:T(8,128)(2,1)} %broadcast_select_fusion), calls=%async_computation.3 | async-start | bytes 4587520 | tf_op jit(solution)/shard_map/all_to_all | solution.py:34
  409.9 64.1 %collective-permute-start.14 = (bf16[64,7168]{1,0:T(8,128)(2,1)}, bf16[64,7168]{1,0:T(8,128)(2,1)}, u32[]{:S(2)}, u32[]{:S(2)}) collective-permute-start(bf16[64,7168]{1,0:T(8,128)(2,1)} %combine_forward.1), channel_id=1, source_target_pairs={{224,0},{0,32},{32,64},{64,96},{96,128},{128,160},{160,192},{192,2... | collective-permute-start | bytes 2752520 | tf_op jit(solution)/shard_map/ppermute | solution.py:25
  455.5 1.5 collective-permute-start.24
  457.1 4.5 collective-permute-start.25
  461.6 4.1 collective-permute-start.26
  465.7 4.6 collective-permute-start.27
  470.4 14.1 %collective-permute-start.28 = (f32[4,7168]{1,0:T(4,128)S(1)}, f32[4,7168]{1,0:T(4,128)}, u32[]{:S(2)}, u32[]{:S(2)}) collective-permute-start(f32[4,7168]{1,0:T(4,128)S(1)} %add.193), channel_id=1, source_target_pairs={{0,16},{1,17},{2,18},{3,19},{4,20},{5,21},{6,22},{7,23},{8,24},{9,... | collective-permute-start | bytes 344072 | tf_op jit(solution)/shard_map/ppermute | solution.py:30
  478.0 23.2 %collective-permute-start.23 = (bf16[64,7168]{1,0:T(8,128)(2,1)S(1)}, bf16[64,7168]{1,0:T(8,128)(2,1)S(1)}, u32[]{:S(2)}, u32[]{:S(2)}) collective-permute-start(bf16[64,7168]{1,0:T(8,128)(2,1)S(1)} %combine_backward.1), channel_id=1, source_target_pairs={{32,0},{64,32},{96,64},{128,96},{160,128},{192,160},{224,192},{0,2... | collective-permute-start | bytes 2752520 | tf_op jit(solution)/shard_map/ppermute | solution.py:25
  (12 other events, 37.0 us)

commit v2 on v1

v2 whole, which is shorter than its diff:
```python
import jax
import jax.numpy as jnp
from jax import lax
from jax.experimental import pallas as pl
from jax.experimental.pallas import tpu as pltpu
from jax.sharding import PartitionSpec as P

CAP = 40
ROUTE_SCALE = 2.5
BF = jnp.bfloat16
F32 = jnp.float32
USED = 36
VMEM_BYTES = 48 * 1024 * 1024


def params(steps):
    return pltpu.CompilerParams(
        dimension_semantics=("arbitrary",) * steps, vmem_limit_bytes=VMEM_BYTES
    )


def shifted(block, axis, distance):
    devices = range(lax.axis_size(axis))
    route = [((i - distance) % len(devices), i) for i in devices]
    return lax.ppermute(block, axis, route)


def exchanged(block, mask):
    route = [(i, i ^ mask) for i in range(lax.axis_size("expert"))]
    return lax.ppermute(block, "expert", route)


def all_to_all(block):
    return lax.all_to_all(block, "expert", split_axis=0, concat_axis=0, tiled=True)


def piece_route(piece):
    members = lax.axis_size("expert")
    step = (0, 2, -1, -3)[piece]
    return [(i, (i + 4 * (step if i // 4 % 2 == 0 else -step)) % members) for i in range(members)]


def hopped(block, piece):
    return lax.ppermute(block, "expert", piece_route(piece))


def to_source(block, piece):
    if not piece:
        return block
    return lax.ppermute(block, "expert", [(b, a) for a, b in piece_route(piece)])


def gate_terms(tok_rows, ids, router_rows):
    experts = router_rows.shape[0]
    logits = lax.dot_general(
        tok_rows, router_rows, (((1,), (1,)), ((), ())), preferred_element_type=F32
    )
    one_hot = (ids[:, :, None] == jnp.arange(experts, dtype=jnp.int32)[None, None, :]).astype(F32)
    probs_m = jax.nn.sigmoid(jnp.sum(one_hot * logits[:, None, :], axis=2))
    total_m = jnp.sum(probs_m, axis=1, keepdims=True)
    return one_hot, probs_m, total_m


def route_plan(ids, experts, level):
    tokens, top = ids.shape
    flat_ids = ids.reshape(tokens * top)
    one_hot = (flat_ids[:, None] == jnp.arange(experts, dtype=jnp.int32)[None, :]).astype(jnp.int32)
    before = jnp.cumsum(one_hot, axis=0) - one_hot
    rank = jnp.sum(before * one_hot, axis=1)
    ahead = flat_ids - level // 2
    ahead = jnp.where(level % 2 == 0, ahead, -ahead) % experts
    piece = jnp.where(ahead == 2, 3, jnp.where(ahead == 3, 2, ahead))
    return (piece * CAP + rank).reshape(tokens, top)


def pack(core, select_f, select_b, select_pairs, rows_f, rows_b, stash, hidden):
    tokens, features = rows_f.shape
    slots, pairs = select_pairs.shape
    lanes = stash.shape[1]
    quarter = lanes // 4
    chips = quarter // hidden
    total = 2 * features + lanes
    block = total // 4

    def body(core_ref, f_ref, b_ref, pairs_ref, rows_f_ref, rows_b_ref, stash_ref, *out_refs):
        def spread(select_ref, source, at):
            got = jnp.dot(select_ref[...], source, preferred_element_type=F32)
            for k in range(2):
                half = got[k * slots // 2 : (k + 1) * slots // 2]
                out_refs[k][:, at : at + source.shape[1]] = half.astype(BF)

        def fill(step):
            first, last = step * block, (step + 1) * block
            for select_ref, ref, start in ((f_ref, rows_f_ref, 0), (b_ref, rows_b_ref, features)):
                low, high = max(first, start), min(last, start + features)
                if low < high:
                    spread(select_ref, ref[:, low - start : high - start], low - first)
            for place in range(4 * chips):
                at = 2 * features + place * hidden
                if first <= at < last:
                    owner = (core_ref[0] + 1 + place // (2 * chips)) % 2
                    part, chip = place // chips % 2, place % chips
                    start = part * 2 * quarter + (2 * chip + owner) * hidden
                    source = stash_ref[:, pl.ds(pl.multiple_of(start, hidden), hidden)]
                    spread(pairs_ref, source, at - first)

        for step in range(4):
            pl.when(pl.program_id(0) == step)(lambda step=step: fill(step))

    def whole(array):
        return pl.BlockSpec(array.shape, lambda j: (0, 0))

    return pl.pallas_call(
        body,
        grid=(4,),
        in_specs=[pl.BlockSpec(memory_space=pltpu.SMEM)]
        + [whole(a) for a in (select_f, select_b, select_pairs, rows_f, rows_b, stash)],
        out_specs=[pl.BlockSpec((slots // 2, block), lambda j: (0, j))] * 2,
        out_shape=[jax.ShapeDtypeStruct((slots // 2, total), BF)] * 2,
        compiler_params=params(1),
        name="pack",
    )(core, select_f, select_b, select_pairs, rows_f, rows_b, stash)


def contract(left, right, right_dim):
    return lax.dot_general(left, right, (((1,), (right_dim,)), ((), ())), preferred_element_type=F32)


def silu_slope(pre_act):
    sigmoid_v = jax.nn.sigmoid(pre_act)
    return sigmoid_v * (1.0 + pre_act * (1.0 - sigmoid_v))


def backward_first(chip, parts, downs):
    rows = parts[0].shape[0]
    chips, count = len(downs), len(parts)
    hidden, features = downs[0].shape
    block = 1792
    steps = features // block
    wide = 2 * chips * hidden

    def body(chip_ref, *refs):
        row_refs, stash_refs, refs = refs[:count], refs[count : 2 * count], refs[2 * count :]
        w_refs, (d_ref, inner_ref, total) = refs[:chips], refs[chips:]
        step = pl.program_id(0)
        left = jnp.concatenate([ref[...] for ref in row_refs], axis=0)
        right = jnp.concatenate([ref[...] for ref in w_refs], axis=0)
        got = contract(left, right, 1)

        @pl.when(step == 0)
        def _():
            total[...] = got

        @pl.when(step > 0)
        def _():
            total[...] += got

        @pl.when(step == steps - 1)
        def _():
            for part, stash_ref in enumerate(stash_refs):
                place = slice(part * rows, (part + 1) * rows)
                inner = jnp.zeros((rows, 1), F32)
                for s in range(chips):
                    start = (chip_ref[0] ^ s) * hidden
                    pre_gate = stash_ref[:, pl.ds(pl.multiple_of(start, hidden), hidden)].astype(F32)
                    start = start + chips * hidden
                    pre_up = stash_ref[:, pl.ds(pl.multiple_of(start, hidden), hidden)].astype(F32)
                    raw = total[place, s * hidden : (s + 1) * hidden]
                    sigmoid_v = jax.nn.sigmoid(pre_gate)
                    activated = pre_gate * sigmoid_v
                    slope = sigmoid_v * (1.0 + pre_gate * (1.0 - sigmoid_v))
                    hidden_b = (activated * pre_up).astype(BF).astype(F32)
                    inner += jnp.sum(hidden_b * raw, axis=1, keepdims=True)
                    at = 2 * s * hidden
                    d_ref[place, at : at + hidden] = (raw * pre_up * slope).astype(BF)
                    d_ref[place, at + hidden : at + 2 * hidden] = (raw * activated).astype(BF)
                inner_ref[place, :] = jnp.broadcast_to(inner, (rows, 128))

    return pl.pallas_call(
        body,
        grid=(steps,),
        in_specs=[pl.BlockSpec(memory_space=pltpu.SMEM)]
        + [pl.BlockSpec((rows, block), lambda j: (0, steps + j))] * count
        + [pl.BlockSpec((rows, wide), lambda j: (0, 2 * features // wide + 1))] * (count // 2)
        + [pl.BlockSpec((rows, wide), lambda j: (0, 2 * features // wide))] * (count // 2)
        + [pl.BlockSpec((hidden, block), lambda j: (0, j))] * chips,
        out_specs=[
            pl.BlockSpec((count * rows, 2 * chips * hidden), lambda j: (0, 0)),
            pl.BlockSpec((count * rows, 128), lambda j: (0, 0)),
        ],
        out_shape=[
            jax.ShapeDtypeStruct((count * rows, 2 * chips * hidden), BF),
            jax.ShapeDtypeStruct((count * rows, 128), F32),
        ],
        scratch_shapes=[pltpu.VMEM((count * rows, chips * hidden), F32)],
        compiler_params=params(1),
        name="backward_first",
    )(chip, *parts, *parts, *downs)


def backward_second(d_joined, weights):
    rows = d_joined.shape[0] // 2
    features, joined = weights[0].shape
    chips = len(weights)
    block = 1792

    def body(d_ref, *refs):
        keep_ref, give_ref = refs[chips:]
        right = jnp.concatenate([ref[...] for ref in refs[:chips]], axis=1)
        got = contract(d_ref[...], right, 1)
        keep_ref[...] = got[:rows].astype(BF)
        give_ref[...] = got[rows:].astype(BF)

    return pl.pallas_call(
        body,
        grid=(features // block,),
        in_specs=[pl.BlockSpec(d_joined.shape, lambda j: (0, 0))]
        + [pl.BlockSpec((block, joined), lambda j: (j, 0))] * chips,
        out_specs=[pl.BlockSpec((rows, block), lambda j: (0, j))] * 2,
        out_shape=[jax.ShapeDtypeStruct((rows, features), BF)] * 2,
        compiler_params=params(1),
        name="backward_second",
    )(d_joined, *weights)


def forward_first(parts, weights):
    rows, count = parts[0].shape[0], len(parts)
    features, joined = weights[0].shape
    chips = len(weights)
    hidden = joined // 2
    block = 1792
    steps = features // block

    def body(*refs):
        row_refs, refs = refs[:count], refs[count:]
        out_ref, total = refs[chips:]
        step = pl.program_id(0)
        right = jnp.concatenate([ref[...] for ref in refs[:chips]], axis=1)
        left = jnp.concatenate([ref[...] for ref in row_refs], axis=0)
        got = contract(left, right, 0)

        @pl.when(step == 0)
        def _():
            total[...] = got

        @pl.when(step > 0)
        def _():
            total[...] += got

        @pl.when(step == steps - 1)
        def _():
            for s in range(chips):
                at = 2 * s * hidden
                gate = total[:, at : at + hidden]
                up = total[:, at + hidden : at + 2 * hidden]
                out_ref[:, s * hidden : (s + 1) * hidden] = (jax.nn.silu(gate) * up).astype(BF)

    return pl.pallas_call(
        body,
        grid=(steps,),
        in_specs=[pl.BlockSpec((rows, block), lambda j: (0, j))] * count
        + [pl.BlockSpec((block, joined), lambda j: (j, 0))] * chips,
        out_specs=pl.BlockSpec((count * rows, chips * hidden), lambda j: (0, 0)),
        out_shape=jax.ShapeDtypeStruct((count * rows, chips * hidden), BF),
        scratch_shapes=[pltpu.VMEM((count * rows, chips * joined), F32)],
        compiler_params=params(1),
        name="forward_first",
    )(*parts, *weights)


def forward_second(hidden_f, downs):
    rows = hidden_f.shape[0] // 2
    hidden, features = downs[0].shape
    chips = len(downs)
    block = 1792

    def body(hidden_ref, *refs):
        keep_ref, give_ref = refs[chips:]
        right = jnp.concatenate([ref[...] for ref in refs[:chips]], axis=0)
        got = contract(hidden_ref[...], right, 0)
        keep_ref[...] = got[:rows].astype(BF)
        give_ref[...] = got[rows:].astype(BF)

    return pl.pallas_call(
        body,
        grid=(features // block,),
        in_specs=[pl.BlockSpec(hidden_f.shape, lambda j: (0, 0))]
        + [pl.BlockSpec((hidden, block), lambda j: (0, j))] * chips,
        out_specs=[pl.BlockSpec((rows, block), lambda j: (0, j))] * 2,
        out_shape=[jax.ShapeDtypeStruct((rows, features), BF)] * 2,
        compiler_params=params(1),
        name="forward_second",
    )(hidden_f, *downs)


def merged(keep, swapped):
    total = (keep.astype(F32) + swapped.astype(F32)).astype(BF)
    return [total[place * CAP : (place + 1) * CAP] for place in (0, 2, 1, 3)]


def combine(picks, factors, returned, rows, extra, name):
    tokens = rows.shape[0]
    features = returned[0].shape[1]
    block = 3584
    top, pieces = len(picks), len(returned)
    slots = picks[0].shape[1]

    def body(*refs):
        pick_refs, factor_ref, refs = refs[:top], refs[top], refs[top + 1 :]
        back_refs, rows_ref, refs = refs[:pieces], refs[pieces], refs[pieces + 1 :]
        out_ref = refs[-1]
        back = jnp.concatenate([ref[...].astype(F32) for ref in back_refs], axis=0).astype(BF)
        total = rows_ref[...].astype(F32)
        for k in range(top):
            picked = jnp.dot(pick_refs[k][...], back, preferred_element_type=F32)
            total += factor_ref[:, k : k + 1] * picked
        if extra is not None:
            score_ref, router_ref = refs[:2]
            for e in range(extra[1].shape[0]):
                total += score_ref[:, e : e + 1] * router_ref[e : e + 1, :].astype(F32)
        out_ref[...] = total.astype(BF)

    in_specs = (
        [pl.BlockSpec((tokens, slots), lambda j: (0, 0))] * top
        + [pl.BlockSpec(factors.shape, lambda j: (0, 0))]
        + [pl.BlockSpec((CAP, block), lambda j: (0, j)) for _ in range(pieces)]
        + [pl.BlockSpec((tokens, block), lambda j: (0, j))]
    )
    operands = list(picks) + [factors] + list(returned) + [rows]
    if extra is not None:
        in_specs += [
            pl.BlockSpec(extra[0].shape, lambda j: (0, 0)),
            pl.BlockSpec((extra[1].shape[0], block), lambda j: (0, j)),
        ]
        operands += list(extra)
    return pl.pallas_call(
        body,
        grid=(features // block,),
        in_specs=in_specs,
        out_specs=pl.BlockSpec((tokens, block), lambda j: (0, j)),
        out_shape=jax.ShapeDtypeStruct((tokens, features), BF),
        compiler_params=params(1),
        name=name,
    )(*operands)


def shards(
    forward_rows,
    forward_ids,
    backward_rows,
    backward_ids,
    backward_grad,
    backward_stash,
    router,
    w_gate,
    w_up,
    w_down,
):
    fwd_rows, fwd_ids = forward_rows[0], forward_ids[0]
    bwd_rows, bwd_ids, bwd_grad = backward_rows[0], backward_ids[0], backward_grad[0]
    router_rows = router[0]
    gate_w, up_w, down_w = w_gate[0, 0], w_up[0, 0], w_down[0, 0]
    members = lax.axis_size("expert")
    experts, features = router_rows.shape
    hidden = down_w.shape[0]
    tokens, top = fwd_ids.shape
    slots = experts * CAP
    index = lax.axis_index("expert")
    level = index // 4
    core = jnp.reshape(index % 2, (1,))
    chip = jnp.reshape(level % 2 * 2 + index // 2 % 2, (1,))
    slot_axis = jnp.arange(slots, dtype=jnp.int32)

    joined_w = jnp.concatenate([gate_w, up_w], axis=1)

    slot_f = route_plan(fwd_ids, experts, level)
    slot_b = route_plan(bwd_ids, experts, level)
    select_f = jnp.sum(slot_axis[:, None, None] == slot_f[None], axis=2).astype(BF)
    select_b = jnp.sum(slot_axis[:, None, None] == slot_b[None], axis=2).astype(BF)
    pairs_b = (slot_axis[:, None] == slot_b.reshape(1, tokens * top)).astype(BF)
    stash = backward_stash[0].reshape(tokens * top, 2 * backward_stash.shape[-1])
    sent = pack(core, select_f, select_b, pairs_b, fwd_rows, bwd_grad, stash, hidden)
    near, far = sent

    first = hopped(far, 2)
    down_y, down_z = exchanged(down_w, 2), exchanged(down_w, 4)
    joined_y, joined_z = exchanged(joined_w, 2), exchanged(joined_w, 4)
    first, down_y, joined_z, down_z, joined_y = lax.optimization_barrier(
        (first, down_y, joined_z, down_z, joined_y)
    )

    own_1 = jnp.concatenate([near[:CAP], first[:CAP]], axis=0)
    own_2 = hopped(jnp.concatenate([near[CAP:], first[CAP:]], axis=0), 1)
    other_1 = exchanged(own_1, 1)
    down_d, joined_d = exchanged(down_y, 4), exchanged(joined_z, 2)
    own_2, other_1, down_d, joined_d = lax.optimization_barrier((own_2, other_1, down_d, joined_d))
    parts = [own_1, own_2, other_1, exchanged(own_2, 1)]
    downs = [down_w, down_y, down_z, down_d]
    joins = [joined_w, joined_y, joined_z, joined_d]

    d_joined, inner = backward_first(chip, parts, downs)
    keep, give = backward_second(d_joined, joins)
    swapped = exchanged(give, 1)
    inner = inner[:slots, 0] + exchanged(inner[slots:, 0], 1)
    inner = jnp.pad(inner.reshape(experts, 1, CAP), ((0, 0), (0, 0), (0, features - CAP))).astype(BF)
    is_inner = lax.broadcasted_iota(jnp.int32, (CAP, 1), 0) == USED
    pieces = [
        jnp.where(is_inner, inner[place], rows)
        for place, rows in zip((0, 2, 1, 3), merged(keep, swapped))
    ]
    parts, pieces = lax.optimization_barrier((parts, pieces))
    back_b = [to_source(rows, k) for k, rows in enumerate(pieces)]
    hidden_f = forward_first(parts, joins)
    keep, give = forward_second(hidden_f, downs)
    swapped = exchanged(give, 1)
    back_f = [to_source(rows, k) for k, rows in enumerate(merged(keep, swapped))]

    one_hot_b, probs_b, total_b = gate_terms(bwd_rows, bwd_ids, router_rows)
    share_b = probs_b / total_b
    scale_b = (ROUTE_SCALE * share_b).astype(BF).astype(F32)
    picks_b = [(slot_b[:, k : k + 1] == slot_axis[None, :]).astype(BF) for k in range(top)]
    inner_all = jnp.concatenate([rows[USED : USED + 1, :CAP] for rows in back_b], axis=1)
    inner_all = inner_all.astype(F32)
    inner_sum = jnp.stack(
        [jnp.sum(picks_b[k].astype(F32) * inner_all, axis=1) for k in range(top)], axis=1
    )
    d_logit = (
        ROUTE_SCALE
        / total_b
        * (inner_sum - jnp.sum(share_b * inner_sum, axis=1, keepdims=True))
        * probs_b
        * (1.0 - probs_b)
    )
    score_grad = jnp.sum(one_hot_b * d_logit[:, :, None], axis=1)
    router_total = jnp.dot(score_grad.T, bwd_rows.astype(F32), precision=lax.Precision.HIGHEST)
    router_total = router_total * (1.0 / (tokens * members))
    shares = jnp.transpose(router_total.reshape(experts, members, features // members), (1, 0, 2))
    shares = all_to_all(shares)
    shares = all_to_all(jnp.broadcast_to(jnp.sum(shares, axis=0)[None], shares.shape))
    router_total = jnp.transpose(shares, (1, 0, 2)).reshape(experts, features)
    back_f, router_total = lax.optimization_barrier((back_f, router_total))
    extra = (score_grad, router_rows)
    input_grad = combine(picks_b, scale_b, back_b, bwd_grad, extra, "combine_backward")
    backward_out_rows = shifted(input_grad, "pipe", -1)

    one_hot_f, probs_f, total_f = gate_terms(fwd_rows, fwd_ids, router_rows)
    weights_f = ROUTE_SCALE * probs_f / total_f
    picks_f = [(slot_f[:, k : k + 1] == slot_axis[None, :]).astype(BF) for k in range(top)]
    layer_out = combine(picks_f, weights_f, back_f, fwd_rows, None, "combine_forward")
    forward_out_rows = shifted(layer_out, "pipe", 1)
    return (forward_out_rows[None], backward_out_rows[None], router_total[None])


def solution(mesh):
    return jax.shard_map(
        shards,
        mesh=mesh,
        in_specs=(
            P("pipe", "expert", None),
            P("pipe", "expert", None),
            P("pipe", "expert", None),
            P("pipe", "expert", None),
            P("pipe", "expert", None),
            P("pipe", "expert", None, None, None),
            P("pipe", None, None),
            P("pipe", "expert", None, None),
            P("pipe", "expert", None, None),
            P("pipe", "expert", None, None),
        ),
        out_specs=(P("pipe", "expert", None), P("pipe", "expert", None), P("pipe", None, None)),
        check_vma=False,
    )
```

time: 509 us -> 446 us (0.88)
  waiting for transfers between devices: 337 us -> 300 us
  starting transfers between devices: 74.8 us -> 52.3 us
  local copies, waits for them, and re-layouts: 23.4 us -> 29.9 us
  other arithmetic: 21.8 us -> 15.8 us
    all_to_all x4 -> x2, waiting for transfers between devices: 90.4 us -> 43.7 us  [all_to_all(): lax.all_to_all(block, 'expert', split_axis=0, concat_axis=0, tiled=True)]
    ppermute x27 -> x11, waiting for transfers between devices: 232 us -> 195 us  [exchanged(): return lax.ppermute(block, 'expert', route)]
    ppermute x0 -> x8, waiting for transfers between devices: none -> 27.7 us  [the longest x6 27.6 us: to_source(): lax.ppermute(block, 'expert', [(b, a) for a, b in piece_route(piece)])]
    ppermute x27 -> x11, starting transfers between devices: 34.5 us -> 14.5 us  [exchanged(): return lax.ppermute(block, 'expert', route)]
    ppermute x0 -> x8, starting transfers between devices: none -> 19.2 us  [the longest x6 10.7 us: to_source(): lax.ppermute(block, 'expert', [(b, a) for a, b in piece_route(piece)])]
    ppermute x2, waiting for transfers between devices: 15.2 us -> 33.5 us  [shifted(): return lax.ppermute(block, axis, route)]
    all_to_all x4 -> x2, starting transfers between devices: 31.2 us -> 13.7 us  [all_to_all(): lax.all_to_all(block, 'expert', split_axis=0, concat_axis=0, tiled=True)]
    unnamed x60 -> x75, local copies, waits for them, and re-layouts: 14.6 us -> 17.3 us
  transfers between devices with their start and end apart: 33 -> 23, of which waited for: 21 -> 10; matrix products, arithmetic and copies ran while one was open for 6% -> 4% of each run, Pallas kernels for 8% -> 6%
where the time goes in v2:
time: 446 us; the launch traced here: 443 us
  waiting for transfers between devices  300 us (67%)
  starting transfers between devices  52.3 us (12%)
  Pallas kernels  41.5 us (9%)
  local copies, waits for them, and re-layouts  29.9 us (7%)
  other arithmetic  15.8 us (4%)
    ppermute x11, waiting for transfers between devices, exchanged(): return lax.ppermute(block, 'expert', route)  195 us
    all_to_all x2, waiting for transfers between devices, all_to_all(): lax.all_to_all(block, 'expert', split_axis=0, concat_axis=0, tiled=True)  43.7 us
    ppermute x2, waiting for transfers between devices, shifted(): return lax.ppermute(block, axis, route)  33.5 us
    ppermute x6, waiting for transfers between devices, to_source(): lax.ppermute(block, 'expert', [(b, a) for a, b in piece_route(piece)])  27.6 us
    unnamed x75, local copies, waits for them, and re-layouts  17.3 us
    ppermute x11, starting transfers between devices, exchanged(): return lax.ppermute(block, 'expert', route)  14.5 us
    all_to_all x2, starting transfers between devices, all_to_all(): lax.all_to_all(block, 'expert', split_axis=0, concat_axis=0, tiled=True)  13.7 us
    ppermute x6, starting transfers between devices, to_source(): lax.ppermute(block, 'expert', [(b, a) for a, b in piece_route(piece)])  10.7 us
  transfers between devices with their start and end apart: 23, of which 10 were waited for; matrix products, arithmetic and copies ran while one was open for 4% of the time, Pallas kernels for 6%

profile of v2, /device:TPU:1, one launch (start us, length us, event | category | flops | bytes accessed | tf_op | source)
XLA Modules:
  0.0 443.4 jit_solution(15200107588436708506)
XLA Ops:
  0.7 4.4 pad_maximum_fusion.refs_0_.refs_4_
  5.1 2.5 collective-permute-start.2
  7.6 1.3 collective-permute-start.4
  11.4 1.2 copy.146
  12.6 1.2 copy-done.6
  13.7 1.2 copy-done.8
  14.9 3.3 pack.1
  18.2 5.4 %collective-permute-start = (bf16[80,16384]{1,0:T(8,128)(2,1)}, bf16[80,16384]{1,0:T(8,128)(2,1)S(1)}, u32[]{:S(2)}, u32[]{:S(2)}) collective-permute-start(bf16[80,16384]{1,0:T(8,128)(2,1)} %get-tuple-element.34), channel_id=1, source_target_pairs={{0,28},{1,29},{2,30},{3,31},{4,8},{5,9},{6,10},{7,11},{8,4},{9,5},... | collective-permute-start | bytes 7864328 | tf_op jit(solution)/shard_map/ppermute | solution.py:44
  23.8 103.3 %collective-permute-done.1.refs_9_.refs_1_ = bf16[128,7168]{1,0:T(8,128)(2,1)} collective-permute-done((bf16[128,7168]{1,0:T(8,128)(2,1)S(1)}, bf16[128,7168]{1,0:T(8,128)(2,1)}, u32[]{:S(2)}, u32[]{:S(2)}) %collective-permute-start.1) | collective-permute-done | bytes 1835040 | tf_op jit(solution)/shard_map/ppermute | solution.py:30
  127.5 3.1 collective-permute-start.5
  130.6 1.3 collective-permute-start.8
  132.0 2.5 collective-permute-start.6
  134.6 2.9 collective-permute-start.7
  137.4 90.3 %collective-permute-done.7.refs_11_.refs_3_ = bf16[128,7168]{1,0:T(8,128)(2,1)S(1)} collective-permute-done((bf16[128,7168]{1,0:T(8,128)(2,1)}, bf16[128,7168]{1,0:T(8,128)(2,1)S(1)}, u32[]{:S(2)}, u32[]{:S(2)}) %collective-permute-start.7) | collective-permute-done | bytes 1835040 | tf_op jit(solution)/shard_map/ppermute | solution.py:30
  227.8 1.5 copy-done.23
  229.8 1.9 copy-done.24
  231.7 2.8 collective-permute-start.9
  237.6 1.5 fusion.36
  239.3 1.5 copy-done.4
  240.8 6.9 %backward_first.1 = (bf16[320,1024]{1,0:T(8,128)(2,1)S(1)}, f32[320,128]{1,0:T(8,128)S(1)}) custom-call(s32[1]{0:T(128)} %bitcast.12.chip_ref, bf16[80,16384]{1,0:T(8,128)(2,1)} %copy-done.1, bf16[80,16384]{1,0:T(8,128)(2,1)} %collective-permute-done.5.refs_1_.refs_5_, bf16[80,16384]{1,0:T(8,128)(2,1)} %copy-done.23, ...), custom_call_target="tpu_custom_call" | custom-call | tf_op jit(solution)/shard_map/backward_first/pallas_call | solution.py:179
  248.4 9.6 %backward_second.1 = (bf16[160,7168]{1,0:T(8,128)(2,1)S(1)}, bf16[160,7168]{1,0:T(8,128)(2,1)}) custom-call(bf16[320,1024]{1,0:T(8,128)(2,1)S(1)} %get-tuple-element.43.d_ref, bf16[7168,256]{1,0:T(8,128)(2,1)} %pad_maximum_fusion.refs_0_.refs_4_, bf16[7168,256]{1,0:T(8,128)(2,1)} %collective-permute-done.4.refs_1_.refs_5_, ...), custom_call_target="tpu_custom_call" | custom-call | tf_op jit(solution)/shard_map/backward_second/pallas_call | solution.py:214
  261.3 0.9 fusion.1
  262.6 1.0 collective-permute-done.10
  263.8 2.3 add_convert_fusion.1
  266.2 1.5 slice_select_fusion
  267.7 1.6 collective-permute-start.18
  270.0 9.6 %forward_first.1.hidden_ref = bf16[320,512]{1,0:T(8,128)(2,1)S(1)} custom-call(bf16[80,16384]{1,0:T(8,128)(2,1)S(1)} %copy-done.2, bf16[80,16384]{1,0:T(8,128)(2,1)} %collective-permute-done.5.refs_1_.refs_5_, bf16[80,16384]{1,0:T(8,128)(2,1)} %copy-done.23, bf16[80,16384]{1,0:T(8,128)(2,1)} %collective-permute-done.9.refs_3_.refs_7_, ...), custom_call_target="tpu_custom_call" | custom-call | tf_op jit(solution)/shard_map/forward_first/pallas_call | solution.py:258
  279.7 6.6 %forward_second.1 = (bf16[160,7168]{1,0:T(8,128)(2,1)}, bf16[160,7168]{1,0:T(8,128)(2,1)}) custom-call(bf16[320,512]{1,0:T(8,128)(2,1)S(1)} %forward_first.1.hidden_ref, bf16[128,7168]{1,0:T(8,128)(2,1)S(1)} %bitcast.59, bf16[128,7168]{1,0:T(8,128)(2,1)} %collective-permute-done.1.refs_9_.refs_1_, bf16[128,7168]{1,0:T(8,128)(2,1)} %collective-permute-done.3.refs_10_.refs_2_, ...), custom_call_target="tpu_custom_call" | custom-call | tf_op jit(solution)/shard_map/forward_second/pallas_call | solution.py:284
  287.6 2.6 collective-permute-start.16
  290.2 4.9 %collective-permute-done.18.refs_6_ = bf16[40,7168]{1,0:T(8,128)(2,1)} collective-permute-done((bf16[40,7168]{1,0:T(8,128)(2,1)}, bf16[40,7168]{1,0:T(8,128)(2,1)}, u32[]{:S(2)}, u32[]{:S(2)}) %collective-permute-start.18) | collective-permute-done | bytes 573472 | tf_op jit(solution)/shard_map/ppermute | solution.py:50
  295.7 11.9 %collective-permute-done.17.refs_5_ = bf16[40,7168]{1,0:T(8,128)(2,1)S(1)} collective-permute-done((bf16[40,7168]{1,0:T(8,128)(2,1)S(1)}, bf16[40,7168]{1,0:T(8,128)(2,1)S(1)}, u32[]{:S(2)}, u32[]{:S(2)}) %collective-permute-start.17) | collective-permute-done | bytes 573472 | tf_op jit(solution)/shard_map/ppermute | solution.py:50
  308.4 10.9 %collective-permute-done.16.refs_4_ = bf16[40,7168]{1,0:T(8,128)(2,1)S(1)} collective-permute-done((bf16[40,7168]{1,0:T(8,128)(2,1)S(1)}, bf16[40,7168]{1,0:T(8,128)(2,1)S(1)}, u32[]{:S(2)}, u32[]{:S(2)}) %collective-permute-start.16) | collective-permute-done | bytes 573472 | tf_op jit(solution)/shard_map/ppermute | solution.py:50
  321.0 3.0 add_convert_fusion
  324.1 1.4 fusion.41
  325.5 3.8 collective-permute-start.13
  329.6 1.8 collective-permute-start.15
  332.7 7.3 %all-to-all-start = ((f32[32,4,224]{2,1,0:T(4,128)}), f32[32,4,224]{2,1,0:T(4,128)S(1)}, u32[]{:S(2)}, u32[]{:S(2)}) async-start(f32[32,4,224]{2,1,0:T(4,128)} %bitcast.55), calls=%async_computation | async-start | bytes 262144 | tf_op jit(solution)/shard_map/all_to_all | solution.py:34
  340.1 43.7 %all-to-all-done = f32[32,4,224]{2,1,0:T(4,128)S(1)} async-done(((f32[32,4,224]{2,1,0:T(4,128)}), f32[32,4,224]{2,1,0:T(4,128)S(1)}, u32[]{:S(2)}, u32[]{:S(2)}) %all-to-all-start) | async-done | bytes 114720 | tf_op jit(solution)/shard_map/all_to_all | solution.py:34
  384.5 6.5 %all-to-all-start.1 = ((f32[32,4,224]{2,1,0:T(4,128)}), f32[32,4,224]{2,1,0:T(4,128)}, u32[]{:S(2)}, u32[]{:S(2)}) async-start(f32[32,4,224]{2,1,0:T(4,128)} %broadcast_in_dim.100), calls=%async_computation.1 | async-start | bytes 262144 | tf_op jit(solution)/shard_map/all_to_all | solution.py:34
  391.9 1.1 copy-done.13
  392.9 1.1 copy-done.15
  394.8 3.3 combine_backward.1
  398.1 4.8 %collective-permute-start.20 = (bf16[64,7168]{1,0:T(8,128)(2,1)}, bf16[64,7168]{1,0:T(8,128)(2,1)S(1)}, u32[]{:S(2)}, u32[]{:S(2)}) collective-permute-start(bf16[64,7168]{1,0:T(8,128)(2,1)} %combine_backward.1), channel_id=1, source_target_pairs={{32,0},{64,32},{96,64},{128,96},{160,128},{192,160},{224,192},{0,2... | collective-permute-start | bytes 2752520 | tf_op jit(solution)/shard_map/ppermute | solution.py:25
  402.9 0.9 copy.144
  404.7 1.1 copy-done.11
  405.8 2.2 combine_forward.1
  408.1 33.0 %collective-permute-done.20 = bf16[64,7168]{1,0:T(8,128)(2,1)S(1)} collective-permute-done((bf16[64,7168]{1,0:T(8,128)(2,1)}, bf16[64,7168]{1,0:T(8,128)(2,1)S(1)}, u32[]{:S(2)}, u32[]{:S(2)}) %collective-permute-start.20) | collective-permute-done | bytes 917536 | tf_op jit(solution)/shard_map/ppermute | solution.py:25
  441.6 0.9 copy.151
  (158 shorter events, 23.0 us)
Async XLA Ops:
  0.6 260.6 %copy-start = (bf16[1,64,7168]{2,1,0:T(8,128)(2,1)S(1)}, bf16[1,64,7168]{2,1,0:T(8,128)(2,1)}, u32[]{:S(2)}) copy-start(bf16[1,64,7168]{2,1,0:T(8,128)(2,1)} %param.12) | copy-start | bytes 2752516
  0.6 8.2 %copy-start.3 = (bf16[1,1,128,7168]{3,2,1,0:T(8,128)(2,1)S(1)}, bf16[1,1,128,7168]{3,2,1,0:T(8,128)(2,1)}, u32[]{:S(2)}) copy-start(bf16[1,1,128,7168]{3,2,1,0:T(8,128)(2,1)} %param.19) | copy-start | bytes 5505028
  0.7 8.4 %copy-start.29 = (s32[1,64,2]{1,2,0:T(2,128)S(1)}, s32[1,64,2]{1,2,0:T(2,128)}, u32[]{:S(2)}) copy-start(s32[1,64,2]{1,2,0:T(2,128)} %param.13) | copy-start | bytes 1540
  0.7 9.3 %copy-start.31 = (s32[1,64,2]{1,2,0:T(2,128)S(1)}, s32[1,64,2]{1,2,0:T(2,128)}, u32[]{:S(2)}) copy-start(s32[1,64,2]{1,2,0:T(2,128)} %param.11) | copy-start | bytes 1540
  5.1 122.0 %collective-permute-start.2 = (bf16[7168,256]{1,0:T(8,128)(2,1)}, bf16[7168,256]{1,0:T(8,128)(2,1)}, u32[]{:S(2)}, u32[]{:S(2)}) collective-permute-start(bf16[7168,256]{1,0:T(8,128)(2,1)} %pad_maximum_fusion.refs_0_.refs_4_), channel_id=1, source_target_pairs={{0,4},{1,5},{2,6},{3,7},{4,0},{5,1},{6,2},{7,3},{8,12},{9,13},{10,... | collective-permute-start | bytes 11010056 | tf_op jit(solution)/shard_map/ppermute | solution.py:30
  7.6 119.5 %collective-permute-start.4 = (bf16[7168,256]{1,0:T(8,128)(2,1)}, bf16[7168,256]{1,0:T(8,128)(2,1)}, u32[]{:S(2)}, u32[]{:S(2)}) collective-permute-start(bf16[7168,256]{1,0:T(8,128)(2,1)} %pad_maximum_fusion.refs_0_.refs_4_), channel_id=1, source_target_pairs={{0,2},{1,3},{2,0},{3,1},{4,6},{5,7},{6,4},{7,5},{8,10},{9,11},{10,... | collective-permute-start | bytes 11010056 | tf_op jit(solution)/shard_map/ppermute | solution.py:30
  8.9 118.2 %collective-permute-start.1 = (bf16[128,7168]{1,0:T(8,128)(2,1)S(1)}, bf16[128,7168]{1,0:T(8,128)(2,1)}, u32[]{:S(2)}, u32[]{:S(2)}) collective-permute-start(bf16[128,7168]{1,0:T(8,128)(2,1)S(1)} %bitcast.56), channel_id=1, source_target_pairs={{0,2},{1,3},{2,0},{3,1},{4,6},{5,7},{6,4},{7,5},{8,10},{9,11},{10,... | collective-permute-start | bytes 5505032 | tf_op jit(solution)/shard_map/ppermute | solution.py:30
  9.0 118.1 %collective-permute-start.3 = (bf16[128,7168]{1,0:T(8,128)(2,1)S(1)}, bf16[128,7168]{1,0:T(8,128)(2,1)}, u32[]{:S(2)}, u32[]{:S(2)}) collective-permute-start(bf16[128,7168]{1,0:T(8,128)(2,1)S(1)} %bitcast.57), channel_id=1, source_target_pairs={{0,4},{1,5},{2,6},{3,7},{4,0},{5,1},{6,2},{7,3},{8,12},{9,13},{10,... | collective-permute-start | bytes 5505032 | tf_op jit(solution)/shard_map/ppermute | solution.py:30
  18.2 108.9 %collective-permute-start = (bf16[80,16384]{1,0:T(8,128)(2,1)}, bf16[80,16384]{1,0:T(8,128)(2,1)S(1)}, u32[]{:S(2)}, u32[]{:S(2)}) collective-permute-start(bf16[80,16384]{1,0:T(8,128)(2,1)} %get-tuple-element.34), channel_id=1, source_target_pairs={{0,28},{1,29},{2,30},{3,31},{4,8},{5,9},{6,10},{7,11},{8,4},{9,5},... | collective-permute-start | bytes 7864328 | tf_op jit(solution)/shard_map/ppermute | solution.py:44
  127.5 100.3 %collective-permute-start.5 = (bf16[80,16384]{1,0:T(8,128)(2,1)S(1)}, bf16[80,16384]{1,0:T(8,128)(2,1)}, u32[]{:S(2)}, u32[]{:S(2)}) collective-permute-start(bf16[80,16384]{1,0:T(8,128)(2,1)S(1)} %pad_maximum_fusion.2), channel_id=1, source_target_pairs={{0,8},{1,9},{2,10},{3,11},{4,28},{5,29},{6,30},{7,31},{8,16},{9,17... | collective-permute-start | bytes 7864328 | tf_op jit(solution)/shard_map/ppermute | solution.py:44
  130.6 98.7 %collective-permute-start.8 = (bf16[7168,256]{1,0:T(8,128)(2,1)}, bf16[7168,256]{1,0:T(8,128)(2,1)S(1)}, u32[]{:S(2)}, u32[]{:S(2)}) collective-permute-start(bf16[7168,256]{1,0:T(8,128)(2,1)} %collective-permute-done.2.refs_2_.refs_6_), channel_id=1, source_target_pairs={{0,2},{1,3},{2,0},{3,1},{4,6},{5,7},{6,4},{7,5},{8,10},{9,11},{10,... | collective-permute-start | bytes 11010056 | tf_op jit(solution)/shard_map/ppermute | solution.py:30
  132.0 107.3 %copy-start.1 = (bf16[80,16384]{1,0:T(8,128)(2,1)}, bf16[80,16384]{1,0:T(8,128)(2,1)S(1)}, u32[]{:S(2)}) copy-start(bf16[80,16384]{1,0:T(8,128)(2,1)S(1)} %pad_maximum_fusion.1.refs_0_.refs_4_) | copy-start | bytes 7864324
  132.0 95.7 %collective-permute-start.6 = (bf16[80,16384]{1,0:T(8,128)(2,1)S(1)}, bf16[80,16384]{1,0:T(8,128)(2,1)S(1)}, u32[]{:S(2)}, u32[]{:S(2)}) collective-permute-start(bf16[80,16384]{1,0:T(8,128)(2,1)S(1)} %pad_maximum_fusion.1.refs_0_.refs_4_), channel_id=1, source_target_pairs={{0,1},{1,0},{2,3},{3,2},{4,5},{5,4},{6,7},{7,6},{8,9},{9,8},{10,11... | collective-permute-start | bytes 7864328 | tf_op jit(solution)/shard_map/ppermute | solution.py:30
  134.6 93.2 %collective-permute-start.7 = (bf16[128,7168]{1,0:T(8,128)(2,1)}, bf16[128,7168]{1,0:T(8,128)(2,1)S(1)}, u32[]{:S(2)}, u32[]{:S(2)}) collective-permute-start(bf16[128,7168]{1,0:T(8,128)(2,1)} %collective-permute-done.1.refs_9_.refs_1_), channel_id=1, source_target_pairs={{0,4},{1,5},{2,6},{3,7},{4,0},{5,1},{6,2},{7,3},{8,12},{9,13},{10,... | collective-permute-start | bytes 5505032 | tf_op jit(solution)/shard_map/ppermute | solution.py:30
  227.8 2.0 copy-start.25
  227.8 1.5 copy-start.23
  229.8 1.9 copy-start.24
  231.7 7.7 %collective-permute-start.9 = (bf16[80,16384]{1,0:T(8,128)(2,1)}, bf16[80,16384]{1,0:T(8,128)(2,1)}, u32[]{:S(2)}, u32[]{:S(2)}) collective-permute-start(bf16[80,16384]{1,0:T(8,128)(2,1)} %collective-permute-done.5.refs_1_.refs_5_), channel_id=1, source_target_pairs={{0,1},{1,0},{2,3},{3,2},{4,5},{5,4},{6,7},{7,6},{8,9},{9,8},{10,11... | collective-permute-start | bytes 7864328 | tf_op jit(solution)/shard_map/ppermute | solution.py:30
  248.4 12.9 %copy-start.21 = (bf16[1,4,7168]{2,1,0:T(4,128)(2,1)S(1)}, bf16[1,4,7168]{2,1,0:T(4,128)(2,1)}, u32[]{:S(2)}) copy-start(bf16[1,4,7168]{2,1,0:T(4,128)(2,1)} %param.16) | copy-start | bytes 172036
  248.4 13.9 %copy-start.17 = (f32[320,128]{1,0:T(8,128)S(1)}, f32[320,128]{1,0:T(8,128)}, u32[]{:S(2)}) copy-start(f32[320,128]{1,0:T(8,128)} %copy-done.16) | copy-start | bytes 491524
  258.0 5.8 %collective-permute-start.11 = (bf16[160,7168]{1,0:T(8,128)(2,1)}, bf16[160,7168]{1,0:T(8,128)(2,1)}, u32[]{:S(2)}, u32[]{:S(2)}) collective-permute-start(bf16[160,7168]{1,0:T(8,128)(2,1)} %get-tuple-element.47), channel_id=1, source_target_pairs={{0,1},{1,0},{2,3},{3,2},{4,5},{5,4},{6,7},{7,6},{8,9},{9,8},{10,11... | collective-permute-start | bytes 6881288 | tf_op jit(solution)/shard_map/ppermute | solution.py:30
  262.4 1.2 collective-permute-start.10
  266.2 3.1 copy-start.34
  266.2 3.9 copy-start.2
  267.7 27.4 %collective-permute-start.18 = (bf16[40,7168]{1,0:T(8,128)(2,1)}, bf16[40,7168]{1,0:T(8,128)(2,1)}, u32[]{:S(2)}, u32[]{:S(2)}) collective-permute-start(bf16[40,7168]{1,0:T(8,128)(2,1)} %get-tuple-element.57), channel_id=1, source_target_pairs={{20,0},{21,1},{22,2},{23,3},{16,4},{17,5},{18,6},{19,7},{28,8},{29... | collective-permute-start | bytes 1720328 | tf_op jit(solution)/shard_map/ppermute | solution.py:50
  270.0 9.6 %copy-start.5 = (bf16[1,1,128,7168]{3,2,1,0:T(8,128)(2,1)S(1)}, bf16[1,1,128,7168]{3,2,1,0:T(8,128)(2,1)}, u32[]{:S(2)}) copy-start(bf16[1,1,128,7168]{3,2,1,0:T(8,128)(2,1)} %param.19) | copy-start | bytes 5505028
  279.7 7.1 %copy-start.28 = (f32[64,2]{1,0:T(8,128)S(1)}, f32[64,2]{1,0:T(8,128)}, u32[]{:S(2)}) copy-start(f32[64,2]{1,0:T(8,128)} %copy.134) | copy-start | bytes 1540
  279.7 7.2 %copy-start.27 = (bf16[40,7168]{1,0:T(8,128)(2,1)S(1)}, bf16[40,7168]{1,0:T(8,128)(2,1)}, u32[]{:S(2)}) copy-start(bf16[40,7168]{1,0:T(8,128)(2,1)} %get-tuple-element.56) | copy-start | bytes 1720324
  279.7 7.9 %copy-start.26 = (bf16[40,7168]{1,0:T(8,128)(2,1)S(1)}, bf16[40,7168]{1,0:T(8,128)(2,1)}, u32[]{:S(2)}) copy-start(bf16[40,7168]{1,0:T(8,128)(2,1)} %get-tuple-element.55) | copy-start | bytes 1720324
  279.7 10.5 %copy-start.10 = (bf16[40,7168]{1,0:T(8,128)(2,1)S(1)}, bf16[40,7168]{1,0:T(8,128)(2,1)}, u32[]{:S(2)}) copy-start(bf16[40,7168]{1,0:T(8,128)(2,1)} %get-tuple-element.54.refs_3_) | copy-start | bytes 1720324
  286.3 34.6 %collective-permute-start.12 = (bf16[160,7168]{1,0:T(8,128)(2,1)}, bf16[160,7168]{1,0:T(8,128)(2,1)}, u32[]{:S(2)}, u32[]{:S(2)}) collective-permute-start(bf16[160,7168]{1,0:T(8,128)(2,1)} %get-tuple-element.53), channel_id=1, source_target_pairs={{0,1},{1,0},{2,3},{3,2},{4,5},{5,4},{6,7},{7,6},{8,9},{9,8},{10,11... | collective-permute-start | bytes 6881288 | tf_op jit(solution)/shard_map/ppermute | solution.py:30
  287.0 20.6 %collective-permute-start.17 = (bf16[40,7168]{1,0:T(8,128)(2,1)S(1)}, bf16[40,7168]{1,0:T(8,128)(2,1)S(1)}, u32[]{:S(2)}, u32[]{:S(2)}) collective-permute-start(bf16[40,7168]{1,0:T(8,128)(2,1)S(1)} %copy-done.27), channel_id=1, source_target_pairs={{28,0},{29,1},{30,2},{31,3},{8,4},{9,5},{10,6},{11,7},{4,8},{5,9},... | collective-permute-start | bytes 1720328 | tf_op jit(solution)/shard_map/ppermute | solution.py:50
  287.6 31.7 %collective-permute-start.16 = (bf16[40,7168]{1,0:T(8,128)(2,1)S(1)}, bf16[40,7168]{1,0:T(8,128)(2,1)S(1)}, u32[]{:S(2)}, u32[]{:S(2)}) collective-permute-start(bf16[40,7168]{1,0:T(8,128)(2,1)S(1)} %copy-done.26), channel_id=1, source_target_pairs={{8,0},{9,1},{10,2},{11,3},{28,4},{29,5},{30,6},{31,7},{16,8},{17,9... | collective-permute-start | bytes 1720328 | tf_op jit(solution)/shard_map/ppermute | solution.py:50
  320.9 10.4 %copy-start.30 = (f32[64,4]{0,1:T(4,128)}, f32[64,4]{0,1:T(4,128)S(1)}, u32[]{:S(2)}) copy-start(f32[64,4]{0,1:T(4,128)S(1)} %select_reduce_fusion.2) | copy-start | bytes 3076
  324.0 16.0 %copy-start.33 = (s32[64]{0:T(128)S(1)}, s32[64]{0:T(128)}, u32[]{:S(2)}) copy-start(s32[64]{0:T(128)} %get-tuple-element.88) | copy-start | bytes 772
  324.0 67.0 %copy-start.32 = (s32[64]{0:T(128)S(1)}, s32[64]{0:T(128)}, u32[]{:S(2)}) copy-start(s32[64]{0:T(128)} %get-tuple-element.87) | copy-start | bytes 772
  324.0 67.8 %copy-start.7 = (bf16[1,64,7168]{2,1,0:T(8,128)(2,1)S(1)}, bf16[1,64,7168]{2,1,0:T(8,128)(2,1)}, u32[]{:S(2)}) copy-start(bf16[1,64,7168]{2,1,0:T(8,128)(2,1)} %param.14) | copy-start | bytes 2752516
  324.0 67.8 %copy-start.19 = (bf16[64,160]{1,0:T(8,128)(2,1)S(1)}, bf16[64,160]{1,0:T(8,128)(2,1)}, u32[]{:S(2)}) copy-start(bf16[64,160]{1,0:T(8,128)(2,1)} %fusion.8.refs_0_) | copy-start | bytes 61444
  324.1 67.8 %copy-start.20 = (bf16[64,160]{1,0:T(8,128)(2,1)S(1)}, bf16[64,160]{1,0:T(8,128)(2,1)}, u32[]{:S(2)}) copy-start(bf16[64,160]{1,0:T(8,128)(2,1)} %fusion.9.refs_1_) | copy-start | bytes 61444
  325.5 79.2 %collective-permute-start.13 = (bf16[40,7168]{1,0:T(8,128)(2,1)}, bf16[40,7168]{1,0:T(8,128)(2,1)}, u32[]{:S(2)}, u32[]{:S(2)}) collective-permute-start(bf16[40,7168]{1,0:T(8,128)(2,1)} %get-tuple-element.81), channel_id=1, source_target_pairs={{8,0},{9,1},{10,2},{11,3},{28,4},{29,5},{30,6},{31,7},{16,8},{17,9... | collective-permute-start | bytes 1720328 | tf_op jit(solution)/shard_map/ppermute | solution.py:50
  329.3 75.4 %collective-permute-start.14 = (bf16[40,7168]{1,0:T(8,128)(2,1)}, bf16[40,7168]{1,0:T(8,128)(2,1)}, u32[]{:S(2)}, u32[]{:S(2)}) collective-permute-start(bf16[40,7168]{1,0:T(8,128)(2,1)} %get-tuple-element.80), channel_id=1, source_target_pairs={{28,0},{29,1},{30,2},{31,3},{8,4},{9,5},{10,6},{11,7},{4,8},{5,9},... | collective-permute-start | bytes 1720328 | tf_op jit(solution)/shard_map/ppermute | solution.py:50
  329.6 75.1 %collective-permute-start.15 = (bf16[40,7168]{1,0:T(8,128)(2,1)}, bf16[40,7168]{1,0:T(8,128)(2,1)}, u32[]{:S(2)}, u32[]{:S(2)}) collective-permute-start(bf16[40,7168]{1,0:T(8,128)(2,1)} %get-tuple-element.79), channel_id=1, source_target_pairs={{20,0},{21,1},{22,2},{23,3},{16,4},{17,5},{18,6},{19,7},{28,8},{29... | collective-permute-start | bytes 1720328 | tf_op jit(solution)/shard_map/ppermute | solution.py:50
  332.7 51.1 %all-to-all-start = ((f32[32,4,224]{2,1,0:T(4,128)}), f32[32,4,224]{2,1,0:T(4,128)S(1)}, u32[]{:S(2)}, u32[]{:S(2)}) async-start(f32[32,4,224]{2,1,0:T(4,128)} %bitcast.55), calls=%async_computation | async-start | bytes 262144 | tf_op jit(solution)/shard_map/all_to_all | solution.py:34
  383.8 20.9 %copy-start.18 = (f32[64,2]{1,0:T(8,128)S(1)}, f32[64,2]{1,0:T(8,128)}, u32[]{:S(2)}) copy-start(f32[64,2]{1,0:T(8,128)} %multiply_divide_fusion.1.refs_2_) | copy-start | bytes 1540
  383.9 20.8 %copy-start.9 = (bf16[1,64,7168]{2,1,0:T(8,128)(2,1)S(1)}, bf16[1,64,7168]{2,1,0:T(8,128)(2,1)}, u32[]{:S(2)}) copy-start(bf16[1,64,7168]{2,1,0:T(8,128)(2,1)} %param.10) | copy-start | bytes 2752516
  384.5 18.4 %all-to-all-start.1 = ((f32[32,4,224]{2,1,0:T(4,128)}), f32[32,4,224]{2,1,0:T(4,128)}, u32[]{:S(2)}, u32[]{:S(2)}) async-start(f32[32,4,224]{2,1,0:T(4,128)} %broadcast_in_dim.100), calls=%async_computation.1 | async-start | bytes 262144 | tf_op jit(solution)/shard_map/all_to_all | solution.py:34
  398.1 43.0 %collective-permute-start.20 = (bf16[64,7168]{1,0:T(8,128)(2,1)}, bf16[64,7168]{1,0:T(8,128)(2,1)S(1)}, u32[]{:S(2)}, u32[]{:S(2)}) collective-permute-start(bf16[64,7168]{1,0:T(8,128)(2,1)} %combine_backward.1), channel_id=1, source_target_pairs={{32,0},{64,32},{96,64},{128,96},{160,128},{192,160},{224,192},{0,2... | collective-permute-start | bytes 2752520 | tf_op jit(solution)/shard_map/ppermute | solution.py:25
  408.0 33.6 %collective-permute-start.19 = (bf16[64,7168]{1,0:T(8,128)(2,1)S(1)}, bf16[64,7168]{1,0:T(8,128)(2,1)S(1)}, u32[]{:S(2)}, u32[]{:S(2)}) collective-permute-start(bf16[64,7168]{1,0:T(8,128)(2,1)S(1)} %combine_forward.1), channel_id=1, source_target_pairs={{224,0},{0,32},{32,64},{64,96},{96,128},{128,160},{160,192},{192,2... | collective-permute-start | bytes 2752520 | tf_op jit(solution)/shard_map/ppermute | solution.py:25
  (10 other events, 10.2 us)

commit v3 on v2

--- a/solution.py
+++ b/solution.py
@@ -159,7 +159,7 @@
         def _():
             for part, stash_ref in enumerate(stash_refs):
                 place = slice(part * rows, (part + 1) * rows)
-                inner = jnp.zeros((rows, 1), F32)
+                products = jnp.zeros((rows, hidden), F32)
                 for s in range(chips):
                     start = (chip_ref[0] ^ s) * hidden
                     pre_gate = stash_ref[:, pl.ds(pl.multiple_of(start, hidden), hidden)].astype(F32)
@@ -170,11 +170,19 @@
                     activated = pre_gate * sigmoid_v
                     slope = sigmoid_v * (1.0 + pre_gate * (1.0 - sigmoid_v))
                     hidden_b = (activated * pre_up).astype(BF).astype(F32)
-                    inner += jnp.sum(hidden_b * raw, axis=1, keepdims=True)
+                    products += hidden_b * raw
                     at = 2 * s * hidden
                     d_ref[place, at : at + hidden] = (raw * pre_up * slope).astype(BF)
                     d_ref[place, at + hidden : at + 2 * hidden] = (raw * activated).astype(BF)
-                inner_ref[place, :] = jnp.broadcast_to(inner, (rows, 128))
+                high = products.astype(BF)
+                low = (products - high.astype(F32)).astype(BF)
+                ones = jnp.ones((8, hidden), BF)
+                for k in range(rows // CAP):
+                    piece = slice(k * CAP, (k + 1) * CAP)
+                    inner = contract(ones, high[piece], 1) + contract(ones, low[piece], 1)
+                    inner = jnp.pad(inner, ((0, 0), (0, hidden - CAP)))
+                    at = 8 * (part * rows // CAP + k)
+                    inner_ref[at : at + 8, :] = inner
 
     return pl.pallas_call(
         body,
@@ -186,11 +194,11 @@
         + [pl.BlockSpec((hidden, block), lambda j: (0, j))] * chips,
         out_specs=[
             pl.BlockSpec((count * rows, 2 * chips * hidden), lambda j: (0, 0)),
-            pl.BlockSpec((count * rows, 128), lambda j: (0, 0)),
+            pl.BlockSpec((count * rows // CAP * 8, hidden), lambda j: (0, 0)),
         ],
         out_shape=[
             jax.ShapeDtypeStruct((count * rows, 2 * chips * hidden), BF),
-            jax.ShapeDtypeStruct((count * rows, 128), F32),
+            jax.ShapeDtypeStruct((count * rows // CAP * 8, hidden), F32),
         ],
         scratch_shapes=[pltpu.VMEM((count * rows, chips * hidden), F32)],
         compiler_params=params(1),
@@ -198,29 +206,40 @@
     )(chip, *parts, *parts, *downs)
 
 
-def backward_second(d_joined, weights):
+def backward_second(d_joined, inner, weights):
     rows = d_joined.shape[0] // 2
     features, joined = weights[0].shape
     chips = len(weights)
     block = 1792
-
-    def body(d_ref, *refs):
-        keep_ref, give_ref = refs[chips:]
+    lanes = inner.shape[1]
+
+    def body(d_ref, inner_ref, *refs):
+        out_refs = refs[chips:]
         right = jnp.concatenate([ref[...] for ref in refs[:chips]], axis=1)
         got = contract(d_ref[...], right, 1)
-        keep_ref[...] = got[:rows].astype(BF)
-        give_ref[...] = got[rows:].astype(BF)
+        for half, out_ref in enumerate(out_refs):
+            out_ref[...] = got[half * rows : (half + 1) * rows].astype(BF)
+
+        @pl.when(pl.program_id(0) == 0)
+        def _():
+            used = lax.broadcasted_iota(jnp.int32, (CAP, lanes), 0) == USED
+            for half, out_ref in enumerate(out_refs):
+                pieces = []
+                for k in range(half * rows // CAP, (half + 1) * rows // CAP):
+                    piece = got[k * CAP : (k + 1) * CAP, :lanes]
+                    pieces.append(jnp.where(used, inner_ref[8 * k : 8 * k + 1, :], piece))
+                out_ref[:, :lanes] = jnp.concatenate(pieces, axis=0).astype(BF)
 
     return pl.pallas_call(
         body,
         grid=(features // block,),
-        in_specs=[pl.BlockSpec(d_joined.shape, lambda j: (0, 0))]
+        in_specs=[pl.BlockSpec(a.shape, lambda j: (0, 0)) for a in (d_joined, inner)]
         + [pl.BlockSpec((block, joined), lambda j: (j, 0))] * chips,
         out_specs=[pl.BlockSpec((rows, block), lambda j: (0, j))] * 2,
         out_shape=[jax.ShapeDtypeStruct((rows, features), BF)] * 2,
         compiler_params=params(1),
         name="backward_second",
-    )(d_joined, *weights)
+    )(d_joined, inner, *weights)
 
 
 def forward_first(parts, weights):
@@ -392,22 +411,17 @@
     own_1 = jnp.concatenate([near[:CAP], first[:CAP]], axis=0)
     own_2 = hopped(jnp.concatenate([near[CAP:], first[CAP:]], axis=0), 1)
     other_1 = exchanged(own_1, 1)
-    down_d, joined_d = exchanged(down_y, 4), exchanged(joined_z, 2)
+    cut = hidden // 3 // 16 * 16
+    down_d = [exchanged(down_z[:cut], 2), exchanged(down_y[cut:], 4)]
+    joined_d = exchanged(joined_z, 2)
     own_2, other_1, down_d, joined_d = lax.optimization_barrier((own_2, other_1, down_d, joined_d))
     parts = [own_1, own_2, other_1, exchanged(own_2, 1)]
-    downs = [down_w, down_y, down_z, down_d]
+    downs = [down_w, down_y, down_z, jnp.concatenate(down_d, axis=0)]
     joins = [joined_w, joined_y, joined_z, joined_d]
 
     d_joined, inner = backward_first(chip, parts, downs)
-    keep, give = backward_second(d_joined, joins)
-    swapped = exchanged(give, 1)
-    inner = inner[:slots, 0] + exchanged(inner[slots:, 0], 1)
-    inner = jnp.pad(inner.reshape(experts, 1, CAP), ((0, 0), (0, 0), (0, features - CAP))).astype(BF)
-    is_inner = lax.broadcasted_iota(jnp.int32, (CAP, 1), 0) == USED
-    pieces = [
-        jnp.where(is_inner, inner[place], rows)
-        for place, rows in zip((0, 2, 1, 3), merged(keep, swapped))
-    ]
+    keep, give = backward_second(d_joined, inner, joins)
+    pieces = merged(keep, exchanged(give, 1))
     parts, pieces = lax.optimization_barrier((parts, pieces))
     back_b = [to_source(rows, k) for k, rows in enumerate(pieces)]
     hidden_f = forward_first(parts, joins)
@@ -415,6 +429,7 @@
     swapped = exchanged(give, 1)
     back_f = [to_source(rows, k) for k, rows in enumerate(merged(keep, swapped))]
 
+    back_b = lax.optimization_barrier(back_b)
     one_hot_b, probs_b, total_b = gate_terms(bwd_rows, bwd_ids, router_rows)
     share_b = probs_b / total_b
     scale_b = (ROUTE_SCALE * share_b).astype(BF).astype(F32)
@@ -436,17 +451,18 @@
     router_total = router_total * (1.0 / (tokens * members))
     shares = jnp.transpose(router_total.reshape(experts, members, features // members), (1, 0, 2))
     shares = all_to_all(shares)
-    shares = all_to_all(jnp.broadcast_to(jnp.sum(shares, axis=0)[None], shares.shape))
-    router_total = jnp.transpose(shares, (1, 0, 2)).reshape(experts, features)
-    back_f, router_total = lax.optimization_barrier((back_f, router_total))
     extra = (score_grad, router_rows)
     input_grad = combine(picks_b, scale_b, back_b, bwd_grad, extra, "combine_backward")
     backward_out_rows = shifted(input_grad, "pipe", -1)
+    back_f, _ = lax.optimization_barrier((back_f, input_grad))
 
     one_hot_f, probs_f, total_f = gate_terms(fwd_rows, fwd_ids, router_rows)
     weights_f = ROUTE_SCALE * probs_f / total_f
     picks_f = [(slot_f[:, k : k + 1] == slot_axis[None, :]).astype(BF) for k in range(top)]
     layer_out = combine(picks_f, weights_f, back_f, fwd_rows, None, "combine_forward")
+    shares, layer_out = lax.optimization_barrier((shares, layer_out))
+    shares = all_to_all(jnp.broadcast_to(jnp.sum(shares, axis=0)[None], shares.shape))
+    router_total = jnp.transpose(shares, (1, 0, 2)).reshape(experts, features)
     forward_out_rows = shifted(layer_out, "pipe", 1)
     return (forward_out_rows[None], backward_out_rows[None], router_total[None])
 

time: 446 us -> 411 us (0.922)
  waiting for transfers between devices: 300 us -> 260 us
  starting transfers between devices: 52.3 us -> 59.9 us
    ppermute x2, waiting for transfers between devices: 33.5 us -> 1.02 us  [shifted(): return lax.ppermute(block, axis, route)]
    all_to_all x2, waiting for transfers between devices: 43.7 us -> 19.5 us  [all_to_all(): lax.all_to_all(block, 'expert', split_axis=0, concat_axis=0, tiled=True)]
    ppermute x6, waiting for transfers between devices: 27.6 us -> 50.2 us  [to_source(): lax.ppermute(block, 'expert', [(b, a) for a, b in piece_route(piece)])]
    ppermute x11, waiting for transfers between devices: 195 us -> 189 us  [exchanged(): return lax.ppermute(block, 'expert', route)]
    unnamed x75 -> x56, local copies, waits for them, and re-layouts: 17.3 us -> 17.2 us
  transfers between devices with their start and end apart: 23 -> 23, of which waited for: 10 -> 11; matrix products, arithmetic and copies ran while one was open for 4% -> 5% of each run, Pallas kernels for 6% -> 6%
where the time goes in v3:
time: 411 us; the launch traced here: 410 us
  waiting for transfers between devices  260 us (63%)
  starting transfers between devices  59.9 us (15%)
  Pallas kernels  41.6 us (10%)
  local copies, waits for them, and re-layouts  31.4 us (8%)
  other arithmetic  14 us (3%)
    ppermute x11, waiting for transfers between devices, exchanged(): return lax.ppermute(block, 'expert', route)  189 us
    ppermute x6, waiting for transfers between devices, to_source(): lax.ppermute(block, 'expert', [(b, a) for a, b in piece_route(piece)])  50.2 us
    all_to_all x2, waiting for transfers between devices, all_to_all(): lax.all_to_all(block, 'expert', split_axis=0, concat_axis=0, tiled=True)  19.5 us
    unnamed x56, local copies, waits for them, and re-layouts  17.2 us
    ppermute x11, starting transfers between devices, exchanged(): return lax.ppermute(block, 'expert', route)  15.4 us
    all_to_all x2, starting transfers between devices, all_to_all(): lax.all_to_all(block, 'expert', split_axis=0, concat_axis=0, tiled=True)  15.1 us
    ppermute x6, starting transfers between devices, to_source(): lax.ppermute(block, 'expert', [(b, a) for a, b in piece_route(piece)])  13.5 us
    pallas_call x1, Pallas kernels, backward_second(): pl.pallas_call(body, grid=(features // block,), in_specs=[pl.BlockSpec(a....  9.66 us
  transfers between devices with their start and end apart: 23, of which 11 were waited for; matrix products, arithmetic and copies ran while one was open for 5% of the time, Pallas kernels for 6%

profile of v3, /device:TPU:1, one launch (start us, length us, event | category | flops | bytes accessed | tf_op | source)
XLA Modules:
  0.0 409.6 jit_solution(8749396150649355229)
XLA Ops:
  0.7 4.3 %pad_maximum_fusion.refs_0_.refs_4_ = bf16[7168,256]{1,0:T(8,128)(2,1)} fusion(bf16[7168,128]{1,0:T(8,128)(2,1)} %bitcast.61, bf16[7168,128]{1,0:T(8,128)(2,1)} %bitcast.62), kind=kLoop, calls=%fused_computation.3 | loop fusion | flops 7340032 | bytes 7340032 | tf_op jit(solution)/shard_map/concatenate | solution.py:393
  5.0 2.5 collective-permute-start.2
  7.4 1.3 collective-permute-start.4
  13.6 1.2 copy-done.9
  14.8 3.3 pack.1
  18.1 5.4 %collective-permute-start = (bf16[80,16384]{1,0:T(8,128)(2,1)}, bf16[80,16384]{1,0:T(8,128)(2,1)S(1)}, u32[]{:S(2)}, u32[]{:S(2)}) collective-permute-start(bf16[80,16384]{1,0:T(8,128)(2,1)} %get-tuple-element.40), channel_id=1, source_target_pairs={{0,28},{1,29},{2,30},{3,31},{4,8},{5,9},{6,10},{7,11},{8,4},{9,5},... | collective-permute-start | bytes 7864328 | tf_op jit(solution)/shard_map/ppermute | solution.py:44
  23.7 103.3 %collective-permute-done.1.refs_9_.refs_1_ = bf16[128,7168]{1,0:T(8,128)(2,1)S(1)} collective-permute-done((bf16[128,7168]{1,0:T(8,128)(2,1)}, bf16[128,7168]{1,0:T(8,128)(2,1)S(1)}, u32[]{:S(2)}, u32[]{:S(2)}) %collective-permute-start.1) | collective-permute-done | bytes 1835040 | tf_op jit(solution)/shard_map/ppermute | solution.py:30
  128.4 3.1 collective-permute-start.5
  131.4 1.3 collective-permute-start.9
  132.9 2.4 collective-permute-start.6
  135.4 2.9 collective-permute-start.8
  139.7 80.6 %collective-permute-done.7 = bf16[32,7168]{1,0:T(8,128)(2,1)S(1)} collective-permute-done((bf16[32,7168]{1,0:T(8,128)(2,1)S(1)}, bf16[32,7168]{1,0:T(8,128)(2,1)S(1)}, u32[]{:S(2)}, u32[]{:S(2)}) %collective-permute-start.7) | collective-permute-done | bytes 458784 | tf_op jit(solution)/shard_map/ppermute | solution.py:30
  220.3 1.5 copy-done.17
  222.4 1.9 copy-done.18
  224.3 3.0 collective-permute-start.10
  227.3 1.2 constant_dynamic-update-slice_fusion.1
  228.5 1.4 constant_dynamic-update-slice_fusion.refs_11_.refs_3_
  229.9 2.2 collective-permute-done.10.refs_3_.refs_7_
  232.2 6.9 %backward_first.1 = (bf16[320,1024]{1,0:T(8,128)(2,1)S(1)}, f32[64,128]{1,0:T(8,128)S(1)}) custom-call(s32[1]{0:T(128)} %bitcast.12.chip_ref, bf16[80,16384]{1,0:T(8,128)(2,1)} %copy-done.1, bf16[80,16384]{1,0:T(8,128)(2,1)} %collective-permute-done.5.refs_1_.refs_5_, bf16[80,16384]{1,0:T(8,128)(2,1)} %copy-done.17, ...), custom_call_target="tpu_custom_call" | custom-call | tf_op jit(solution)/shard_map/backward_first/pallas_call | solution.py:187
  239.1 9.7 %backward_second.1 = (bf16[160,7168]{1,0:T(8,128)(2,1)S(1)}, bf16[160,7168]{1,0:T(8,128)(2,1)}) custom-call(bf16[320,1024]{1,0:T(8,128)(2,1)S(1)} %get-tuple-element.49.d_ref, f32[64,128]{1,0:T(8,128)S(1)} %get-tuple-element.50.inner_ref, bf16[7168,256]{1,0:T(8,128)(2,1)} %pad_maximum_fusion.refs_0_.refs_4_, ...), custom_call_target="tpu_custom_call" | custom-call | tf_op jit(solution)/shard_map/backward_second/pallas_call | solution.py:233
  248.8 1.4 copy-done.12
  252.2 2.7 collective-permute-done.11
  254.9 3.0 add_convert_fusion.1
  258.0 1.2 fusion.38
  259.2 2.2 collective-permute-start.12
  261.4 3.0 collective-permute-start.13
  264.9 9.6 %forward_first.1.hidden_ref = bf16[320,512]{1,0:T(8,128)(2,1)S(1)} custom-call(bf16[80,16384]{1,0:T(8,128)(2,1)S(1)} %copy-done.2, bf16[80,16384]{1,0:T(8,128)(2,1)} %collective-permute-done.5.refs_1_.refs_5_, bf16[80,16384]{1,0:T(8,128)(2,1)} %copy-done.17, bf16[80,16384]{1,0:T(8,128)(2,1)} %collective-permute-done.10.refs_3_.refs_7_, ...), custom_call_target="tpu_custom_call" | custom-call | tf_op jit(solution)/shard_map/forward_first/pallas_call | solution.py:277
  274.6 6.5 %forward_second.1 = (bf16[160,7168]{1,0:T(8,128)(2,1)}, bf16[160,7168]{1,0:T(8,128)(2,1)}) custom-call(bf16[320,512]{1,0:T(8,128)(2,1)S(1)} %forward_first.1.hidden_ref, bf16[128,7168]{1,0:T(8,128)(2,1)} %bitcast.9.refs_8_.refs_0_, bf16[128,7168]{1,0:T(8,128)(2,1)S(1)} %copy-done.6, bf16[128,7168]{1,0:T(8,128)(2,1)} %collective-permute-done.3.refs_10_.refs_2_, ...), custom_call_target="tpu_custom_call" | custom-call | tf_op jit(solution)/shard_map/forward_second/pallas_call | solution.py:303
  281.0 1.2 collective-permute-start.15
  282.6 7.5 %collective-permute-done.13.refs_5_ = bf16[40,7168]{1,0:T(8,128)(2,1)} collective-permute-done((bf16[40,7168]{1,0:T(8,128)(2,1)}, bf16[40,7168]{1,0:T(8,128)(2,1)}, u32[]{:S(2)}, u32[]{:S(2)}) %collective-permute-start.13) | collective-permute-done | bytes 573472 | tf_op jit(solution)/shard_map/ppermute | solution.py:50
  290.1 20.5 %collective-permute-done.14.refs_6_ = bf16[40,7168]{1,0:T(8,128)(2,1)} collective-permute-done((bf16[40,7168]{1,0:T(8,128)(2,1)}, bf16[40,7168]{1,0:T(8,128)(2,1)}, u32[]{:S(2)}, u32[]{:S(2)}) %collective-permute-start.14) | collective-permute-done | bytes 573472 | tf_op jit(solution)/shard_map/ppermute | solution.py:50
  313.5 3.0 add_convert_fusion
  316.6 1.4 fusion.37
  318.0 4.8 %collective-permute-start.16 = (bf16[40,7168]{1,0:T(8,128)(2,1)}, bf16[40,7168]{1,0:T(8,128)(2,1)}, u32[]{:S(2)}, u32[]{:S(2)}) collective-permute-start(bf16[40,7168]{1,0:T(8,128)(2,1)} %get-tuple-element.83), channel_id=1, source_target_pairs={{8,0},{9,1},{10,2},{11,3},{28,4},{29,5},{30,6},{31,7},{16,8},{17,9... | collective-permute-start | bytes 1720328 | tf_op jit(solution)/shard_map/ppermute | solution.py:50
  322.8 3.1 collective-permute-start.17
  327.0 1.7 reshape.154
  328.7 1.6 copy.148
  330.3 9.2 %all-to-all-start = ((f32[32,4,224]{2,1,0:T(4,128)}), f32[32,4,224]{2,1,0:T(4,128)}, u32[]{:S(2)}, u32[]{:S(2)}) async-start(f32[32,4,224]{2,1,0:T(4,128)} %bitcast.65), calls=%async_computation | async-start | bytes 262144 | tf_op jit(solution)/shard_map/all_to_all | solution.py:34
  342.4 3.4 combine_backward.1
  345.8 4.8 %collective-permute-start.20 = (bf16[64,7168]{1,0:T(8,128)(2,1)}, bf16[64,7168]{1,0:T(8,128)(2,1)}, u32[]{:S(2)}, u32[]{:S(2)}) collective-permute-start(bf16[64,7168]{1,0:T(8,128)(2,1)} %combine_backward.1), channel_id=1, source_target_pairs={{32,0},{64,32},{96,64},{128,96},{160,128},{192,160},{224,192},{0,2... | collective-permute-start | bytes 2752520 | tf_op jit(solution)/shard_map/ppermute | solution.py:25
  350.6 4.2 %collective-permute-done.17.refs_5_ = bf16[40,7168]{1,0:T(8,128)(2,1)} collective-permute-done((bf16[40,7168]{1,0:T(8,128)(2,1)}, bf16[40,7168]{1,0:T(8,128)(2,1)}, u32[]{:S(2)}, u32[]{:S(2)}) %collective-permute-start.17) | collective-permute-done | bytes 573472 | tf_op jit(solution)/shard_map/ppermute | solution.py:50
  354.8 18.0 %collective-permute-done.18.refs_6_ = bf16[40,7168]{1,0:T(8,128)(2,1)} collective-permute-done((bf16[40,7168]{1,0:T(8,128)(2,1)}, bf16[40,7168]{1,0:T(8,128)(2,1)}, u32[]{:S(2)}, u32[]{:S(2)}) %collective-permute-start.18) | collective-permute-done | bytes 573472 | tf_op jit(solution)/shard_map/ppermute | solution.py:50
  372.8 2.2 combine_forward.1
  375.0 5.1 %all-to-all-done = f32[32,4,224]{2,1,0:T(4,128)} async-done(((f32[32,4,224]{2,1,0:T(4,128)}), f32[32,4,224]{2,1,0:T(4,128)}, u32[]{:S(2)}, u32[]{:S(2)}) %all-to-all-start) | async-done | bytes 114720 | tf_op jit(solution)/shard_map/all_to_all | solution.py:34
  380.1 2.6 collective-permute-start.19
  384.4 5.9 %all-to-all-start.1 = ((f32[32,4,224]{2,1,0:T(4,128)}), f32[32,4,224]{2,1,0:T(4,128)S(1)}, u32[]{:S(2)}, u32[]{:S(2)}) async-start(f32[32,4,224]{2,1,0:T(4,128)} %broadcast_in_dim.13), calls=%async_computation.1 | async-start | bytes 262144 | tf_op jit(solution)/shard_map/all_to_all | solution.py:34
  390.2 14.4 %all-to-all-done.1 = f32[32,4,224]{2,1,0:T(4,128)S(1)} async-done(((f32[32,4,224]{2,1,0:T(4,128)}), f32[32,4,224]{2,1,0:T(4,128)S(1)}, u32[]{:S(2)}, u32[]{:S(2)}) %all-to-all-start.1) | async-done | bytes 114720 | tf_op jit(solution)/shard_map/all_to_all | solution.py:34
  407.5 2.2 copy.153
  (137 shorter events, 22.5 us)
Async XLA Ops:
  0.6 250.3 %copy-start = (bf16[1,64,7168]{2,1,0:T(8,128)(2,1)S(1)}, bf16[1,64,7168]{2,1,0:T(8,128)(2,1)}, u32[]{:S(2)}) copy-start(bf16[1,64,7168]{2,1,0:T(8,128)(2,1)} %param.12) | copy-start | bytes 2752516
  0.6 8.3 %copy-start.22 = (s32[1,64,2]{1,2,0:T(2,128)S(1)}, s32[1,64,2]{1,2,0:T(2,128)}, u32[]{:S(2)}) copy-start(s32[1,64,2]{1,2,0:T(2,128)} %param.13) | copy-start | bytes 1540
  0.7 9.2 %copy-start.24 = (s32[1,64,2]{1,2,0:T(2,128)S(1)}, s32[1,64,2]{1,2,0:T(2,128)}, u32[]{:S(2)}) copy-start(s32[1,64,2]{1,2,0:T(2,128)} %param.11) | copy-start | bytes 1540
  5.0 122.0 %collective-permute-start.2 = (bf16[7168,256]{1,0:T(8,128)(2,1)}, bf16[7168,256]{1,0:T(8,128)(2,1)}, u32[]{:S(2)}, u32[]{:S(2)}) collective-permute-start(bf16[7168,256]{1,0:T(8,128)(2,1)} %pad_maximum_fusion.refs_0_.refs_4_), channel_id=1, source_target_pairs={{0,4},{1,5},{2,6},{3,7},{4,0},{5,1},{6,2},{7,3},{8,12},{9,13},{10,... | collective-permute-start | bytes 11010056 | tf_op jit(solution)/shard_map/ppermute | solution.py:30
  7.4 119.6 %collective-permute-start.4 = (bf16[7168,256]{1,0:T(8,128)(2,1)}, bf16[7168,256]{1,0:T(8,128)(2,1)}, u32[]{:S(2)}, u32[]{:S(2)}) collective-permute-start(bf16[7168,256]{1,0:T(8,128)(2,1)} %pad_maximum_fusion.refs_0_.refs_4_), channel_id=1, source_target_pairs={{0,2},{1,3},{2,0},{3,1},{4,6},{5,7},{6,4},{7,5},{8,10},{9,11},{10,... | collective-permute-start | bytes 11010056 | tf_op jit(solution)/shard_map/ppermute | solution.py:30
  8.7 118.2 %collective-permute-start.1 = (bf16[128,7168]{1,0:T(8,128)(2,1)}, bf16[128,7168]{1,0:T(8,128)(2,1)S(1)}, u32[]{:S(2)}, u32[]{:S(2)}) collective-permute-start(bf16[128,7168]{1,0:T(8,128)(2,1)} %bitcast.9.refs_8_.refs_0_), channel_id=1, source_target_pairs={{0,2},{1,3},{2,0},{3,1},{4,6},{5,7},{6,4},{7,5},{8,10},{9,11},{10,... | collective-permute-start | bytes 5505032 | tf_op jit(solution)/shard_map/ppermute | solution.py:30
  8.9 118.1 %collective-permute-start.3 = (bf16[128,7168]{1,0:T(8,128)(2,1)}, bf16[128,7168]{1,0:T(8,128)(2,1)}, u32[]{:S(2)}, u32[]{:S(2)}) collective-permute-start(bf16[128,7168]{1,0:T(8,128)(2,1)} %bitcast.9.refs_8_.refs_0_), channel_id=1, source_target_pairs={{0,4},{1,5},{2,6},{3,7},{4,0},{5,1},{6,2},{7,3},{8,12},{9,13},{10,... | collective-permute-start | bytes 5505032 | tf_op jit(solution)/shard_map/ppermute | solution.py:30
  12.4 1.2 copy-start.7
  13.6 1.2 copy-start.9
  18.1 108.9 %collective-permute-start = (bf16[80,16384]{1,0:T(8,128)(2,1)}, bf16[80,16384]{1,0:T(8,128)(2,1)S(1)}, u32[]{:S(2)}, u32[]{:S(2)}) collective-permute-start(bf16[80,16384]{1,0:T(8,128)(2,1)} %get-tuple-element.40), channel_id=1, source_target_pairs={{0,28},{1,29},{2,30},{3,31},{4,8},{5,9},{6,10},{7,11},{8,4},{9,5},... | collective-permute-start | bytes 7864328 | tf_op jit(solution)/shard_map/ppermute | solution.py:44
  127.0 1.2 copy-start.3
  128.4 91.9 %collective-permute-start.5 = (bf16[80,16384]{1,0:T(8,128)(2,1)S(1)}, bf16[80,16384]{1,0:T(8,128)(2,1)}, u32[]{:S(2)}, u32[]{:S(2)}) collective-permute-start(bf16[80,16384]{1,0:T(8,128)(2,1)S(1)} %pad_maximum_fusion.2), channel_id=1, source_target_pairs={{0,8},{1,9},{2,10},{3,11},{4,28},{5,29},{6,30},{7,31},{8,16},{9,17... | collective-permute-start | bytes 7864328 | tf_op jit(solution)/shard_map/ppermute | solution.py:44
  131.4 90.4 %collective-permute-start.9 = (bf16[7168,256]{1,0:T(8,128)(2,1)}, bf16[7168,256]{1,0:T(8,128)(2,1)S(1)}, u32[]{:S(2)}, u32[]{:S(2)}) collective-permute-start(bf16[7168,256]{1,0:T(8,128)(2,1)} %collective-permute-done.2.refs_2_.refs_6_), channel_id=1, source_target_pairs={{0,2},{1,3},{2,0},{3,1},{4,6},{5,7},{6,4},{7,5},{8,10},{9,11},{10,... | collective-permute-start | bytes 11010056 | tf_op jit(solution)/shard_map/ppermute | solution.py:30
  132.7 2.6 copy-start.4
  132.9 95.6 %copy-start.1 = (bf16[80,16384]{1,0:T(8,128)(2,1)}, bf16[80,16384]{1,0:T(8,128)(2,1)S(1)}, u32[]{:S(2)}) copy-start(bf16[80,16384]{1,0:T(8,128)(2,1)S(1)} %pad_maximum_fusion.1.refs_0_.refs_4_) | copy-start | bytes 7864324
  132.9 87.4 %collective-permute-start.6 = (bf16[80,16384]{1,0:T(8,128)(2,1)S(1)}, bf16[80,16384]{1,0:T(8,128)(2,1)S(1)}, u32[]{:S(2)}, u32[]{:S(2)}) collective-permute-start(bf16[80,16384]{1,0:T(8,128)(2,1)S(1)} %pad_maximum_fusion.1.refs_0_.refs_4_), channel_id=1, source_target_pairs={{0,1},{1,0},{2,3},{3,2},{4,5},{5,4},{6,7},{7,6},{8,9},{9,8},{10,11... | collective-permute-start | bytes 7864328 | tf_op jit(solution)/shard_map/ppermute | solution.py:30
  135.4 84.8 %collective-permute-start.8 = (bf16[96,7168]{1,0:T(8,128)(2,1)S(1)}, bf16[96,7168]{1,0:T(8,128)(2,1)S(1)}, u32[]{:S(2)}, u32[]{:S(2)}) collective-permute-start(bf16[96,7168]{1,0:T(8,128)(2,1)S(1)} %slice.72), channel_id=1, source_target_pairs={{0,4},{1,5},{2,6},{3,7},{4,0},{5,1},{6,2},{7,3},{8,12},{9,13},{10,... | collective-permute-start | bytes 4128776 | tf_op jit(solution)/shard_map/ppermute | solution.py:30
  139.4 80.8 %collective-permute-start.7 = (bf16[32,7168]{1,0:T(8,128)(2,1)S(1)}, bf16[32,7168]{1,0:T(8,128)(2,1)S(1)}, u32[]{:S(2)}, u32[]{:S(2)}) collective-permute-start(bf16[32,7168]{1,0:T(8,128)(2,1)S(1)} %slice.71), channel_id=1, source_target_pairs={{0,2},{1,3},{2,0},{3,1},{4,6},{5,7},{6,4},{7,5},{8,10},{9,11},{10,... | collective-permute-start | bytes 1376264 | tf_op jit(solution)/shard_map/ppermute | solution.py:30
  220.3 1.6 copy-start.21
  220.3 2.2 copy-start.20
  220.3 1.5 copy-start.17
  222.4 1.9 copy-start.18
  224.3 7.8 %collective-permute-start.10 = (bf16[80,16384]{1,0:T(8,128)(2,1)}, bf16[80,16384]{1,0:T(8,128)(2,1)}, u32[]{:S(2)}, u32[]{:S(2)}) collective-permute-start(bf16[80,16384]{1,0:T(8,128)(2,1)} %collective-permute-done.5.refs_1_.refs_5_), channel_id=1, source_target_pairs={{0,1},{1,0},{2,3},{3,2},{4,5},{5,4},{6,7},{7,6},{8,9},{9,8},{10,11... | collective-permute-start | bytes 7864328 | tf_op jit(solution)/shard_map/ppermute | solution.py:30
  227.3 4.9 %copy-start.5 = (bf16[128,7168]{1,0:T(8,128)(2,1)S(1)}, bf16[128,7168]{1,0:T(8,128)(2,1)}, u32[]{:S(2)}) copy-start(bf16[128,7168]{1,0:T(8,128)(2,1)} %copy-done.3) | copy-start | bytes 5505028
  229.9 2.3 copy-start.19
  239.1 11.8 %copy-start.15 = (bf16[1,4,7168]{2,1,0:T(4,128)(2,1)S(1)}, bf16[1,4,7168]{2,1,0:T(4,128)(2,1)}, u32[]{:S(2)}) copy-start(bf16[1,4,7168]{2,1,0:T(4,128)(2,1)} %param.16) | copy-start | bytes 172036
  239.1 12.7 %copy-start.10 = (bf16[1,64,7168]{2,1,0:T(8,128)(2,1)S(1)}, bf16[1,64,7168]{2,1,0:T(8,128)(2,1)}, u32[]{:S(2)}) copy-start(bf16[1,64,7168]{2,1,0:T(8,128)(2,1)} %param.10) | copy-start | bytes 2752516
  248.8 1.4 copy-start.12
  250.2 4.8 %collective-permute-start.11 = (bf16[160,7168]{1,0:T(8,128)(2,1)}, bf16[160,7168]{1,0:T(8,128)(2,1)}, u32[]{:S(2)}, u32[]{:S(2)}) collective-permute-start(bf16[160,7168]{1,0:T(8,128)(2,1)} %get-tuple-element.54), channel_id=1, source_target_pairs={{0,1},{1,0},{2,3},{3,2},{4,5},{5,4},{6,7},{7,6},{8,9},{9,8},{10,11... | collective-permute-start | bytes 6881288 | tf_op jit(solution)/shard_map/ppermute | solution.py:30
  258.0 6.9 %copy-start.2 = (bf16[80,16384]{1,0:T(8,128)(2,1)S(1)}, bf16[80,16384]{1,0:T(8,128)(2,1)}, u32[]{:S(2)}) copy-start(bf16[80,16384]{1,0:T(8,128)(2,1)} %copy-done.1) | copy-start | bytes 7864324
  259.2 23.4 %collective-permute-start.12 = (bf16[40,7168]{1,0:T(8,128)(2,1)}, bf16[40,7168]{1,0:T(8,128)(2,1)S(1)}, u32[]{:S(2)}, u32[]{:S(2)}) collective-permute-start(bf16[40,7168]{1,0:T(8,128)(2,1)} %get-tuple-element.56), channel_id=1, source_target_pairs={{8,0},{9,1},{10,2},{11,3},{28,4},{29,5},{30,6},{31,7},{16,8},{17,9... | collective-permute-start | bytes 1720328 | tf_op jit(solution)/shard_map/ppermute | solution.py:50
  261.4 28.7 %collective-permute-start.13 = (bf16[40,7168]{1,0:T(8,128)(2,1)}, bf16[40,7168]{1,0:T(8,128)(2,1)}, u32[]{:S(2)}, u32[]{:S(2)}) collective-permute-start(bf16[40,7168]{1,0:T(8,128)(2,1)} %get-tuple-element.57), channel_id=1, source_target_pairs={{28,0},{29,1},{30,2},{31,3},{8,4},{9,5},{10,6},{11,7},{4,8},{5,9},... | collective-permute-start | bytes 1720328 | tf_op jit(solution)/shard_map/ppermute | solution.py:50
  264.5 46.1 %collective-permute-start.14 = (bf16[40,7168]{1,0:T(8,128)(2,1)}, bf16[40,7168]{1,0:T(8,128)(2,1)}, u32[]{:S(2)}, u32[]{:S(2)}) collective-permute-start(bf16[40,7168]{1,0:T(8,128)(2,1)} %get-tuple-element.58), channel_id=1, source_target_pairs={{20,0},{21,1},{22,2},{23,3},{16,4},{17,5},{18,6},{19,7},{28,8},{29... | collective-permute-start | bytes 1720328 | tf_op jit(solution)/shard_map/ppermute | solution.py:50
  264.9 9.7 %copy-start.6 = (bf16[128,7168]{1,0:T(8,128)(2,1)S(1)}, bf16[128,7168]{1,0:T(8,128)(2,1)}, u32[]{:S(2)}) copy-start(bf16[128,7168]{1,0:T(8,128)(2,1)} %copy-done.3) | copy-start | bytes 5505028
  281.0 32.5 %collective-permute-start.15 = (bf16[160,7168]{1,0:T(8,128)(2,1)}, bf16[160,7168]{1,0:T(8,128)(2,1)}, u32[]{:S(2)}, u32[]{:S(2)}) collective-permute-start(bf16[160,7168]{1,0:T(8,128)(2,1)} %get-tuple-element.68), channel_id=1, source_target_pairs={{0,1},{1,0},{2,3},{3,2},{4,5},{5,4},{6,7},{7,6},{8,9},{9,8},{10,11... | collective-permute-start | bytes 6881288 | tf_op jit(solution)/shard_map/ppermute | solution.py:30
  311.9 0.8 copy-start.13
  316.6 23.8 %copy-start.8 = (bf16[1,64,7168]{2,1,0:T(8,128)(2,1)S(1)}, bf16[1,64,7168]{2,1,0:T(8,128)(2,1)}, u32[]{:S(2)}) copy-start(bf16[1,64,7168]{2,1,0:T(8,128)(2,1)} %param.14) | copy-start | bytes 2752516
  318.0 32.6 %collective-permute-start.16 = (bf16[40,7168]{1,0:T(8,128)(2,1)}, bf16[40,7168]{1,0:T(8,128)(2,1)}, u32[]{:S(2)}, u32[]{:S(2)}) collective-permute-start(bf16[40,7168]{1,0:T(8,128)(2,1)} %get-tuple-element.83), channel_id=1, source_target_pairs={{8,0},{9,1},{10,2},{11,3},{28,4},{29,5},{30,6},{31,7},{16,8},{17,9... | collective-permute-start | bytes 1720328 | tf_op jit(solution)/shard_map/ppermute | solution.py:50
  322.8 32.0 %collective-permute-start.17 = (bf16[40,7168]{1,0:T(8,128)(2,1)}, bf16[40,7168]{1,0:T(8,128)(2,1)}, u32[]{:S(2)}, u32[]{:S(2)}) collective-permute-start(bf16[40,7168]{1,0:T(8,128)(2,1)} %get-tuple-element.82), channel_id=1, source_target_pairs={{28,0},{29,1},{30,2},{31,3},{8,4},{9,5},{10,6},{11,7},{4,8},{5,9},... | collective-permute-start | bytes 1720328 | tf_op jit(solution)/shard_map/ppermute | solution.py:50
  325.8 47.0 %collective-permute-start.18 = (bf16[40,7168]{1,0:T(8,128)(2,1)}, bf16[40,7168]{1,0:T(8,128)(2,1)}, u32[]{:S(2)}, u32[]{:S(2)}) collective-permute-start(bf16[40,7168]{1,0:T(8,128)(2,1)} %get-tuple-element.81), channel_id=1, source_target_pairs={{20,0},{21,1},{22,2},{23,3},{16,4},{17,5},{18,6},{19,7},{28,8},{29... | collective-permute-start | bytes 1720328 | tf_op jit(solution)/shard_map/ppermute | solution.py:50
  325.9 13.7 %copy-start.23 = (f32[64,4]{0,1:T(4,128)}, f32[64,4]{0,1:T(4,128)S(1)}, u32[]{:S(2)}) copy-start(f32[64,4]{0,1:T(4,128)S(1)} %select_reduce_fusion.3) | copy-start | bytes 3076
  330.3 49.8 %all-to-all-start = ((f32[32,4,224]{2,1,0:T(4,128)}), f32[32,4,224]{2,1,0:T(4,128)}, u32[]{:S(2)}, u32[]{:S(2)}) async-start(f32[32,4,224]{2,1,0:T(4,128)} %bitcast.65), calls=%async_computation | async-start | bytes 262144 | tf_op jit(solution)/shard_map/all_to_all | solution.py:34
  340.4 32.4 %copy-start.11 = (bf16[40,7168]{1,0:T(8,128)(2,1)S(1)}, bf16[40,7168]{1,0:T(8,128)(2,1)}, u32[]{:S(2)}) copy-start(bf16[40,7168]{1,0:T(8,128)(2,1)} %get-tuple-element.69.refs_3_) | copy-start | bytes 1720324
  340.4 1.1 copy-start.14
  341.5 0.8 copy-start.16
  345.8 44.5 %collective-permute-start.20 = (bf16[64,7168]{1,0:T(8,128)(2,1)}, bf16[64,7168]{1,0:T(8,128)(2,1)}, u32[]{:S(2)}, u32[]{:S(2)}) collective-permute-start(bf16[64,7168]{1,0:T(8,128)(2,1)} %combine_backward.1), channel_id=1, source_target_pairs={{32,0},{64,32},{96,64},{128,96},{160,128},{192,160},{224,192},{0,2... | collective-permute-start | bytes 2752520 | tf_op jit(solution)/shard_map/ppermute | solution.py:25
  380.1 26.4 %collective-permute-start.19 = (bf16[64,7168]{1,0:T(8,128)(2,1)S(1)}, bf16[64,7168]{1,0:T(8,128)(2,1)S(1)}, u32[]{:S(2)}, u32[]{:S(2)}) collective-permute-start(bf16[64,7168]{1,0:T(8,128)(2,1)S(1)} %combine_forward.1), channel_id=1, source_target_pairs={{224,0},{0,32},{32,64},{64,96},{96,128},{128,160},{160,192},{192,2... | collective-permute-start | bytes 2752520 | tf_op jit(solution)/shard_map/ppermute | solution.py:25
  384.4 20.3 %all-to-all-start.1 = ((f32[32,4,224]{2,1,0:T(4,128)}), f32[32,4,224]{2,1,0:T(4,128)S(1)}, u32[]{:S(2)}, u32[]{:S(2)}) async-start(f32[32,4,224]{2,1,0:T(4,128)} %broadcast_in_dim.13), calls=%async_computation.1 | async-start | bytes 262144 | tf_op jit(solution)/shard_map/all_to_all | solution.py:34

commit v4 on v3

--- a/solution.py
+++ b/solution.py
@@ -48,6 +48,16 @@
     if not piece:
         return block
     return lax.ppermute(block, "expert", [(b, a) for a, b in piece_route(piece)])
+
+
+def to_next(block, piece):
+    sections, members = lax.axis_size("pipe"), lax.axis_size("expert")
+    route = [
+        (p * members + b, (p + 1) % sections * members + a)
+        for p in range(sections)
+        for a, b in piece_route(piece)
+    ]
+    return lax.ppermute(block, ("pipe", "expert"), route)
 
 
 def gate_terms(tok_rows, ids, router_rows):
@@ -422,14 +432,18 @@
     d_joined, inner = backward_first(chip, parts, downs)
     keep, give = backward_second(d_joined, inner, joins)
     pieces = merged(keep, exchanged(give, 1))
-    parts, pieces = lax.optimization_barrier((parts, pieces))
+    _, probs_f, total_f = gate_terms(fwd_rows, fwd_ids, router_rows)
+    weights_f = ROUTE_SCALE * probs_f / total_f
+    plan_f = shifted(jnp.concatenate([slot_f.astype(F32), weights_f], axis=1), "pipe", 1)
+    parts, pieces, plan_f = lax.optimization_barrier((parts, pieces, plan_f))
+    next_rows = shifted(fwd_rows, "pipe", 1)
     back_b = [to_source(rows, k) for k, rows in enumerate(pieces)]
     hidden_f = forward_first(parts, joins)
     keep, give = forward_second(hidden_f, downs)
     swapped = exchanged(give, 1)
-    back_f = [to_source(rows, k) for k, rows in enumerate(merged(keep, swapped))]
-
-    back_b = lax.optimization_barrier(back_b)
+    back_f = [to_next(rows, k) for k, rows in enumerate(merged(keep, swapped))]
+
+    back_b, next_rows = lax.optimization_barrier((back_b, next_rows))
     one_hot_b, probs_b, total_b = gate_terms(bwd_rows, bwd_ids, router_rows)
     share_b = probs_b / total_b
     scale_b = (ROUTE_SCALE * share_b).astype(BF).astype(F32)
@@ -456,15 +470,13 @@
     backward_out_rows = shifted(input_grad, "pipe", -1)
     back_f, _ = lax.optimization_barrier((back_f, input_grad))
 
-    one_hot_f, probs_f, total_f = gate_terms(fwd_rows, fwd_ids, router_rows)
-    weights_f = ROUTE_SCALE * probs_f / total_f
+    slot_f, weights_f = plan_f[:, :top].astype(jnp.int32), plan_f[:, top:]
     picks_f = [(slot_f[:, k : k + 1] == slot_axis[None, :]).astype(BF) for k in range(top)]
-    layer_out = combine(picks_f, weights_f, back_f, fwd_rows, None, "combine_forward")
+    layer_out = combine(picks_f, weights_f, back_f, next_rows, None, "combine_forward")
     shares, layer_out = lax.optimization_barrier((shares, layer_out))
     shares = all_to_all(jnp.broadcast_to(jnp.sum(shares, axis=0)[None], shares.shape))
     router_total = jnp.transpose(shares, (1, 0, 2)).reshape(experts, features)
-    forward_out_rows = shifted(layer_out, "pipe", 1)
-    return (forward_out_rows[None], backward_out_rows[None], router_total[None])
+    return (layer_out[None], backward_out_rows[None], router_total[None])
 
 
 def solution(mesh):

time: 411 us -> 438 us (1.066)
  waiting for transfers between devices: 260 us -> 284 us
  starting transfers between devices: 59.9 us -> 65.6 us
  local copies, waits for them, and re-layouts: 31.4 us -> 26.2 us
    ppermute x0 -> x4, waiting for transfers between devices: none -> 39.3 us  [to_next(): return lax.ppermute(block, ('pipe', 'expert'), route)]
    ppermute x6 -> x3, waiting for transfers between devices: 50.2 us -> 26.2 us  [to_source(): lax.ppermute(block, 'expert', [(b, a) for a, b in piece_route(piece)])]
    ppermute x2 -> x3, waiting for transfers between devices: 1.02 us -> 16.9 us  [shifted(): return lax.ppermute(block, axis, route)]
    ppermute x0 -> x4, starting transfers between devices: none -> 10.5 us  [to_next(): return lax.ppermute(block, ('pipe', 'expert'), route)]
    ppermute x6 -> x3, starting transfers between devices: 13.5 us -> 5.68 us  [to_source(): lax.ppermute(block, 'expert', [(b, a) for a, b in piece_route(piece)])]
    unnamed x56 -> x57, local copies, waits for them, and re-layouts: 17.2 us -> 16.6 us
  transfers between devices with their start and end apart: 23 -> 25, of which waited for: 11 -> 10; matrix products, arithmetic and copies ran while one was open for 5% -> 5% of each run, Pallas kernels for 6% -> 6%
where the time goes in v4:
time: 438 us; the launch traced here: 433 us
  waiting for transfers between devices  284 us (65%)
  starting transfers between devices  65.6 us (15%)
  Pallas kernels  42 us (10%)
  local copies, waits for them, and re-layouts  26.2 us (6%)
  other arithmetic  11.8 us (3%)
    ppermute x11, waiting for transfers between devices, exchanged(): return lax.ppermute(block, 'expert', route)  186 us
    ppermute x4, waiting for transfers between devices, to_next(): return lax.ppermute(block, ('pipe', 'expert'), route)  39.3 us
    ppermute x3, waiting for transfers between devices, to_source(): lax.ppermute(block, 'expert', [(b, a) for a, b in piece_route(piece)])  26.2 us
    all_to_all x2, starting transfers between devices, all_to_all(): lax.all_to_all(block, 'expert', split_axis=0, concat_axis=0, tiled=True)  17.9 us
    ppermute x3, waiting for transfers between devices, shifted(): return lax.ppermute(block, axis, route)  16.9 us
    unnamed x57, local copies, waits for them, and re-layouts  16.6 us
    ppermute x11, starting transfers between devices, exchanged(): return lax.ppermute(block, 'expert', route)  15.8 us
    all_to_all x2, waiting for transfers between devices, all_to_all(): lax.all_to_all(block, 'expert', split_axis=0, concat_axis=0, tiled=True)  15.8 us
  transfers between devices with their start and end apart: 25, of which 10 were waited for; matrix products, arithmetic and copies ran while one was open for 5% of the time, Pallas kernels for 6%

profile of v4, /device:TPU:1, one launch (start us, length us, event | category | flops | bytes accessed | tf_op | source)
XLA Modules:
  0.0 433.4 jit_solution(1365025206220927744)
XLA Ops:
  0.7 4.3 pad_maximum_fusion.refs_0_.refs_4_
  5.0 2.5 collective-permute-start.2
  7.4 1.3 collective-permute-start.4
  11.3 1.2 copy.157
  12.5 1.2 copy-done.7
  13.7 4.5 %pack.1 = (bf16[80,16384]{1,0:T(8,128)(2,1)S(1)}, bf16[80,16384]{1,0:T(8,128)(2,1)}) custom-call(s32[1]{0:T(128)} %bitcast.4.core_ref, bf16[160,64]{1,0:T(8,128)(2,1)S(1)} %copy.141.f_ref, bf16[160,64]{1,0:T(8,128)(2,1)S(1)} %copy.142.b_ref, bf16[160,128]{1,0:T(8,128)(2,1)S(1)} %fusion.3.pairs_ref, bf16[64,7168]{1,0:T(8,128)(2,1)} %bitcast.7.rows_f_ref, ...), custom_call_target="tpu_custom_call" | custom-call | tf_op jit(solution)/shard_map/pack/pallas_call | solution.py:123
  18.1 5.4 %collective-permute-start = (bf16[80,16384]{1,0:T(8,128)(2,1)}, bf16[80,16384]{1,0:T(8,128)(2,1)S(1)}, u32[]{:S(2)}, u32[]{:S(2)}) collective-permute-start(bf16[80,16384]{1,0:T(8,128)(2,1)} %get-tuple-element.42), channel_id=1, source_target_pairs={{0,28},{1,29},{2,30},{3,31},{4,8},{5,9},{6,10},{7,11},{8,4},{9,5},... | collective-permute-start | bytes 7864328 | tf_op jit(solution)/shard_map/ppermute | solution.py:44
  23.8 103.2 %collective-permute-done.1.refs_9_.refs_1_ = bf16[128,7168]{1,0:T(8,128)(2,1)S(1)} collective-permute-done((bf16[128,7168]{1,0:T(8,128)(2,1)}, bf16[128,7168]{1,0:T(8,128)(2,1)S(1)}, u32[]{:S(2)}, u32[]{:S(2)}) %collective-permute-start.1) | collective-permute-done | bytes 1835040 | tf_op jit(solution)/shard_map/ppermute | solution.py:30
  128.4 3.1 collective-permute-start.5
  131.4 1.3 collective-permute-start.9
  132.9 2.4 collective-permute-start.6
  135.4 2.9 collective-permute-start.8
  139.7 80.6 %collective-permute-done.7 = bf16[32,7168]{1,0:T(8,128)(2,1)S(1)} collective-permute-done((bf16[32,7168]{1,0:T(8,128)(2,1)S(1)}, bf16[32,7168]{1,0:T(8,128)(2,1)S(1)}, u32[]{:S(2)}, u32[]{:S(2)}) %collective-permute-start.7) | collective-permute-done | bytes 458784 | tf_op jit(solution)/shard_map/ppermute | solution.py:30
  220.3 1.5 copy-done.16
  222.5 1.9 copy-done.17
  224.4 3.0 collective-permute-start.10
  227.3 1.2 constant_dynamic-update-slice_fusion.1
  228.5 1.4 constant_dynamic-update-slice_fusion.refs_11_.refs_3_
  230.0 2.2 collective-permute-done.10.refs_3_.refs_7_
  232.2 6.9 %backward_first.1 = (bf16[320,1024]{1,0:T(8,128)(2,1)S(1)}, f32[64,128]{1,0:T(8,128)S(1)}) custom-call(s32[1]{0:T(128)} %bitcast.12.chip_ref, bf16[80,16384]{1,0:T(8,128)(2,1)} %copy-done.1, bf16[80,16384]{1,0:T(8,128)(2,1)} %collective-permute-done.5.refs_1_.refs_5_, bf16[80,16384]{1,0:T(8,128)(2,1)} %copy-done.16, ...), custom_call_target="tpu_custom_call" | custom-call | tf_op jit(solution)/shard_map/backward_first/pallas_call | solution.py:197
  239.2 9.6 %backward_second.1 = (bf16[160,7168]{1,0:T(8,128)(2,1)S(1)}, bf16[160,7168]{1,0:T(8,128)(2,1)}) custom-call(bf16[320,1024]{1,0:T(8,128)(2,1)S(1)} %get-tuple-element.51.d_ref, f32[64,128]{1,0:T(8,128)S(1)} %get-tuple-element.52.inner_ref, bf16[7168,256]{1,0:T(8,128)(2,1)} %pad_maximum_fusion.refs_0_.refs_4_, ...), custom_call_target="tpu_custom_call" | custom-call | tf_op jit(solution)/shard_map/backward_second/pallas_call | solution.py:243
  249.1 2.9 collective-permute-start.16
  252.4 1.5 fusion.32
  256.2 2.3 add_convert_fusion.1
  258.7 16.9 %collective-permute-done.12 = f32[64,4]{1,0:T(8,128)S(1)} collective-permute-done((f32[64,4]{1,0:T(8,128)S(1)}, f32[64,4]{1,0:T(8,128)S(1)}, u32[]{:S(2)}, u32[]{:S(2)}) %collective-permute-start.12) | collective-permute-done | bytes 1056 | tf_op jit(solution)/shard_map/ppermute | solution.py:25
  275.6 2.2 collective-permute-start.13
  277.8 3.0 collective-permute-start.14
  281.4 9.6 %forward_first.1.hidden_ref = bf16[320,512]{1,0:T(8,128)(2,1)S(1)} custom-call(bf16[80,16384]{1,0:T(8,128)(2,1)S(1)} %copy-done.2, bf16[80,16384]{1,0:T(8,128)(2,1)} %collective-permute-done.5.refs_1_.refs_5_, bf16[80,16384]{1,0:T(8,128)(2,1)} %copy-done.16, bf16[80,16384]{1,0:T(8,128)(2,1)} %collective-permute-done.10.refs_3_.refs_7_, ...), custom_call_target="tpu_custom_call" | custom-call | tf_op jit(solution)/shard_map/forward_first/pallas_call | solution.py:287
  291.1 6.5 %forward_second.1 = (bf16[160,7168]{1,0:T(8,128)(2,1)}, bf16[160,7168]{1,0:T(8,128)(2,1)}) custom-call(bf16[320,512]{1,0:T(8,128)(2,1)S(1)} %forward_first.1.hidden_ref, bf16[128,7168]{1,0:T(8,128)(2,1)} %bitcast.9.refs_8_.refs_0_, bf16[128,7168]{1,0:T(8,128)(2,1)S(1)} %copy-done.6, bf16[128,7168]{1,0:T(8,128)(2,1)} %collective-permute-done.3.refs_10_.refs_2_, ...), custom_call_target="tpu_custom_call" | custom-call | tf_op jit(solution)/shard_map/forward_second/pallas_call | solution.py:313
  297.6 1.7 collective-permute-start.17
  300.0 5.7 %collective-permute-done.14.refs_5_ = bf16[40,7168]{1,0:T(8,128)(2,1)S(1)} collective-permute-done((bf16[40,7168]{1,0:T(8,128)(2,1)S(1)}, bf16[40,7168]{1,0:T(8,128)(2,1)S(1)}, u32[]{:S(2)}, u32[]{:S(2)}) %collective-permute-start.14) | collective-permute-done | bytes 573472 | tf_op jit(solution)/shard_map/ppermute | solution.py:50
  305.7 20.5 %collective-permute-done.15.refs_6_ = bf16[40,7168]{1,0:T(8,128)(2,1)S(1)} collective-permute-done((bf16[40,7168]{1,0:T(8,128)(2,1)S(1)}, bf16[40,7168]{1,0:T(8,128)(2,1)S(1)}, u32[]{:S(2)}, u32[]{:S(2)}) %collective-permute-start.15) | collective-permute-done | bytes 573472 | tf_op jit(solution)/shard_map/ppermute | solution.py:50
  330.6 1.1 copy-done.12
  331.7 1.1 copy-done.14
  332.7 1.8 combine_backward.1
  334.6 3.2 collective-permute-start.22
  337.8 2.3 add_convert_fusion
  340.1 1.4 fusion.38
  341.6 6.1 %collective-permute-start.19 = (bf16[40,7168]{1,0:T(8,128)(2,1)}, bf16[40,7168]{1,0:T(8,128)(2,1)S(1)}, u32[]{:S(2)}, u32[]{:S(2)}) collective-permute-start(bf16[40,7168]{1,0:T(8,128)(2,1)} %get-tuple-element.89), channel_id=1, source_target_pairs={{8,32},{9,33},{10,34},{11,35},{28,36},{29,37},{30,38},{31,39},{16,... | collective-permute-start | bytes 1720328 | tf_op jit(solution)/shard_map/ppermute | solution.py:60
  347.7 3.7 collective-permute-start.20
  353.5 11.4 %all-to-all-start = ((f32[32,4,224]{2,1,0:T(4,128)}), f32[32,4,224]{2,1,0:T(4,128)S(1)}, u32[]{:S(2)}, u32[]{:S(2)}) async-start(f32[32,4,224]{2,1,0:T(4,128)} %bitcast.50), calls=%async_computation | async-start | bytes 262144 | tf_op jit(solution)/shard_map/all_to_all | solution.py:34
  365.0 30.3 %collective-permute-done.18.refs_3_ = bf16[40,7168]{1,0:T(8,128)(2,1)S(1)} collective-permute-done((bf16[40,7168]{1,0:T(8,128)(2,1)}, bf16[40,7168]{1,0:T(8,128)(2,1)S(1)}, u32[]{:S(2)}, u32[]{:S(2)}) %collective-permute-start.18) | collective-permute-done | bytes 573472 | tf_op jit(solution)/shard_map/ppermute | solution.py:60
  395.4 8.9 %collective-permute-done.21.refs_6_ = bf16[40,7168]{1,0:T(8,128)(2,1)} collective-permute-done((bf16[40,7168]{1,0:T(8,128)(2,1)}, bf16[40,7168]{1,0:T(8,128)(2,1)}, u32[]{:S(2)}, u32[]{:S(2)}) %collective-permute-start.21) | collective-permute-done | bytes 573472 | tf_op jit(solution)/shard_map/ppermute | solution.py:60
  404.3 3.0 combine_forward.1
  407.3 6.5 %all-to-all-done = f32[32,4,224]{2,1,0:T(4,128)S(1)} async-done(((f32[32,4,224]{2,1,0:T(4,128)}), f32[32,4,224]{2,1,0:T(4,128)S(1)}, u32[]{:S(2)}, u32[]{:S(2)}) %all-to-all-start) | async-done | bytes 114720 | tf_op jit(solution)/shard_map/all_to_all | solution.py:34
  414.6 6.5 %all-to-all-start.1 = ((f32[32,4,224]{2,1,0:T(4,128)}), f32[32,4,224]{2,1,0:T(4,128)S(1)}, u32[]{:S(2)}, u32[]{:S(2)}) async-start(f32[32,4,224]{2,1,0:T(4,128)} %broadcast_in_dim.13), calls=%async_computation.1 | async-start | bytes 262144 | tf_op jit(solution)/shard_map/all_to_all | solution.py:34
  421.1 9.3 %all-to-all-done.1 = f32[32,4,224]{2,1,0:T(4,128)S(1)} async-done(((f32[32,4,224]{2,1,0:T(4,128)}), f32[32,4,224]{2,1,0:T(4,128)S(1)}, u32[]{:S(2)}, u32[]{:S(2)}) %all-to-all-start.1) | async-done | bytes 114720 | tf_op jit(solution)/shard_map/all_to_all | solution.py:34
  431.2 2.2 copy.162
  (147 shorter events, 18.8 us)
Async XLA Ops:
  0.6 254.9 %copy-start = (bf16[1,64,7168]{2,1,0:T(8,128)(2,1)S(1)}, bf16[1,64,7168]{2,1,0:T(8,128)(2,1)}, u32[]{:S(2)}) copy-start(bf16[1,64,7168]{2,1,0:T(8,128)(2,1)} %param.12) | copy-start | bytes 2752516
  0.6 8.3 %copy-start.22 = (s32[1,64,2]{1,2,0:T(2,128)S(1)}, s32[1,64,2]{1,2,0:T(2,128)}, u32[]{:S(2)}) copy-start(s32[1,64,2]{1,2,0:T(2,128)} %param.13) | copy-start | bytes 1540
  0.7 9.5 %copy-start.23 = (s32[1,64,2]{1,2,0:T(2,128)S(1)}, s32[1,64,2]{1,2,0:T(2,128)}, u32[]{:S(2)}) copy-start(s32[1,64,2]{1,2,0:T(2,128)} %param.11) | copy-start | bytes 1540
  5.0 122.0 %collective-permute-start.2 = (bf16[7168,256]{1,0:T(8,128)(2,1)}, bf16[7168,256]{1,0:T(8,128)(2,1)}, u32[]{:S(2)}, u32[]{:S(2)}) collective-permute-start(bf16[7168,256]{1,0:T(8,128)(2,1)} %pad_maximum_fusion.refs_0_.refs_4_), channel_id=1, source_target_pairs={{0,4},{1,5},{2,6},{3,7},{4,0},{5,1},{6,2},{7,3},{8,12},{9,13},{10,... | collective-permute-start | bytes 11010056 | tf_op jit(solution)/shard_map/ppermute | solution.py:30
  7.4 119.6 %collective-permute-start.4 = (bf16[7168,256]{1,0:T(8,128)(2,1)}, bf16[7168,256]{1,0:T(8,128)(2,1)}, u32[]{:S(2)}, u32[]{:S(2)}) collective-permute-start(bf16[7168,256]{1,0:T(8,128)(2,1)} %pad_maximum_fusion.refs_0_.refs_4_), channel_id=1, source_target_pairs={{0,2},{1,3},{2,0},{3,1},{4,6},{5,7},{6,4},{7,5},{8,10},{9,11},{10,... | collective-permute-start | bytes 11010056 | tf_op jit(solution)/shard_map/ppermute | solution.py:30
  8.7 118.2 %collective-permute-start.1 = (bf16[128,7168]{1,0:T(8,128)(2,1)}, bf16[128,7168]{1,0:T(8,128)(2,1)S(1)}, u32[]{:S(2)}, u32[]{:S(2)}) collective-permute-start(bf16[128,7168]{1,0:T(8,128)(2,1)} %bitcast.9.refs_8_.refs_0_), channel_id=1, source_target_pairs={{0,2},{1,3},{2,0},{3,1},{4,6},{5,7},{6,4},{7,5},{8,10},{9,11},{10,... | collective-permute-start | bytes 5505032 | tf_op jit(solution)/shard_map/ppermute | solution.py:30
  8.9 118.1 %collective-permute-start.3 = (bf16[128,7168]{1,0:T(8,128)(2,1)}, bf16[128,7168]{1,0:T(8,128)(2,1)}, u32[]{:S(2)}, u32[]{:S(2)}) collective-permute-start(bf16[128,7168]{1,0:T(8,128)(2,1)} %bitcast.9.refs_8_.refs_0_), channel_id=1, source_target_pairs={{0,4},{1,5},{2,6},{3,7},{4,0},{5,1},{6,2},{7,3},{8,12},{9,13},{10,... | collective-permute-start | bytes 5505032 | tf_op jit(solution)/shard_map/ppermute | solution.py:30
  12.5 1.2 copy-start.7
  18.1 108.8 %collective-permute-start = (bf16[80,16384]{1,0:T(8,128)(2,1)}, bf16[80,16384]{1,0:T(8,128)(2,1)S(1)}, u32[]{:S(2)}, u32[]{:S(2)}) collective-permute-start(bf16[80,16384]{1,0:T(8,128)(2,1)} %get-tuple-element.42), channel_id=1, source_target_pairs={{0,28},{1,29},{2,30},{3,31},{4,8},{5,9},{6,10},{7,11},{8,4},{9,5},... | collective-permute-start | bytes 7864328 | tf_op jit(solution)/shard_map/ppermute | solution.py:44
  127.0 1.2 copy-start.3
  128.4 91.9 %collective-permute-start.5 = (bf16[80,16384]{1,0:T(8,128)(2,1)S(1)}, bf16[80,16384]{1,0:T(8,128)(2,1)}, u32[]{:S(2)}, u32[]{:S(2)}) collective-permute-start(bf16[80,16384]{1,0:T(8,128)(2,1)S(1)} %pad_maximum_fusion.2), channel_id=1, source_target_pairs={{0,8},{1,9},{2,10},{3,11},{4,28},{5,29},{6,30},{7,31},{8,16},{9,17... | collective-permute-start | bytes 7864328 | tf_op jit(solution)/shard_map/ppermute | solution.py:44
  131.4 90.4 %collective-permute-start.9 = (bf16[7168,256]{1,0:T(8,128)(2,1)}, bf16[7168,256]{1,0:T(8,128)(2,1)S(1)}, u32[]{:S(2)}, u32[]{:S(2)}) collective-permute-start(bf16[7168,256]{1,0:T(8,128)(2,1)} %collective-permute-done.2.refs_2_.refs_6_), channel_id=1, source_target_pairs={{0,2},{1,3},{2,0},{3,1},{4,6},{5,7},{6,4},{7,5},{8,10},{9,11},{10,... | collective-permute-start | bytes 11010056 | tf_op jit(solution)/shard_map/ppermute | solution.py:30
  132.7 2.6 copy-start.4
  132.9 95.6 %copy-start.1 = (bf16[80,16384]{1,0:T(8,128)(2,1)}, bf16[80,16384]{1,0:T(8,128)(2,1)S(1)}, u32[]{:S(2)}) copy-start(bf16[80,16384]{1,0:T(8,128)(2,1)S(1)} %pad_maximum_fusion.1.refs_0_.refs_4_) | copy-start | bytes 7864324
  132.9 87.4 %collective-permute-start.6 = (bf16[80,16384]{1,0:T(8,128)(2,1)S(1)}, bf16[80,16384]{1,0:T(8,128)(2,1)S(1)}, u32[]{:S(2)}, u32[]{:S(2)}) collective-permute-start(bf16[80,16384]{1,0:T(8,128)(2,1)S(1)} %pad_maximum_fusion.1.refs_0_.refs_4_), channel_id=1, source_target_pairs={{0,1},{1,0},{2,3},{3,2},{4,5},{5,4},{6,7},{7,6},{8,9},{9,8},{10,11... | collective-permute-start | bytes 7864328 | tf_op jit(solution)/shard_map/ppermute | solution.py:30
  135.4 84.8 %collective-permute-start.8 = (bf16[96,7168]{1,0:T(8,128)(2,1)S(1)}, bf16[96,7168]{1,0:T(8,128)(2,1)S(1)}, u32[]{:S(2)}, u32[]{:S(2)}) collective-permute-start(bf16[96,7168]{1,0:T(8,128)(2,1)S(1)} %slice.78), channel_id=1, source_target_pairs={{0,4},{1,5},{2,6},{3,7},{4,0},{5,1},{6,2},{7,3},{8,12},{9,13},{10,... | collective-permute-start | bytes 4128776 | tf_op jit(solution)/shard_map/ppermute | solution.py:30
  139.4 80.8 %collective-permute-start.7 = (bf16[32,7168]{1,0:T(8,128)(2,1)S(1)}, bf16[32,7168]{1,0:T(8,128)(2,1)S(1)}, u32[]{:S(2)}, u32[]{:S(2)}) collective-permute-start(bf16[32,7168]{1,0:T(8,128)(2,1)S(1)} %slice.77), channel_id=1, source_target_pairs={{0,2},{1,3},{2,0},{3,1},{4,6},{5,7},{6,4},{7,5},{8,10},{9,11},{10,... | collective-permute-start | bytes 1376264 | tf_op jit(solution)/shard_map/ppermute | solution.py:30
  220.3 1.6 copy-start.21
  220.3 2.2 copy-start.20
  220.3 1.5 copy-start.16
  222.4 1.9 copy-start.17
  224.4 7.8 %collective-permute-start.10 = (bf16[80,16384]{1,0:T(8,128)(2,1)}, bf16[80,16384]{1,0:T(8,128)(2,1)}, u32[]{:S(2)}, u32[]{:S(2)}) collective-permute-start(bf16[80,16384]{1,0:T(8,128)(2,1)} %collective-permute-done.5.refs_1_.refs_5_), channel_id=1, source_target_pairs={{0,1},{1,0},{2,3},{3,2},{4,5},{5,4},{6,7},{7,6},{8,9},{9,8},{10,11... | collective-permute-start | bytes 7864328 | tf_op jit(solution)/shard_map/ppermute | solution.py:30
  227.3 4.9 %copy-start.5 = (bf16[128,7168]{1,0:T(8,128)(2,1)S(1)}, bf16[128,7168]{1,0:T(8,128)(2,1)}, u32[]{:S(2)}) copy-start(bf16[128,7168]{1,0:T(8,128)(2,1)} %copy-done.3) | copy-start | bytes 5505028
  229.9 2.3 copy-start.18
  239.1 13.3 %copy-start.15 = (bf16[1,4,7168]{2,1,0:T(4,128)(2,1)S(1)}, bf16[1,4,7168]{2,1,0:T(4,128)(2,1)}, u32[]{:S(2)}) copy-start(bf16[1,4,7168]{2,1,0:T(4,128)(2,1)} %param.16) | copy-start | bytes 172036
  248.7 7.5 %collective-permute-start.11 = (bf16[160,7168]{1,0:T(8,128)(2,1)}, bf16[160,7168]{1,0:T(8,128)(2,1)}, u32[]{:S(2)}, u32[]{:S(2)}) collective-permute-start(bf16[160,7168]{1,0:T(8,128)(2,1)} %get-tuple-element.56), channel_id=1, source_target_pairs={{0,1},{1,0},{2,3},{3,2},{4,5},{5,4},{6,7},{7,6},{8,9},{9,8},{10,11... | collective-permute-start | bytes 6881288 | tf_op jit(solution)/shard_map/ppermute | solution.py:30
  249.1 50.9 %collective-permute-start.16 = (bf16[64,7168]{1,0:T(8,128)(2,1)}, bf16[64,7168]{1,0:T(8,128)(2,1)}, u32[]{:S(2)}, u32[]{:S(2)}) collective-permute-start(bf16[64,7168]{1,0:T(8,128)(2,1)} %bitcast.7.rows_f_ref), channel_id=1, source_target_pairs={{224,0},{0,32},{32,64},{64,96},{96,128},{128,160},{160,192},{192,2... | collective-permute-start | bytes 2752520 | tf_op jit(solution)/shard_map/ppermute | solution.py:25
  254.5 21.1 %collective-permute-start.12 = (f32[64,4]{1,0:T(8,128)S(1)}, f32[64,4]{1,0:T(8,128)S(1)}, u32[]{:S(2)}, u32[]{:S(2)}) collective-permute-start(f32[64,4]{1,0:T(8,128)S(1)} %copy.148), channel_id=1, source_target_pairs={{224,0},{0,32},{32,64},{64,96},{96,128},{128,160},{160,192},{192,2... | collective-permute-start | bytes 3080 | tf_op jit(solution)/shard_map/ppermute | solution.py:25
  258.5 22.8 %copy-start.2 = (bf16[80,16384]{1,0:T(8,128)(2,1)S(1)}, bf16[80,16384]{1,0:T(8,128)(2,1)}, u32[]{:S(2)}) copy-start(bf16[80,16384]{1,0:T(8,128)(2,1)} %copy-done.1) | copy-start | bytes 7864324
  275.6 24.4 %collective-permute-start.13 = (bf16[40,7168]{1,0:T(8,128)(2,1)S(1)}, bf16[40,7168]{1,0:T(8,128)(2,1)S(1)}, u32[]{:S(2)}, u32[]{:S(2)}) collective-permute-start(bf16[40,7168]{1,0:T(8,128)(2,1)S(1)} %get-tuple-element.58), channel_id=1, source_target_pairs={{8,0},{9,1},{10,2},{11,3},{28,4},{29,5},{30,6},{31,7},{16,8},{17,9... | collective-permute-start | bytes 1720328 | tf_op jit(solution)/shard_map/ppermute | solution.py:50
  277.8 27.9 %collective-permute-start.14 = (bf16[40,7168]{1,0:T(8,128)(2,1)S(1)}, bf16[40,7168]{1,0:T(8,128)(2,1)S(1)}, u32[]{:S(2)}, u32[]{:S(2)}) collective-permute-start(bf16[40,7168]{1,0:T(8,128)(2,1)S(1)} %get-tuple-element.59), channel_id=1, source_target_pairs={{28,0},{29,1},{30,2},{31,3},{8,4},{9,5},{10,6},{11,7},{4,8},{5,9},... | collective-permute-start | bytes 1720328 | tf_op jit(solution)/shard_map/ppermute | solution.py:50
  280.9 45.3 %collective-permute-start.15 = (bf16[40,7168]{1,0:T(8,128)(2,1)S(1)}, bf16[40,7168]{1,0:T(8,128)(2,1)S(1)}, u32[]{:S(2)}, u32[]{:S(2)}) collective-permute-start(bf16[40,7168]{1,0:T(8,128)(2,1)S(1)} %get-tuple-element.60), channel_id=1, source_target_pairs={{20,0},{21,1},{22,2},{23,3},{16,4},{17,5},{18,6},{19,7},{28,8},{29... | collective-permute-start | bytes 1720328 | tf_op jit(solution)/shard_map/ppermute | solution.py:50
  281.4 9.7 %copy-start.6 = (bf16[128,7168]{1,0:T(8,128)(2,1)S(1)}, bf16[128,7168]{1,0:T(8,128)(2,1)}, u32[]{:S(2)}) copy-start(bf16[128,7168]{1,0:T(8,128)(2,1)} %copy-done.3) | copy-start | bytes 5505028
  291.1 38.5 %copy-start.8 = (bf16[1,64,7168]{2,1,0:T(8,128)(2,1)S(1)}, bf16[1,64,7168]{2,1,0:T(8,128)(2,1)}, u32[]{:S(2)}) copy-start(bf16[1,64,7168]{2,1,0:T(8,128)(2,1)} %param.14) | copy-start | bytes 2752516
  297.6 40.2 %collective-permute-start.17 = (bf16[160,7168]{1,0:T(8,128)(2,1)}, bf16[160,7168]{1,0:T(8,128)(2,1)}, u32[]{:S(2)}, u32[]{:S(2)}) collective-permute-start(bf16[160,7168]{1,0:T(8,128)(2,1)} %get-tuple-element.71), channel_id=1, source_target_pairs={{0,1},{1,0},{2,3},{3,2},{4,5},{5,4},{6,7},{7,6},{8,9},{9,8},{10,11... | collective-permute-start | bytes 6881288 | tf_op jit(solution)/shard_map/ppermute | solution.py:30
  329.5 1.1 copy-start.10
  330.6 1.1 copy-start.12
  331.7 1.1 copy-start.14
  332.7 5.1 %copy-start.19 = (bf16[160,7168]{1,0:T(8,128)(2,1)S(1)}, bf16[160,7168]{1,0:T(8,128)(2,1)}, u32[]{:S(2)}) copy-start(bf16[160,7168]{1,0:T(8,128)(2,1)} %get-tuple-element.70) | copy-start | bytes 6881284
  334.6 86.6 %collective-permute-start.22 = (bf16[64,7168]{1,0:T(8,128)(2,1)S(1)}, bf16[64,7168]{1,0:T(8,128)(2,1)}, u32[]{:S(2)}, u32[]{:S(2)}) collective-permute-start(bf16[64,7168]{1,0:T(8,128)(2,1)S(1)} %combine_backward.1), channel_id=1, source_target_pairs={{32,0},{64,32},{96,64},{128,96},{160,128},{192,160},{224,192},{0,2... | collective-permute-start | bytes 2752520 | tf_op jit(solution)/shard_map/ppermute | solution.py:25
  340.1 12.0 %copy-start.25 = (s32[64]{0:T(128)S(1)}, s32[64]{0:T(128)}, u32[]{:S(2)}) copy-start(s32[64]{0:T(128)} %get-tuple-element.80) | copy-start | bytes 772
  340.1 24.8 %copy-start.24 = (s32[64]{0:T(128)S(1)}, s32[64]{0:T(128)}, u32[]{:S(2)}) copy-start(s32[64]{0:T(128)} %get-tuple-element.79) | copy-start | bytes 772
  341.6 53.8 %collective-permute-start.18 = (bf16[40,7168]{1,0:T(8,128)(2,1)}, bf16[40,7168]{1,0:T(8,128)(2,1)S(1)}, u32[]{:S(2)}, u32[]{:S(2)}) collective-permute-start(bf16[40,7168]{1,0:T(8,128)(2,1)} %get-tuple-element.90), channel_id=1, source_target_pairs={{0,32},{1,33},{2,34},{3,35},{4,36},{5,37},{6,38},{7,39},{8,40},{9,... | collective-permute-start | bytes 1720328 | tf_op jit(solution)/shard_map/ppermute | solution.py:60
  341.6 53.7 %collective-permute-start.19 = (bf16[40,7168]{1,0:T(8,128)(2,1)}, bf16[40,7168]{1,0:T(8,128)(2,1)S(1)}, u32[]{:S(2)}, u32[]{:S(2)}) collective-permute-start(bf16[40,7168]{1,0:T(8,128)(2,1)} %get-tuple-element.89), channel_id=1, source_target_pairs={{8,32},{9,33},{10,34},{11,35},{28,36},{29,37},{30,38},{31,39},{16,... | collective-permute-start | bytes 1720328 | tf_op jit(solution)/shard_map/ppermute | solution.py:60
  347.7 47.7 %collective-permute-start.20 = (bf16[40,7168]{1,0:T(8,128)(2,1)}, bf16[40,7168]{1,0:T(8,128)(2,1)}, u32[]{:S(2)}, u32[]{:S(2)}) collective-permute-start(bf16[40,7168]{1,0:T(8,128)(2,1)} %get-tuple-element.88), channel_id=1, source_target_pairs={{28,32},{29,33},{30,34},{31,35},{8,36},{9,37},{10,38},{11,39},{4,4... | collective-permute-start | bytes 1720328 | tf_op jit(solution)/shard_map/ppermute | solution.py:60
  351.4 52.9 %collective-permute-start.21 = (bf16[40,7168]{1,0:T(8,128)(2,1)}, bf16[40,7168]{1,0:T(8,128)(2,1)}, u32[]{:S(2)}, u32[]{:S(2)}) collective-permute-start(bf16[40,7168]{1,0:T(8,128)(2,1)} %get-tuple-element.87), channel_id=1, source_target_pairs={{20,32},{21,33},{22,34},{23,35},{16,36},{17,37},{18,38},{19,39},{2... | collective-permute-start | bytes 1720328 | tf_op jit(solution)/shard_map/ppermute | solution.py:60
  353.5 60.3 %all-to-all-start = ((f32[32,4,224]{2,1,0:T(4,128)}), f32[32,4,224]{2,1,0:T(4,128)S(1)}, u32[]{:S(2)}, u32[]{:S(2)}) async-start(f32[32,4,224]{2,1,0:T(4,128)} %bitcast.50), calls=%async_computation | async-start | bytes 262144 | tf_op jit(solution)/shard_map/all_to_all | solution.py:34
  414.6 15.8 %all-to-all-start.1 = ((f32[32,4,224]{2,1,0:T(4,128)}), f32[32,4,224]{2,1,0:T(4,128)S(1)}, u32[]{:S(2)}, u32[]{:S(2)}) async-start(f32[32,4,224]{2,1,0:T(4,128)} %broadcast_in_dim.13), calls=%async_computation.1 | async-start | bytes 262144 | tf_op jit(solution)/shard_map/all_to_all | solution.py:34
  (3 other events, 2.4 us)

commit v5 on v3

--- a/solution.py
+++ b/solution.py
@@ -313,8 +313,8 @@
 
 
 def merged(keep, swapped):
-    total = (keep.astype(F32) + swapped.astype(F32)).astype(BF)
-    return [total[place * CAP : (place + 1) * CAP] for place in (0, 2, 1, 3)]
+    places = [slice(place * CAP, (place + 1) * CAP) for place in (0, 2, 1, 3)]
+    return [(keep[at].astype(F32) + swapped[at].astype(F32)).astype(BF) for at in places]
 
 
 def combine(picks, factors, returned, rows, extra, name):

time: 411 us -> 409 us (level)
  local copies, waits for them, and re-layouts: 31.4 us -> 22.5 us
  waiting for transfers between devices: 260 us -> 266 us
    ppermute x6, waiting for transfers between devices: 50.2 us -> 55.8 us  [to_source(): lax.ppermute(block, 'expert', [(b, a) for a, b in piece_route(piece)])]
    unnamed x56 -> x42, local copies, waits for them, and re-layouts: 17.2 us -> 13.1 us
  transfers between devices with their start and end apart: 23 -> 23, of which waited for: 11 -> 11; matrix products, arithmetic and copies ran while one was open for 5% -> 4% of each run, Pallas kernels for 6% -> 6%
where the time goes in v5:
time: 409 us; the launch traced here: 408 us
  waiting for transfers between devices  266 us (65%)
  starting transfers between devices  60.2 us (15%)
  Pallas kernels  41.7 us (10%)
  local copies, waits for them, and re-layouts  22.5 us (6%)
  other arithmetic  14.8 us (4%)
    ppermute x11, waiting for transfers between devices, exchanged(): return lax.ppermute(block, 'expert', route)  189 us
    ppermute x6, waiting for transfers between devices, to_source(): lax.ppermute(block, 'expert', [(b, a) for a, b in piece_route(piece)])  55.8 us
    all_to_all x2, waiting for transfers between devices, all_to_all(): lax.all_to_all(block, 'expert', split_axis=0, concat_axis=0, tiled=True)  20.2 us
    all_to_all x2, starting transfers between devices, all_to_all(): lax.all_to_all(block, 'expert', split_axis=0, concat_axis=0, tiled=True)  15.5 us
    ppermute x11, starting transfers between devices, exchanged(): return lax.ppermute(block, 'expert', route)  15.4 us
    ppermute x6, starting transfers between devices, to_source(): lax.ppermute(block, 'expert', [(b, a) for a, b in piece_route(piece)])  13.5 us
    unnamed x42, local copies, waits for them, and re-layouts  13.1 us
    pallas_call x1, Pallas kernels, backward_second(): pl.pallas_call(body, grid=(features // block,), in_specs=[pl.BlockSpec(a....  9.64 us
  transfers between devices with their start and end apart: 23, of which 11 were waited for; matrix products, arithmetic and copies ran while one was open for 4% of the time, Pallas kernels for 6%

profile of v5, /device:TPU:1, one launch (start us, length us, event | category | flops | bytes accessed | tf_op | source)
XLA Modules:
  0.0 408.3 jit_solution(5973630142029060926)
XLA Ops:
  0.7 4.3 %pad_maximum_fusion.refs_0_.refs_4_ = bf16[7168,256]{1,0:T(8,128)(2,1)} fusion(bf16[7168,128]{1,0:T(8,128)(2,1)} %bitcast.61, bf16[7168,128]{1,0:T(8,128)(2,1)} %bitcast.62), kind=kLoop, calls=%fused_computation.1 | loop fusion | flops 7340032 | bytes 7340032 | tf_op jit(solution)/shard_map/concatenate | solution.py:393
  5.0 2.5 collective-permute-start.2
  7.5 1.3 collective-permute-start.4
  11.3 1.2 copy.146
  12.5 1.2 copy-done.6
  13.6 1.2 copy-done.8
  14.8 3.4 pack.1
  18.2 5.4 %collective-permute-start = (bf16[80,16384]{1,0:T(8,128)(2,1)}, bf16[80,16384]{1,0:T(8,128)(2,1)S(1)}, u32[]{:S(2)}, u32[]{:S(2)}) collective-permute-start(bf16[80,16384]{1,0:T(8,128)(2,1)} %get-tuple-element.40), channel_id=1, source_target_pairs={{0,28},{1,29},{2,30},{3,31},{4,8},{5,9},{6,10},{7,11},{8,4},{9,5},... | collective-permute-start | bytes 7864328 | tf_op jit(solution)/shard_map/ppermute | solution.py:44
  23.8 103.2 %collective-permute-done.1.refs_9_.refs_1_ = bf16[128,7168]{1,0:T(8,128)(2,1)S(1)} collective-permute-done((bf16[128,7168]{1,0:T(8,128)(2,1)}, bf16[128,7168]{1,0:T(8,128)(2,1)S(1)}, u32[]{:S(2)}, u32[]{:S(2)}) %collective-permute-start.1) | collective-permute-done | bytes 1835040 | tf_op jit(solution)/shard_map/ppermute | solution.py:30
  127.2 1.1 copy-done.3
  128.5 3.1 collective-permute-start.5
  131.5 1.3 collective-permute-start.9
  133.0 2.4 collective-permute-start.6
  135.5 2.9 collective-permute-start.8
  138.5 1.0 slice.95
  139.8 80.6 %collective-permute-done.7 = bf16[32,7168]{1,0:T(8,128)(2,1)S(1)} collective-permute-done((bf16[32,7168]{1,0:T(8,128)(2,1)S(1)}, bf16[32,7168]{1,0:T(8,128)(2,1)S(1)}, u32[]{:S(2)}, u32[]{:S(2)}) %collective-permute-start.7) | collective-permute-done | bytes 458784 | tf_op jit(solution)/shard_map/ppermute | solution.py:30
  220.4 1.5 copy-done.12
  222.3 1.9 copy-done.13
  224.2 3.0 collective-permute-start.10
  227.2 1.6 constant_dynamic-update-slice_fusion.refs_11_.refs_3_
  228.7 3.3 collective-permute-done.10.refs_3_.refs_7_
  232.0 6.9 %backward_first.1 = (bf16[320,1024]{1,0:T(8,128)(2,1)S(1)}, f32[64,128]{1,0:T(8,128)S(1)}) custom-call(s32[1]{0:T(128)} %bitcast.12.chip_ref, bf16[80,16384]{1,0:T(8,128)(2,1)} %copy-done.1, bf16[80,16384]{1,0:T(8,128)(2,1)} %collective-permute-done.5.refs_1_.refs_5_, bf16[80,16384]{1,0:T(8,128)(2,1)} %copy-done.12, ...), custom_call_target="tpu_custom_call" | custom-call | tf_op jit(solution)/shard_map/backward_first/pallas_call | solution.py:187
  239.0 9.6 %backward_second.1 = (bf16[160,7168]{1,0:T(8,128)(2,1)S(1)}, bf16[160,7168]{1,0:T(8,128)(2,1)}) custom-call(bf16[320,1024]{1,0:T(8,128)(2,1)S(1)} %get-tuple-element.49.d_ref, f32[64,128]{1,0:T(8,128)S(1)} %get-tuple-element.50.inner_ref, bf16[7168,256]{1,0:T(8,128)(2,1)} %pad_maximum_fusion.refs_0_.refs_4_, ...), custom_call_target="tpu_custom_call" | custom-call | tf_op jit(solution)/shard_map/backward_second/pallas_call | solution.py:233
  248.6 1.4 copy-done.10
  251.7 1.5 fusion.31
  253.3 1.6 collective-permute-done.11
  254.8 4.0 add_convert_fusion.4
  258.8 2.2 collective-permute-start.12
  261.0 3.0 collective-permute-start.13
  264.5 9.5 %forward_first.1.hidden_ref = bf16[320,512]{1,0:T(8,128)(2,1)S(1)} custom-call(bf16[80,16384]{1,0:T(8,128)(2,1)S(1)} %copy-done.2, bf16[80,16384]{1,0:T(8,128)(2,1)} %collective-permute-done.5.refs_1_.refs_5_, bf16[80,16384]{1,0:T(8,128)(2,1)} %copy-done.12, bf16[80,16384]{1,0:T(8,128)(2,1)} %collective-permute-done.10.refs_3_.refs_7_, ...), custom_call_target="tpu_custom_call" | custom-call | tf_op jit(solution)/shard_map/forward_first/pallas_call | solution.py:277
  274.0 6.4 %forward_second.1 = (bf16[160,7168]{1,0:T(8,128)(2,1)}, bf16[160,7168]{1,0:T(8,128)(2,1)}) custom-call(bf16[320,512]{1,0:T(8,128)(2,1)S(1)} %forward_first.1.hidden_ref, bf16[128,7168]{1,0:T(8,128)(2,1)} %bitcast.9.refs_8_.refs_0_, bf16[128,7168]{1,0:T(8,128)(2,1)S(1)} %copy-done.5, bf16[128,7168]{1,0:T(8,128)(2,1)} %collective-permute-done.3.refs_10_.refs_2_, ...), custom_call_target="tpu_custom_call" | custom-call | tf_op jit(solution)/shard_map/forward_second/pallas_call | solution.py:303
  280.5 1.2 collective-permute-start.15
  282.0 7.7 %collective-permute-done.13.refs_5_ = bf16[40,7168]{1,0:T(8,128)(2,1)} collective-permute-done((bf16[40,7168]{1,0:T(8,128)(2,1)}, bf16[40,7168]{1,0:T(8,128)(2,1)}, u32[]{:S(2)}, u32[]{:S(2)}) %collective-permute-start.13) | collective-permute-done | bytes 573472 | tf_op jit(solution)/shard_map/ppermute | solution.py:50
  289.7 20.5 %collective-permute-done.14.refs_6_ = bf16[40,7168]{1,0:T(8,128)(2,1)} collective-permute-done((bf16[40,7168]{1,0:T(8,128)(2,1)}, bf16[40,7168]{1,0:T(8,128)(2,1)}, u32[]{:S(2)}, u32[]{:S(2)}) %collective-permute-start.14) | collective-permute-done | bytes 573472 | tf_op jit(solution)/shard_map/ppermute | solution.py:50
  313.0 3.8 add_convert_fusion
  316.8 4.7 %collective-permute-start.16 = (bf16[40,7168]{1,0:T(8,128)(2,1)}, bf16[40,7168]{1,0:T(8,128)(2,1)}, u32[]{:S(2)}, u32[]{:S(2)}) collective-permute-start(bf16[40,7168]{1,0:T(8,128)(2,1)} %get-tuple-element.79), channel_id=1, source_target_pairs={{8,0},{9,1},{10,2},{11,3},{28,4},{29,5},{30,6},{31,7},{16,8},{17,9... | collective-permute-start | bytes 1720328 | tf_op jit(solution)/shard_map/ppermute | solution.py:50
  321.5 3.0 collective-permute-start.17
  325.9 9.5 %all-to-all-start = ((f32[32,4,224]{2,1,0:T(4,128)}), f32[32,4,224]{2,1,0:T(4,128)S(1)}, u32[]{:S(2)}, u32[]{:S(2)}) async-start(f32[32,4,224]{2,1,0:T(4,128)} %bitcast.54), calls=%async_computation | async-start | bytes 262144 | tf_op jit(solution)/shard_map/all_to_all | solution.py:34
  335.6 3.6 combine_backward.1
  339.1 4.8 %collective-permute-start.20 = (bf16[64,7168]{1,0:T(8,128)(2,1)}, bf16[64,7168]{1,0:T(8,128)(2,1)}, u32[]{:S(2)}, u32[]{:S(2)}) collective-permute-start(bf16[64,7168]{1,0:T(8,128)(2,1)} %combine_backward.1), channel_id=1, source_target_pairs={{32,0},{64,32},{96,64},{128,96},{160,128},{192,160},{224,192},{0,2... | collective-permute-start | bytes 2752520 | tf_op jit(solution)/shard_map/ppermute | solution.py:25
  344.0 9.4 %collective-permute-done.17.refs_5_ = bf16[40,7168]{1,0:T(8,128)(2,1)} collective-permute-done((bf16[40,7168]{1,0:T(8,128)(2,1)}, bf16[40,7168]{1,0:T(8,128)(2,1)}, u32[]{:S(2)}, u32[]{:S(2)}) %collective-permute-start.17) | collective-permute-done | bytes 573472 | tf_op jit(solution)/shard_map/ppermute | solution.py:50
  353.4 18.2 %collective-permute-done.18.refs_6_ = bf16[40,7168]{1,0:T(8,128)(2,1)} collective-permute-done((bf16[40,7168]{1,0:T(8,128)(2,1)}, bf16[40,7168]{1,0:T(8,128)(2,1)}, u32[]{:S(2)}, u32[]{:S(2)}) %collective-permute-start.18) | collective-permute-done | bytes 573472 | tf_op jit(solution)/shard_map/ppermute | solution.py:50
  371.6 2.2 combine_forward.1
  373.8 5.0 %all-to-all-done = f32[32,4,224]{2,1,0:T(4,128)S(1)} async-done(((f32[32,4,224]{2,1,0:T(4,128)}), f32[32,4,224]{2,1,0:T(4,128)S(1)}, u32[]{:S(2)}, u32[]{:S(2)}) %all-to-all-start) | async-done | bytes 114720 | tf_op jit(solution)/shard_map/all_to_all | solution.py:34
  378.8 2.6 collective-permute-start.19
  382.1 6.0 %all-to-all-start.1 = ((f32[32,4,224]{2,1,0:T(4,128)}), f32[32,4,224]{2,1,0:T(4,128)S(1)}, u32[]{:S(2)}, u32[]{:S(2)}) async-start(f32[32,4,224]{2,1,0:T(4,128)} %broadcast_in_dim.13), calls=%async_computation.1 | async-start | bytes 262144 | tf_op jit(solution)/shard_map/all_to_all | solution.py:34
  388.1 15.2 %all-to-all-done.1 = f32[32,4,224]{2,1,0:T(4,128)S(1)} async-done(((f32[32,4,224]{2,1,0:T(4,128)}), f32[32,4,224]{2,1,0:T(4,128)S(1)}, u32[]{:S(2)}, u32[]{:S(2)}) %all-to-all-start.1) | async-done | bytes 114720 | tf_op jit(solution)/shard_map/all_to_all | solution.py:34
  406.1 2.2 copy.153
  (121 shorter events, 14.2 us)
Async XLA Ops:
  0.6 250.2 %copy-start = (bf16[1,64,7168]{2,1,0:T(8,128)(2,1)S(1)}, bf16[1,64,7168]{2,1,0:T(8,128)(2,1)}, u32[]{:S(2)}) copy-start(bf16[1,64,7168]{2,1,0:T(8,128)(2,1)} %param.12) | copy-start | bytes 2752516
  0.6 8.3 %copy-start.16 = (s32[1,64,2]{1,2,0:T(2,128)S(1)}, s32[1,64,2]{1,2,0:T(2,128)}, u32[]{:S(2)}) copy-start(s32[1,64,2]{1,2,0:T(2,128)} %param.13) | copy-start | bytes 1540
  0.7 9.2 %copy-start.17 = (s32[1,64,2]{1,2,0:T(2,128)S(1)}, s32[1,64,2]{1,2,0:T(2,128)}, u32[]{:S(2)}) copy-start(s32[1,64,2]{1,2,0:T(2,128)} %param.11) | copy-start | bytes 1540
  5.0 122.0 %collective-permute-start.2 = (bf16[7168,256]{1,0:T(8,128)(2,1)}, bf16[7168,256]{1,0:T(8,128)(2,1)}, u32[]{:S(2)}, u32[]{:S(2)}) collective-permute-start(bf16[7168,256]{1,0:T(8,128)(2,1)} %pad_maximum_fusion.refs_0_.refs_4_), channel_id=1, source_target_pairs={{0,4},{1,5},{2,6},{3,7},{4,0},{5,1},{6,2},{7,3},{8,12},{9,13},{10,... | collective-permute-start | bytes 11010056 | tf_op jit(solution)/shard_map/ppermute | solution.py:30
  7.5 119.6 %collective-permute-start.4 = (bf16[7168,256]{1,0:T(8,128)(2,1)}, bf16[7168,256]{1,0:T(8,128)(2,1)}, u32[]{:S(2)}, u32[]{:S(2)}) collective-permute-start(bf16[7168,256]{1,0:T(8,128)(2,1)} %pad_maximum_fusion.refs_0_.refs_4_), channel_id=1, source_target_pairs={{0,2},{1,3},{2,0},{3,1},{4,6},{5,7},{6,4},{7,5},{8,10},{9,11},{10,... | collective-permute-start | bytes 11010056 | tf_op jit(solution)/shard_map/ppermute | solution.py:30
  8.8 118.2 %collective-permute-start.1 = (bf16[128,7168]{1,0:T(8,128)(2,1)}, bf16[128,7168]{1,0:T(8,128)(2,1)S(1)}, u32[]{:S(2)}, u32[]{:S(2)}) collective-permute-start(bf16[128,7168]{1,0:T(8,128)(2,1)} %bitcast.9.refs_8_.refs_0_), channel_id=1, source_target_pairs={{0,2},{1,3},{2,0},{3,1},{4,6},{5,7},{6,4},{7,5},{8,10},{9,11},{10,... | collective-permute-start | bytes 5505032 | tf_op jit(solution)/shard_map/ppermute | solution.py:30
  8.9 118.1 %collective-permute-start.3 = (bf16[128,7168]{1,0:T(8,128)(2,1)}, bf16[128,7168]{1,0:T(8,128)(2,1)}, u32[]{:S(2)}, u32[]{:S(2)}) collective-permute-start(bf16[128,7168]{1,0:T(8,128)(2,1)} %bitcast.9.refs_8_.refs_0_), channel_id=1, source_target_pairs={{0,4},{1,5},{2,6},{3,7},{4,0},{5,1},{6,2},{7,3},{8,12},{9,13},{10,... | collective-permute-start | bytes 5505032 | tf_op jit(solution)/shard_map/ppermute | solution.py:30
  12.5 1.2 copy-start.6
  13.6 1.2 copy-start.8
  18.2 108.8 %collective-permute-start = (bf16[80,16384]{1,0:T(8,128)(2,1)}, bf16[80,16384]{1,0:T(8,128)(2,1)S(1)}, u32[]{:S(2)}, u32[]{:S(2)}) collective-permute-start(bf16[80,16384]{1,0:T(8,128)(2,1)} %get-tuple-element.40), channel_id=1, source_target_pairs={{0,28},{1,29},{2,30},{3,31},{4,8},{5,9},{6,10},{7,11},{8,4},{9,5},... | collective-permute-start | bytes 7864328 | tf_op jit(solution)/shard_map/ppermute | solution.py:44
  127.0 1.3 copy-start.3
  128.5 91.9 %collective-permute-start.5 = (bf16[80,16384]{1,0:T(8,128)(2,1)S(1)}, bf16[80,16384]{1,0:T(8,128)(2,1)}, u32[]{:S(2)}, u32[]{:S(2)}) collective-permute-start(bf16[80,16384]{1,0:T(8,128)(2,1)S(1)} %pad_maximum_fusion.2), channel_id=1, source_target_pairs={{0,8},{1,9},{2,10},{3,11},{4,28},{5,29},{6,30},{7,31},{8,16},{9,17... | collective-permute-start | bytes 7864328 | tf_op jit(solution)/shard_map/ppermute | solution.py:44
  131.5 90.4 %collective-permute-start.9 = (bf16[7168,256]{1,0:T(8,128)(2,1)}, bf16[7168,256]{1,0:T(8,128)(2,1)S(1)}, u32[]{:S(2)}, u32[]{:S(2)}) collective-permute-start(bf16[7168,256]{1,0:T(8,128)(2,1)} %collective-permute-done.2.refs_2_.refs_6_), channel_id=1, source_target_pairs={{0,2},{1,3},{2,0},{3,1},{4,6},{5,7},{6,4},{7,5},{8,10},{9,11},{10,... | collective-permute-start | bytes 11010056 | tf_op jit(solution)/shard_map/ppermute | solution.py:30
  132.8 2.6 copy-start.4
  133.0 6.5 %copy-start.1 = (bf16[80,16384]{1,0:T(8,128)(2,1)}, bf16[80,16384]{1,0:T(8,128)(2,1)S(1)}, u32[]{:S(2)}) copy-start(bf16[80,16384]{1,0:T(8,128)(2,1)S(1)} %pad_maximum_fusion.1.refs_0_.refs_4_) | copy-start | bytes 7864324
  133.0 87.3 %collective-permute-start.6 = (bf16[80,16384]{1,0:T(8,128)(2,1)S(1)}, bf16[80,16384]{1,0:T(8,128)(2,1)S(1)}, u32[]{:S(2)}, u32[]{:S(2)}) collective-permute-start(bf16[80,16384]{1,0:T(8,128)(2,1)S(1)} %pad_maximum_fusion.1.refs_0_.refs_4_), channel_id=1, source_target_pairs={{0,1},{1,0},{2,3},{3,2},{4,5},{5,4},{6,7},{7,6},{8,9},{9,8},{10,11... | collective-permute-start | bytes 7864328 | tf_op jit(solution)/shard_map/ppermute | solution.py:30
  135.5 84.8 %collective-permute-start.8 = (bf16[96,7168]{1,0:T(8,128)(2,1)S(1)}, bf16[96,7168]{1,0:T(8,128)(2,1)S(1)}, u32[]{:S(2)}, u32[]{:S(2)}) collective-permute-start(bf16[96,7168]{1,0:T(8,128)(2,1)S(1)} %slice.96), channel_id=1, source_target_pairs={{0,4},{1,5},{2,6},{3,7},{4,0},{5,1},{6,2},{7,3},{8,12},{9,13},{10,... | collective-permute-start | bytes 4128776 | tf_op jit(solution)/shard_map/ppermute | solution.py:30
  139.5 80.8 %collective-permute-start.7 = (bf16[32,7168]{1,0:T(8,128)(2,1)S(1)}, bf16[32,7168]{1,0:T(8,128)(2,1)S(1)}, u32[]{:S(2)}, u32[]{:S(2)}) collective-permute-start(bf16[32,7168]{1,0:T(8,128)(2,1)S(1)} %slice.95), channel_id=1, source_target_pairs={{0,2},{1,3},{2,0},{3,1},{4,6},{5,7},{6,4},{7,5},{8,10},{9,11},{10,... | collective-permute-start | bytes 1376264 | tf_op jit(solution)/shard_map/ppermute | solution.py:30
  220.4 1.9 copy-start.15
  220.4 1.5 copy-start.12
  222.3 1.9 copy-start.13
  224.2 7.8 %collective-permute-start.10 = (bf16[80,16384]{1,0:T(8,128)(2,1)}, bf16[80,16384]{1,0:T(8,128)(2,1)}, u32[]{:S(2)}, u32[]{:S(2)}) collective-permute-start(bf16[80,16384]{1,0:T(8,128)(2,1)} %collective-permute-done.5.refs_1_.refs_5_), channel_id=1, source_target_pairs={{0,1},{1,0},{2,3},{3,2},{4,5},{5,4},{6,7},{7,6},{8,9},{9,8},{10,11... | collective-permute-start | bytes 7864328 | tf_op jit(solution)/shard_map/ppermute | solution.py:30
  227.1 4.9 %copy-start.5 = (bf16[128,7168]{1,0:T(8,128)(2,1)S(1)}, bf16[128,7168]{1,0:T(8,128)(2,1)}, u32[]{:S(2)}) copy-start(bf16[128,7168]{1,0:T(8,128)(2,1)} %copy-done.3) | copy-start | bytes 5505028
  228.7 3.3 copy-start.14
  238.9 11.9 %copy-start.11 = (bf16[1,4,7168]{2,1,0:T(4,128)(2,1)S(1)}, bf16[1,4,7168]{2,1,0:T(4,128)(2,1)}, u32[]{:S(2)}) copy-start(bf16[1,4,7168]{2,1,0:T(4,128)(2,1)} %param.16) | copy-start | bytes 172036
  248.6 1.4 copy-start.10
  250.0 4.8 %collective-permute-start.11 = (bf16[160,7168]{1,0:T(8,128)(2,1)}, bf16[160,7168]{1,0:T(8,128)(2,1)}, u32[]{:S(2)}, u32[]{:S(2)}) collective-permute-start(bf16[160,7168]{1,0:T(8,128)(2,1)} %get-tuple-element.54), channel_id=1, source_target_pairs={{0,1},{1,0},{2,3},{3,2},{4,5},{5,4},{6,7},{7,6},{8,9},{9,8},{10,11... | collective-permute-start | bytes 6881288 | tf_op jit(solution)/shard_map/ppermute | solution.py:30
  254.8 9.7 %copy-start.2 = (bf16[80,16384]{1,0:T(8,128)(2,1)S(1)}, bf16[80,16384]{1,0:T(8,128)(2,1)}, u32[]{:S(2)}) copy-start(bf16[80,16384]{1,0:T(8,128)(2,1)} %copy-done.1) | copy-start | bytes 7864324
  258.8 23.2 %collective-permute-start.12 = (bf16[40,7168]{1,0:T(8,128)(2,1)}, bf16[40,7168]{1,0:T(8,128)(2,1)}, u32[]{:S(2)}, u32[]{:S(2)}) collective-permute-start(bf16[40,7168]{1,0:T(8,128)(2,1)} %get-tuple-element.56), channel_id=1, source_target_pairs={{8,0},{9,1},{10,2},{11,3},{28,4},{29,5},{30,6},{31,7},{16,8},{17,9... | collective-permute-start | bytes 1720328 | tf_op jit(solution)/shard_map/ppermute | solution.py:50
  261.0 28.7 %collective-permute-start.13 = (bf16[40,7168]{1,0:T(8,128)(2,1)}, bf16[40,7168]{1,0:T(8,128)(2,1)}, u32[]{:S(2)}, u32[]{:S(2)}) collective-permute-start(bf16[40,7168]{1,0:T(8,128)(2,1)} %get-tuple-element.57), channel_id=1, source_target_pairs={{28,0},{29,1},{30,2},{31,3},{8,4},{9,5},{10,6},{11,7},{4,8},{5,9},... | collective-permute-start | bytes 1720328 | tf_op jit(solution)/shard_map/ppermute | solution.py:50
  264.0 46.2 %collective-permute-start.14 = (bf16[40,7168]{1,0:T(8,128)(2,1)}, bf16[40,7168]{1,0:T(8,128)(2,1)}, u32[]{:S(2)}, u32[]{:S(2)}) collective-permute-start(bf16[40,7168]{1,0:T(8,128)(2,1)} %get-tuple-element.58), channel_id=1, source_target_pairs={{20,0},{21,1},{22,2},{23,3},{16,4},{17,5},{18,6},{19,7},{28,8},{29... | collective-permute-start | bytes 1720328 | tf_op jit(solution)/shard_map/ppermute | solution.py:50
  280.5 32.5 %collective-permute-start.15 = (bf16[160,7168]{1,0:T(8,128)(2,1)}, bf16[160,7168]{1,0:T(8,128)(2,1)}, u32[]{:S(2)}, u32[]{:S(2)}) collective-permute-start(bf16[160,7168]{1,0:T(8,128)(2,1)} %get-tuple-element.68), channel_id=1, source_target_pairs={{0,1},{1,0},{2,3},{3,2},{4,5},{5,4},{6,7},{7,6},{8,9},{9,8},{10,11... | collective-permute-start | bytes 6881288 | tf_op jit(solution)/shard_map/ppermute | solution.py:30
  316.8 18.8 %copy-start.7 = (bf16[1,64,7168]{2,1,0:T(8,128)(2,1)S(1)}, bf16[1,64,7168]{2,1,0:T(8,128)(2,1)}, u32[]{:S(2)}) copy-start(bf16[1,64,7168]{2,1,0:T(8,128)(2,1)} %param.14) | copy-start | bytes 2752516
  316.8 27.2 %collective-permute-start.16 = (bf16[40,7168]{1,0:T(8,128)(2,1)}, bf16[40,7168]{1,0:T(8,128)(2,1)}, u32[]{:S(2)}, u32[]{:S(2)}) collective-permute-start(bf16[40,7168]{1,0:T(8,128)(2,1)} %get-tuple-element.79), channel_id=1, source_target_pairs={{8,0},{9,1},{10,2},{11,3},{28,4},{29,5},{30,6},{31,7},{16,8},{17,9... | collective-permute-start | bytes 1720328 | tf_op jit(solution)/shard_map/ppermute | solution.py:50
  321.5 31.8 %collective-permute-start.17 = (bf16[40,7168]{1,0:T(8,128)(2,1)}, bf16[40,7168]{1,0:T(8,128)(2,1)}, u32[]{:S(2)}, u32[]{:S(2)}) collective-permute-start(bf16[40,7168]{1,0:T(8,128)(2,1)} %get-tuple-element.78), channel_id=1, source_target_pairs={{28,0},{29,1},{30,2},{31,3},{8,4},{9,5},{10,6},{11,7},{4,8},{5,9},... | collective-permute-start | bytes 1720328 | tf_op jit(solution)/shard_map/ppermute | solution.py:50
  324.6 47.0 %collective-permute-start.18 = (bf16[40,7168]{1,0:T(8,128)(2,1)}, bf16[40,7168]{1,0:T(8,128)(2,1)}, u32[]{:S(2)}, u32[]{:S(2)}) collective-permute-start(bf16[40,7168]{1,0:T(8,128)(2,1)} %get-tuple-element.77), channel_id=1, source_target_pairs={{20,0},{21,1},{22,2},{23,3},{16,4},{17,5},{18,6},{19,7},{28,8},{29... | collective-permute-start | bytes 1720328 | tf_op jit(solution)/shard_map/ppermute | solution.py:50
  325.9 52.8 %all-to-all-start = ((f32[32,4,224]{2,1,0:T(4,128)}), f32[32,4,224]{2,1,0:T(4,128)S(1)}, u32[]{:S(2)}, u32[]{:S(2)}) async-start(f32[32,4,224]{2,1,0:T(4,128)} %bitcast.54), calls=%async_computation | async-start | bytes 262144 | tf_op jit(solution)/shard_map/all_to_all | solution.py:34
  335.6 36.0 %copy-start.9 = (bf16[1,64,7168]{2,1,0:T(8,128)(2,1)S(1)}, bf16[1,64,7168]{2,1,0:T(8,128)(2,1)}, u32[]{:S(2)}) copy-start(bf16[1,64,7168]{2,1,0:T(8,128)(2,1)} %param.10) | copy-start | bytes 2752516
  339.1 49.0 %collective-permute-start.20 = (bf16[64,7168]{1,0:T(8,128)(2,1)}, bf16[64,7168]{1,0:T(8,128)(2,1)}, u32[]{:S(2)}, u32[]{:S(2)}) collective-permute-start(bf16[64,7168]{1,0:T(8,128)(2,1)} %combine_backward.1), channel_id=1, source_target_pairs={{32,0},{64,32},{96,64},{128,96},{160,128},{192,160},{224,192},{0,2... | collective-permute-start | bytes 2752520 | tf_op jit(solution)/shard_map/ppermute | solution.py:25
  378.8 26.4 %collective-permute-start.19 = (bf16[64,7168]{1,0:T(8,128)(2,1)S(1)}, bf16[64,7168]{1,0:T(8,128)(2,1)S(1)}, u32[]{:S(2)}, u32[]{:S(2)}) collective-permute-start(bf16[64,7168]{1,0:T(8,128)(2,1)S(1)} %combine_forward.1), channel_id=1, source_target_pairs={{224,0},{0,32},{32,64},{64,96},{96,128},{128,160},{160,192},{192,2... | collective-permute-start | bytes 2752520 | tf_op jit(solution)/shard_map/ppermute | solution.py:25
  382.1 21.2 %all-to-all-start.1 = ((f32[32,4,224]{2,1,0:T(4,128)}), f32[32,4,224]{2,1,0:T(4,128)S(1)}, u32[]{:S(2)}, u32[]{:S(2)}) async-start(f32[32,4,224]{2,1,0:T(4,128)} %broadcast_in_dim.13), calls=%async_computation.1 | async-start | bytes 262144 | tf_op jit(solution)/shard_map/all_to_all | solution.py:34

commit v6 on v5

--- a/solution.py
+++ b/solution.py
@@ -411,7 +411,7 @@
     own_1 = jnp.concatenate([near[:CAP], first[:CAP]], axis=0)
     own_2 = hopped(jnp.concatenate([near[CAP:], first[CAP:]], axis=0), 1)
     other_1 = exchanged(own_1, 1)
-    cut = hidden // 3 // 16 * 16
+    cut = hidden // 8
     down_d = [exchanged(down_z[:cut], 2), exchanged(down_y[cut:], 4)]
     joined_d = exchanged(joined_z, 2)
     own_2, other_1, down_d, joined_d = lax.optimization_barrier((own_2, other_1, down_d, joined_d))

time: 409 us -> 409 us (level)
  starting transfers between devices: 60.2 us -> 56 us
    ppermute x6, starting transfers between devices: 13.5 us -> 8.42 us  [to_source(): lax.ppermute(block, 'expert', [(b, a) for a, b in piece_route(piece)])]
    ppermute x6, waiting for transfers between devices: 55.8 us -> 60.6 us  [to_source(): lax.ppermute(block, 'expert', [(b, a) for a, b in piece_route(piece)])]
    all_to_all x2, waiting for transfers between devices: 20.2 us -> 15.7 us  [all_to_all(): lax.all_to_all(block, 'expert', split_axis=0, concat_axis=0, tiled=True)]
  transfers between devices with their start and end apart: 23 -> 23, of which waited for: 11 -> 12; matrix products, arithmetic and copies ran while one was open for 4% -> 4% of each run, Pallas kernels for 6% -> 6%
where the time goes in v6:
time: 409 us; the launch traced here: 408 us
  waiting for transfers between devices  269 us (66%)
  starting transfers between devices  56 us (14%)
  Pallas kernels  41.7 us (10%)
  local copies, waits for them, and re-layouts  22.6 us (6%)
  other arithmetic  14.8 us (4%)
    ppermute x11, waiting for transfers between devices, exchanged(): return lax.ppermute(block, 'expert', route)  192 us
    ppermute x6, waiting for transfers between devices, to_source(): lax.ppermute(block, 'expert', [(b, a) for a, b in piece_route(piece)])  60.6 us
    all_to_all x2, starting transfers between devices, all_to_all(): lax.all_to_all(block, 'expert', split_axis=0, concat_axis=0, tiled=True)  16.6 us
    all_to_all x2, waiting for transfers between devices, all_to_all(): lax.all_to_all(block, 'expert', split_axis=0, concat_axis=0, tiled=True)  15.7 us
    ppermute x11, starting transfers between devices, exchanged(): return lax.ppermute(block, 'expert', route)  15.1 us
    unnamed x42, local copies, waits for them, and re-layouts  13.2 us
    pallas_call x1, Pallas kernels, backward_second(): pl.pallas_call(body, grid=(features // block,), in_specs=[pl.BlockSpec(a....  9.63 us
    pallas_call x1, Pallas kernels, forward_first(): pl.pallas_call(body, grid=(steps,), in_specs=[pl.BlockSpec((rows, block),...  9.53 us
  transfers between devices with their start and end apart: 23, of which 12 were waited for; matrix products, arithmetic and copies ran while one was open for 4% of the time, Pallas kernels for 6%

profile of v6, /device:TPU:1, one launch (start us, length us, event | category | flops | bytes accessed | tf_op | source)
XLA Modules:
  0.0 408.1 jit_solution(1674464566536762964)
XLA Ops:
  0.7 4.3 %pad_maximum_fusion.refs_0_.refs_4_ = bf16[7168,256]{1,0:T(8,128)(2,1)} fusion(bf16[7168,128]{1,0:T(8,128)(2,1)} %bitcast.61, bf16[7168,128]{1,0:T(8,128)(2,1)} %bitcast.62), kind=kLoop, calls=%fused_computation.1 | loop fusion | flops 7340032 | bytes 7340032 | tf_op jit(solution)/shard_map/concatenate | solution.py:393
  5.0 2.5 collective-permute-start.2
  7.5 1.3 collective-permute-start.4
  11.3 1.2 copy.146
  12.5 1.2 copy-done.6
  13.6 1.2 copy-done.8
  14.8 3.4 pack.1
  18.2 5.4 %collective-permute-start = (bf16[80,16384]{1,0:T(8,128)(2,1)}, bf16[80,16384]{1,0:T(8,128)(2,1)S(1)}, u32[]{:S(2)}, u32[]{:S(2)}) collective-permute-start(bf16[80,16384]{1,0:T(8,128)(2,1)} %get-tuple-element.40), channel_id=1, source_target_pairs={{0,28},{1,29},{2,30},{3,31},{4,8},{5,9},{6,10},{7,11},{8,4},{9,5},... | collective-permute-start | bytes 7864328 | tf_op jit(solution)/shard_map/ppermute | solution.py:44
  23.8 103.2 %collective-permute-done.1.refs_9_.refs_1_ = bf16[128,7168]{1,0:T(8,128)(2,1)S(1)} collective-permute-done((bf16[128,7168]{1,0:T(8,128)(2,1)}, bf16[128,7168]{1,0:T(8,128)(2,1)S(1)}, u32[]{:S(2)}, u32[]{:S(2)}) %collective-permute-start.1) | collective-permute-done | bytes 1835040 | tf_op jit(solution)/shard_map/ppermute | solution.py:30
  127.2 1.1 copy-done.3
  128.5 3.1 collective-permute-start.5
  131.5 1.3 collective-permute-start.9
  133.0 2.4 collective-permute-start.6
  135.5 2.9 collective-permute-start.8
  138.5 1.0 slice.95
  139.7 75.7 %collective-permute-done.7 = bf16[16,7168]{1,0:T(8,128)(2,1)S(1)} collective-permute-done((bf16[16,7168]{1,0:T(8,128)(2,1)S(1)}, bf16[16,7168]{1,0:T(8,128)(2,1)S(1)}, u32[]{:S(2)}, u32[]{:S(2)}) %collective-permute-start.7) | collective-permute-done | bytes 229408 | tf_op jit(solution)/shard_map/ppermute | solution.py:30
  215.4 8.5 %collective-permute-done.8 = bf16[112,7168]{1,0:T(8,128)(2,1)S(1)} collective-permute-done((bf16[112,7168]{1,0:T(8,128)(2,1)S(1)}, bf16[112,7168]{1,0:T(8,128)(2,1)S(1)}, u32[]{:S(2)}, u32[]{:S(2)}) %collective-permute-start.8) | collective-permute-done | bytes 1605664 | tf_op jit(solution)/shard_map/ppermute | solution.py:30
  223.9 1.5 copy-done.12
  225.9 1.9 copy-done.13
  227.8 2.7 collective-permute-start.10
  230.5 1.7 constant_dynamic-update-slice_fusion.refs_11_.refs_3_
  232.2 3.2 collective-permute-done.10.refs_3_.refs_7_
  235.4 6.9 %backward_first.1 = (bf16[320,1024]{1,0:T(8,128)(2,1)S(1)}, f32[64,128]{1,0:T(8,128)S(1)}) custom-call(s32[1]{0:T(128)} %bitcast.12.chip_ref, bf16[80,16384]{1,0:T(8,128)(2,1)} %copy-done.1, bf16[80,16384]{1,0:T(8,128)(2,1)} %collective-permute-done.5.refs_1_.refs_5_, bf16[80,16384]{1,0:T(8,128)(2,1)} %copy-done.12, ...), custom_call_target="tpu_custom_call" | custom-call | tf_op jit(solution)/shard_map/backward_first/pallas_call | solution.py:187
  242.3 9.6 %backward_second.1 = (bf16[160,7168]{1,0:T(8,128)(2,1)S(1)}, bf16[160,7168]{1,0:T(8,128)(2,1)}) custom-call(bf16[320,1024]{1,0:T(8,128)(2,1)S(1)} %get-tuple-element.49.d_ref, f32[64,128]{1,0:T(8,128)S(1)} %get-tuple-element.50.inner_ref, bf16[7168,256]{1,0:T(8,128)(2,1)} %pad_maximum_fusion.refs_0_.refs_4_, ...), custom_call_target="tpu_custom_call" | custom-call | tf_op jit(solution)/shard_map/backward_second/pallas_call | solution.py:233
  252.0 1.4 copy-done.10
  255.1 1.5 fusion.31
  256.6 1.5 collective-permute-done.11
  258.2 4.0 add_convert_fusion.4
  262.1 1.2 collective-permute-start.12
  264.5 9.5 %forward_first.1.hidden_ref = bf16[320,512]{1,0:T(8,128)(2,1)S(1)} custom-call(bf16[80,16384]{1,0:T(8,128)(2,1)S(1)} %copy-done.2, bf16[80,16384]{1,0:T(8,128)(2,1)} %collective-permute-done.5.refs_1_.refs_5_, bf16[80,16384]{1,0:T(8,128)(2,1)} %copy-done.12, bf16[80,16384]{1,0:T(8,128)(2,1)} %collective-permute-done.10.refs_3_.refs_7_, ...), custom_call_target="tpu_custom_call" | custom-call | tf_op jit(solution)/shard_map/forward_first/pallas_call | solution.py:277
  274.1 6.4 %forward_second.1 = (bf16[160,7168]{1,0:T(8,128)(2,1)}, bf16[160,7168]{1,0:T(8,128)(2,1)}) custom-call(bf16[320,512]{1,0:T(8,128)(2,1)S(1)} %forward_first.1.hidden_ref, bf16[128,7168]{1,0:T(8,128)(2,1)} %bitcast.9.refs_8_.refs_0_, bf16[128,7168]{1,0:T(8,128)(2,1)S(1)} %copy-done.5, bf16[128,7168]{1,0:T(8,128)(2,1)} %collective-permute-done.3.refs_10_.refs_2_, ...), custom_call_target="tpu_custom_call" | custom-call | tf_op jit(solution)/shard_map/forward_second/pallas_call | solution.py:303
  280.5 1.2 collective-permute-start.15
  282.1 7.1 %collective-permute-done.13.refs_5_ = bf16[40,7168]{1,0:T(8,128)(2,1)} collective-permute-done((bf16[40,7168]{1,0:T(8,128)(2,1)}, bf16[40,7168]{1,0:T(8,128)(2,1)}, u32[]{:S(2)}, u32[]{:S(2)}) %collective-permute-start.13) | collective-permute-done | bytes 573472 | tf_op jit(solution)/shard_map/ppermute | solution.py:50
  289.2 23.3 %collective-permute-done.14.refs_6_ = bf16[40,7168]{1,0:T(8,128)(2,1)} collective-permute-done((bf16[40,7168]{1,0:T(8,128)(2,1)}, bf16[40,7168]{1,0:T(8,128)(2,1)}, u32[]{:S(2)}, u32[]{:S(2)}) %collective-permute-start.14) | collective-permute-done | bytes 573472 | tf_op jit(solution)/shard_map/ppermute | solution.py:50
  315.3 3.8 add_convert_fusion
  319.1 4.8 %collective-permute-start.16 = (bf16[40,7168]{1,0:T(8,128)(2,1)}, bf16[40,7168]{1,0:T(8,128)(2,1)}, u32[]{:S(2)}, u32[]{:S(2)}) collective-permute-start(bf16[40,7168]{1,0:T(8,128)(2,1)} %get-tuple-element.79), channel_id=1, source_target_pairs={{8,0},{9,1},{10,2},{11,3},{28,4},{29,5},{30,6},{31,7},{16,8},{17,9... | collective-permute-start | bytes 1720328 | tf_op jit(solution)/shard_map/ppermute | solution.py:50
  326.5 8.6 %all-to-all-start = ((f32[32,4,224]{2,1,0:T(4,128)}), f32[32,4,224]{2,1,0:T(4,128)S(1)}, u32[]{:S(2)}, u32[]{:S(2)}) async-start(f32[32,4,224]{2,1,0:T(4,128)} %bitcast.54), calls=%async_computation | async-start | bytes 262144 | tf_op jit(solution)/shard_map/all_to_all | solution.py:34
  335.4 3.6 combine_backward.1
  338.9 4.8 %collective-permute-start.20 = (bf16[64,7168]{1,0:T(8,128)(2,1)}, bf16[64,7168]{1,0:T(8,128)(2,1)}, u32[]{:S(2)}, u32[]{:S(2)}) collective-permute-start(bf16[64,7168]{1,0:T(8,128)(2,1)} %combine_backward.1), channel_id=1, source_target_pairs={{32,0},{64,32},{96,64},{128,96},{160,128},{192,160},{224,192},{0,2... | collective-permute-start | bytes 2752520 | tf_op jit(solution)/shard_map/ppermute | solution.py:25
  343.8 6.4 %collective-permute-done.17.refs_5_ = bf16[40,7168]{1,0:T(8,128)(2,1)} collective-permute-done((bf16[40,7168]{1,0:T(8,128)(2,1)}, bf16[40,7168]{1,0:T(8,128)(2,1)}, u32[]{:S(2)}, u32[]{:S(2)}) %collective-permute-start.17) | collective-permute-done | bytes 573472 | tf_op jit(solution)/shard_map/ppermute | solution.py:50
  350.2 23.7 %collective-permute-done.18.refs_6_ = bf16[40,7168]{1,0:T(8,128)(2,1)} collective-permute-done((bf16[40,7168]{1,0:T(8,128)(2,1)}, bf16[40,7168]{1,0:T(8,128)(2,1)}, u32[]{:S(2)}, u32[]{:S(2)}) %collective-permute-start.18) | collective-permute-done | bytes 573472 | tf_op jit(solution)/shard_map/ppermute | solution.py:50
  373.9 2.2 combine_forward.1
  376.1 2.4 all-to-all-done
  378.6 2.6 collective-permute-start.19
  381.9 8.0 %all-to-all-start.1 = ((f32[32,4,224]{2,1,0:T(4,128)}), f32[32,4,224]{2,1,0:T(4,128)S(1)}, u32[]{:S(2)}, u32[]{:S(2)}) async-start(f32[32,4,224]{2,1,0:T(4,128)} %broadcast_in_dim.13), calls=%async_computation.1 | async-start | bytes 262144 | tf_op jit(solution)/shard_map/all_to_all | solution.py:34
  389.9 13.3 %all-to-all-done.1 = f32[32,4,224]{2,1,0:T(4,128)S(1)} async-done(((f32[32,4,224]{2,1,0:T(4,128)}), f32[32,4,224]{2,1,0:T(4,128)S(1)}, u32[]{:S(2)}, u32[]{:S(2)}) %all-to-all-start.1) | async-done | bytes 114720 | tf_op jit(solution)/shard_map/all_to_all | solution.py:34
  404.0 1.0 collective-permute-done.19
  405.9 2.2 copy.153
  (121 shorter events, 15.3 us)
Async XLA Ops:
  0.6 253.5 %copy-start = (bf16[1,64,7168]{2,1,0:T(8,128)(2,1)S(1)}, bf16[1,64,7168]{2,1,0:T(8,128)(2,1)}, u32[]{:S(2)}) copy-start(bf16[1,64,7168]{2,1,0:T(8,128)(2,1)} %param.12) | copy-start | bytes 2752516
  0.6 8.3 %copy-start.16 = (s32[1,64,2]{1,2,0:T(2,128)S(1)}, s32[1,64,2]{1,2,0:T(2,128)}, u32[]{:S(2)}) copy-start(s32[1,64,2]{1,2,0:T(2,128)} %param.13) | copy-start | bytes 1540
  0.7 9.2 %copy-start.17 = (s32[1,64,2]{1,2,0:T(2,128)S(1)}, s32[1,64,2]{1,2,0:T(2,128)}, u32[]{:S(2)}) copy-start(s32[1,64,2]{1,2,0:T(2,128)} %param.11) | copy-start | bytes 1540
  5.0 122.0 %collective-permute-start.2 = (bf16[7168,256]{1,0:T(8,128)(2,1)}, bf16[7168,256]{1,0:T(8,128)(2,1)}, u32[]{:S(2)}, u32[]{:S(2)}) collective-permute-start(bf16[7168,256]{1,0:T(8,128)(2,1)} %pad_maximum_fusion.refs_0_.refs_4_), channel_id=1, source_target_pairs={{0,4},{1,5},{2,6},{3,7},{4,0},{5,1},{6,2},{7,3},{8,12},{9,13},{10,... | collective-permute-start | bytes 11010056 | tf_op jit(solution)/shard_map/ppermute | solution.py:30
  7.5 119.6 %collective-permute-start.4 = (bf16[7168,256]{1,0:T(8,128)(2,1)}, bf16[7168,256]{1,0:T(8,128)(2,1)}, u32[]{:S(2)}, u32[]{:S(2)}) collective-permute-start(bf16[7168,256]{1,0:T(8,128)(2,1)} %pad_maximum_fusion.refs_0_.refs_4_), channel_id=1, source_target_pairs={{0,2},{1,3},{2,0},{3,1},{4,6},{5,7},{6,4},{7,5},{8,10},{9,11},{10,... | collective-permute-start | bytes 11010056 | tf_op jit(solution)/shard_map/ppermute | solution.py:30
  8.8 118.2 %collective-permute-start.1 = (bf16[128,7168]{1,0:T(8,128)(2,1)}, bf16[128,7168]{1,0:T(8,128)(2,1)S(1)}, u32[]{:S(2)}, u32[]{:S(2)}) collective-permute-start(bf16[128,7168]{1,0:T(8,128)(2,1)} %bitcast.9.refs_8_.refs_0_), channel_id=1, source_target_pairs={{0,2},{1,3},{2,0},{3,1},{4,6},{5,7},{6,4},{7,5},{8,10},{9,11},{10,... | collective-permute-start | bytes 5505032 | tf_op jit(solution)/shard_map/ppermute | solution.py:30
  8.9 118.1 %collective-permute-start.3 = (bf16[128,7168]{1,0:T(8,128)(2,1)}, bf16[128,7168]{1,0:T(8,128)(2,1)}, u32[]{:S(2)}, u32[]{:S(2)}) collective-permute-start(bf16[128,7168]{1,0:T(8,128)(2,1)} %bitcast.9.refs_8_.refs_0_), channel_id=1, source_target_pairs={{0,4},{1,5},{2,6},{3,7},{4,0},{5,1},{6,2},{7,3},{8,12},{9,13},{10,... | collective-permute-start | bytes 5505032 | tf_op jit(solution)/shard_map/ppermute | solution.py:30
  12.5 1.2 copy-start.6
  13.6 1.2 copy-start.8
  18.2 108.8 %collective-permute-start = (bf16[80,16384]{1,0:T(8,128)(2,1)}, bf16[80,16384]{1,0:T(8,128)(2,1)S(1)}, u32[]{:S(2)}, u32[]{:S(2)}) collective-permute-start(bf16[80,16384]{1,0:T(8,128)(2,1)} %get-tuple-element.40), channel_id=1, source_target_pairs={{0,28},{1,29},{2,30},{3,31},{4,8},{5,9},{6,10},{7,11},{8,4},{9,5},... | collective-permute-start | bytes 7864328 | tf_op jit(solution)/shard_map/ppermute | solution.py:44
  127.0 1.3 copy-start.3
  128.5 95.5 %collective-permute-start.5 = (bf16[80,16384]{1,0:T(8,128)(2,1)S(1)}, bf16[80,16384]{1,0:T(8,128)(2,1)}, u32[]{:S(2)}, u32[]{:S(2)}) collective-permute-start(bf16[80,16384]{1,0:T(8,128)(2,1)S(1)} %pad_maximum_fusion.2), channel_id=1, source_target_pairs={{0,8},{1,9},{2,10},{3,11},{4,28},{5,29},{6,30},{7,31},{8,16},{9,17... | collective-permute-start | bytes 7864328 | tf_op jit(solution)/shard_map/ppermute | solution.py:44
  131.5 93.9 %collective-permute-start.9 = (bf16[7168,256]{1,0:T(8,128)(2,1)}, bf16[7168,256]{1,0:T(8,128)(2,1)S(1)}, u32[]{:S(2)}, u32[]{:S(2)}) collective-permute-start(bf16[7168,256]{1,0:T(8,128)(2,1)} %collective-permute-done.2.refs_2_.refs_6_), channel_id=1, source_target_pairs={{0,2},{1,3},{2,0},{3,1},{4,6},{5,7},{6,4},{7,5},{8,10},{9,11},{10,... | collective-permute-start | bytes 11010056 | tf_op jit(solution)/shard_map/ppermute | solution.py:30
  132.8 2.6 copy-start.4
  133.0 6.4 %copy-start.1 = (bf16[80,16384]{1,0:T(8,128)(2,1)}, bf16[80,16384]{1,0:T(8,128)(2,1)S(1)}, u32[]{:S(2)}) copy-start(bf16[80,16384]{1,0:T(8,128)(2,1)S(1)} %pad_maximum_fusion.1.refs_0_.refs_4_) | copy-start | bytes 7864324
  133.0 90.9 %collective-permute-start.6 = (bf16[80,16384]{1,0:T(8,128)(2,1)S(1)}, bf16[80,16384]{1,0:T(8,128)(2,1)S(1)}, u32[]{:S(2)}, u32[]{:S(2)}) collective-permute-start(bf16[80,16384]{1,0:T(8,128)(2,1)S(1)} %pad_maximum_fusion.1.refs_0_.refs_4_), channel_id=1, source_target_pairs={{0,1},{1,0},{2,3},{3,2},{4,5},{5,4},{6,7},{7,6},{8,9},{9,8},{10,11... | collective-permute-start | bytes 7864328 | tf_op jit(solution)/shard_map/ppermute | solution.py:30
  135.5 88.4 %collective-permute-start.8 = (bf16[112,7168]{1,0:T(8,128)(2,1)S(1)}, bf16[112,7168]{1,0:T(8,128)(2,1)S(1)}, u32[]{:S(2)}, u32[]{:S(2)}) collective-permute-start(bf16[112,7168]{1,0:T(8,128)(2,1)S(1)} %slice.96), channel_id=1, source_target_pairs={{0,4},{1,5},{2,6},{3,7},{4,0},{5,1},{6,2},{7,3},{8,12},{9,13},{10,... | collective-permute-start | bytes 4816904 | tf_op jit(solution)/shard_map/ppermute | solution.py:30
  139.5 76.0 %collective-permute-start.7 = (bf16[16,7168]{1,0:T(8,128)(2,1)S(1)}, bf16[16,7168]{1,0:T(8,128)(2,1)S(1)}, u32[]{:S(2)}, u32[]{:S(2)}) collective-permute-start(bf16[16,7168]{1,0:T(8,128)(2,1)S(1)} %slice.95), channel_id=1, source_target_pairs={{0,2},{1,3},{2,0},{3,1},{4,6},{5,7},{6,4},{7,5},{8,10},{9,11},{10,... | collective-permute-start | bytes 688136 | tf_op jit(solution)/shard_map/ppermute | solution.py:30
  223.9 2.0 copy-start.15
  223.9 1.5 copy-start.12
  225.9 1.9 copy-start.13
  227.8 7.6 %collective-permute-start.10 = (bf16[80,16384]{1,0:T(8,128)(2,1)}, bf16[80,16384]{1,0:T(8,128)(2,1)}, u32[]{:S(2)}, u32[]{:S(2)}) collective-permute-start(bf16[80,16384]{1,0:T(8,128)(2,1)} %collective-permute-done.5.refs_1_.refs_5_), channel_id=1, source_target_pairs={{0,1},{1,0},{2,3},{3,2},{4,5},{5,4},{6,7},{7,6},{8,9},{9,8},{10,11... | collective-permute-start | bytes 7864328 | tf_op jit(solution)/shard_map/ppermute | solution.py:30
  230.5 4.9 %copy-start.5 = (bf16[128,7168]{1,0:T(8,128)(2,1)S(1)}, bf16[128,7168]{1,0:T(8,128)(2,1)}, u32[]{:S(2)}) copy-start(bf16[128,7168]{1,0:T(8,128)(2,1)} %copy-done.3) | copy-start | bytes 5505028
  232.2 3.2 copy-start.14
  242.3 11.9 %copy-start.11 = (bf16[1,4,7168]{2,1,0:T(4,128)(2,1)S(1)}, bf16[1,4,7168]{2,1,0:T(4,128)(2,1)}, u32[]{:S(2)}) copy-start(bf16[1,4,7168]{2,1,0:T(4,128)(2,1)} %param.16) | copy-start | bytes 172036
  252.0 1.4 copy-start.10
  253.4 4.8 %collective-permute-start.11 = (bf16[160,7168]{1,0:T(8,128)(2,1)}, bf16[160,7168]{1,0:T(8,128)(2,1)}, u32[]{:S(2)}, u32[]{:S(2)}) collective-permute-start(bf16[160,7168]{1,0:T(8,128)(2,1)} %get-tuple-element.54), channel_id=1, source_target_pairs={{0,1},{1,0},{2,3},{3,2},{4,5},{5,4},{6,7},{7,6},{8,9},{9,8},{10,11... | collective-permute-start | bytes 6881288 | tf_op jit(solution)/shard_map/ppermute | solution.py:30
  258.2 6.3 %copy-start.2 = (bf16[80,16384]{1,0:T(8,128)(2,1)S(1)}, bf16[80,16384]{1,0:T(8,128)(2,1)}, u32[]{:S(2)}) copy-start(bf16[80,16384]{1,0:T(8,128)(2,1)} %copy-done.1) | copy-start | bytes 7864324
  262.1 19.9 %collective-permute-start.12 = (bf16[40,7168]{1,0:T(8,128)(2,1)}, bf16[40,7168]{1,0:T(8,128)(2,1)}, u32[]{:S(2)}, u32[]{:S(2)}) collective-permute-start(bf16[40,7168]{1,0:T(8,128)(2,1)} %get-tuple-element.56), channel_id=1, source_target_pairs={{8,0},{9,1},{10,2},{11,3},{28,4},{29,5},{30,6},{31,7},{16,8},{17,9... | collective-permute-start | bytes 1720328 | tf_op jit(solution)/shard_map/ppermute | solution.py:50
  263.3 25.8 %collective-permute-start.13 = (bf16[40,7168]{1,0:T(8,128)(2,1)}, bf16[40,7168]{1,0:T(8,128)(2,1)}, u32[]{:S(2)}, u32[]{:S(2)}) collective-permute-start(bf16[40,7168]{1,0:T(8,128)(2,1)} %get-tuple-element.57), channel_id=1, source_target_pairs={{28,0},{29,1},{30,2},{31,3},{8,4},{9,5},{10,6},{11,7},{4,8},{5,9},... | collective-permute-start | bytes 1720328 | tf_op jit(solution)/shard_map/ppermute | solution.py:50
  263.8 48.7 %collective-permute-start.14 = (bf16[40,7168]{1,0:T(8,128)(2,1)}, bf16[40,7168]{1,0:T(8,128)(2,1)}, u32[]{:S(2)}, u32[]{:S(2)}) collective-permute-start(bf16[40,7168]{1,0:T(8,128)(2,1)} %get-tuple-element.58), channel_id=1, source_target_pairs={{20,0},{21,1},{22,2},{23,3},{16,4},{17,5},{18,6},{19,7},{28,8},{29... | collective-permute-start | bytes 1720328 | tf_op jit(solution)/shard_map/ppermute | solution.py:50
  280.5 34.8 %collective-permute-start.15 = (bf16[160,7168]{1,0:T(8,128)(2,1)}, bf16[160,7168]{1,0:T(8,128)(2,1)}, u32[]{:S(2)}, u32[]{:S(2)}) collective-permute-start(bf16[160,7168]{1,0:T(8,128)(2,1)} %get-tuple-element.68), channel_id=1, source_target_pairs={{0,1},{1,0},{2,3},{3,2},{4,5},{5,4},{6,7},{7,6},{8,9},{9,8},{10,11... | collective-permute-start | bytes 6881288 | tf_op jit(solution)/shard_map/ppermute | solution.py:30
  319.1 16.3 %copy-start.7 = (bf16[1,64,7168]{2,1,0:T(8,128)(2,1)S(1)}, bf16[1,64,7168]{2,1,0:T(8,128)(2,1)}, u32[]{:S(2)}) copy-start(bf16[1,64,7168]{2,1,0:T(8,128)(2,1)} %param.14) | copy-start | bytes 2752516
  319.1 24.6 %collective-permute-start.16 = (bf16[40,7168]{1,0:T(8,128)(2,1)}, bf16[40,7168]{1,0:T(8,128)(2,1)}, u32[]{:S(2)}, u32[]{:S(2)}) collective-permute-start(bf16[40,7168]{1,0:T(8,128)(2,1)} %get-tuple-element.79), channel_id=1, source_target_pairs={{8,0},{9,1},{10,2},{11,3},{28,4},{29,5},{30,6},{31,7},{16,8},{17,9... | collective-permute-start | bytes 1720328 | tf_op jit(solution)/shard_map/ppermute | solution.py:50
  323.9 26.3 %collective-permute-start.17 = (bf16[40,7168]{1,0:T(8,128)(2,1)}, bf16[40,7168]{1,0:T(8,128)(2,1)}, u32[]{:S(2)}, u32[]{:S(2)}) collective-permute-start(bf16[40,7168]{1,0:T(8,128)(2,1)} %get-tuple-element.78), channel_id=1, source_target_pairs={{28,0},{29,1},{30,2},{31,3},{8,4},{9,5},{10,6},{11,7},{4,8},{5,9},... | collective-permute-start | bytes 1720328 | tf_op jit(solution)/shard_map/ppermute | solution.py:50
  324.4 49.5 %collective-permute-start.18 = (bf16[40,7168]{1,0:T(8,128)(2,1)}, bf16[40,7168]{1,0:T(8,128)(2,1)}, u32[]{:S(2)}, u32[]{:S(2)}) collective-permute-start(bf16[40,7168]{1,0:T(8,128)(2,1)} %get-tuple-element.77), channel_id=1, source_target_pairs={{20,0},{21,1},{22,2},{23,3},{16,4},{17,5},{18,6},{19,7},{28,8},{29... | collective-permute-start | bytes 1720328 | tf_op jit(solution)/shard_map/ppermute | solution.py:50
  326.5 52.0 %all-to-all-start = ((f32[32,4,224]{2,1,0:T(4,128)}), f32[32,4,224]{2,1,0:T(4,128)S(1)}, u32[]{:S(2)}, u32[]{:S(2)}) async-start(f32[32,4,224]{2,1,0:T(4,128)} %bitcast.54), calls=%async_computation | async-start | bytes 262144 | tf_op jit(solution)/shard_map/all_to_all | solution.py:34
  335.4 38.5 %copy-start.9 = (bf16[1,64,7168]{2,1,0:T(8,128)(2,1)S(1)}, bf16[1,64,7168]{2,1,0:T(8,128)(2,1)}, u32[]{:S(2)}) copy-start(bf16[1,64,7168]{2,1,0:T(8,128)(2,1)} %param.10) | copy-start | bytes 2752516
  338.9 50.9 %collective-permute-start.20 = (bf16[64,7168]{1,0:T(8,128)(2,1)}, bf16[64,7168]{1,0:T(8,128)(2,1)}, u32[]{:S(2)}, u32[]{:S(2)}) collective-permute-start(bf16[64,7168]{1,0:T(8,128)(2,1)} %combine_backward.1), channel_id=1, source_target_pairs={{32,0},{64,32},{96,64},{128,96},{160,128},{192,160},{224,192},{0,2... | collective-permute-start | bytes 2752520 | tf_op jit(solution)/shard_map/ppermute | solution.py:25
  378.6 26.4 %collective-permute-start.19 = (bf16[64,7168]{1,0:T(8,128)(2,1)S(1)}, bf16[64,7168]{1,0:T(8,128)(2,1)S(1)}, u32[]{:S(2)}, u32[]{:S(2)}) collective-permute-start(bf16[64,7168]{1,0:T(8,128)(2,1)S(1)} %combine_forward.1), channel_id=1, source_target_pairs={{224,0},{0,32},{32,64},{64,96},{96,128},{128,160},{160,192},{192,2... | collective-permute-start | bytes 2752520 | tf_op jit(solution)/shard_map/ppermute | solution.py:25
  381.9 21.2 %all-to-all-start.1 = ((f32[32,4,224]{2,1,0:T(4,128)}), f32[32,4,224]{2,1,0:T(4,128)S(1)}, u32[]{:S(2)}, u32[]{:S(2)}) async-start(f32[32,4,224]{2,1,0:T(4,128)} %broadcast_in_dim.13), calls=%async_computation.1 | async-start | bytes 262144 | tf_op jit(solution)/shard_map/all_to_all | solution.py:34
